TPU v7x, 32 devices: a whole 2x2x4 slice. The times are simulated.
32 devices in a mesh: gx: 16 (over z, y, x), gy: 2 (over core).
Axes of the slice: x: 2, y: 2, z: 4, core: 2. Of those that a mesh axis runs over, the one named last changes fastest.
Arguments:
- magnetization: float32 [3, 256, 32, 512], P(None, 'gx', 'gy'), may hold values from -2.2 to 2.2
- easy_axes: float32 [3, 256, 32, 512], P(None, 'gx', 'gy'), may hold values from -6 to 6
- pins: float32 [2, 3, 32, 512], P(None, None, 'gy'), may hold values from -4 to 4
Outputs:
- final_field: float32 [3, 256, 32, 512], P(None, 'gx', 'gy')
All inputs are finite; a program needn't handle non-finite values.
Results may differ from a plain program's by a relative error of at most 0.0003.
Values sent between devices are 32-bit elements; how exact they have to be, the bound alone decides.
No kernel may reach another device: no remote copies, remote signals or barrier semaphores. Data moves between devices by JAX's collectives and lax.ppermute only.
A program may use at most 64 MiB of HBM per device.

v0:
```python
import jax
import jax.numpy as jnp
import numpy as np
from jax import lax
from jax.sharding import PartitionSpec as P

STEPS = 2


diffusion = 4000.0
anisotropy_rate = 0.3
torque_rate = 0.2
exchange_rate = 0.1
norm_floor = 0.5


def with_halo(block, sides, width):
    for axis, dim in sides:
        count = lax.axis_size(axis)
        forward = [(i, i + 1) for i in range(count - 1)]
        forward.append((count - 1, 0))
        backward = [(target, source) for source, target in forward]
        low = lax.ppermute(
            lax.slice_in_dim(block, block.shape[dim] - width, None, axis=dim), axis, forward
        )
        high = lax.ppermute(lax.slice_in_dim(block, 0, width, axis=dim), axis, backward)
        block = jnp.concatenate([low, block, high], axis=dim)
    return block


def block_inverse(inner_count):
    leading = 1.0 + 2.0 * diffusion
    theta = [1.0, leading]
    for index in range(2, inner_count + 1):
        theta.append(leading * theta[index - 1] - diffusion * diffusion * theta[index - 2])
    inverse = np.zeros((inner_count, inner_count))
    for row in range(inner_count):
        for column in range(inner_count):
            small = min(row, column)
            large = max(row, column)
            inverse[row, column] = (
                diffusion ** (large - small)
                * theta[small]
                * theta[inner_count - 1 - large]
                / theta[inner_count]
            )
    return inverse


def interface_tables(planes, groups):
    inner_count = planes - 2
    inverse = block_inverse(inner_count)
    diagonal = 1.0 + 2.0 * diffusion - diffusion * diffusion * inverse[0, 0]
    within = -diffusion * diffusion * inverse[0, inner_count - 1]
    count = 2 * groups
    numbers = np.arange(count)
    lower_band = np.where(numbers % 2 == 1, within, -diffusion)
    lower_band[0] = 0.0
    upper_band = np.where(numbers % 2 == 0, within, -diffusion)
    upper_band[count - 1] = 0.0
    middle = np.full(count, diagonal)
    pivots = np.zeros(count)
    pivots[0] = middle[0]
    for index in range(1, count):
        pivots[index] = (
            middle[index] - lower_band[index] * upper_band[index - 1] / pivots[index - 1]
        )
    factors = np.zeros(count)
    factors[1:] = lower_band[1:] / pivots[:-1]
    return (inverse, lower_band, middle, upper_band, pivots, factors)


def per_device(magnetization, easy_axes, pins):
    planes = magnetization.shape[1]
    groups = lax.axis_size("gx")
    position = lax.axis_index("gx")
    inverse, lower_band, middle, upper_band, pivots, factors = interface_tables(planes, groups)
    inverse_here = jnp.asarray(inverse, jnp.float32)
    edge_first = diffusion * inverse_here[:, 0:1]
    edge_last = diffusion * inverse_here[:, -1:]
    lower_here = jnp.asarray(lower_band, jnp.float32)
    middle_here = jnp.asarray(middle, jnp.float32)
    upper_here = jnp.asarray(upper_band, jnp.float32)
    is_first = (position == 0).astype(jnp.float32)
    is_last = (position == groups - 1).astype(jnp.float32)
    field = magnetization
    for stepno in range(STEPS):
        for component in range(3):
            projection = jnp.sum(field * easy_axes, axis=0)
            source = field[component] + anisotropy_rate * projection * easy_axes[component]
            source = source.at[0].add(diffusion * is_first * pins[0, component])
            source = source.at[-1].add(diffusion * is_last * pins[1, component])
            columns = source.reshape(planes, -1)
            inner = jnp.dot(
                inverse_here,
                columns[1:-1],
                precision=lax.Precision.HIGHEST,
                preferred_element_type=jnp.float32,
            )
            reduced = jnp.stack(
                [columns[0] + diffusion * inner[0], columns[-1] + diffusion * inner[-1]]
            )
            grouped = lax.all_to_all(reduced, "gx", split_axis=1, concat_axis=0, tiled=True)
            solved = lax.linalg.tridiagonal_solve(lower_here, middle_here, upper_here, grouped)
            boundary = lax.all_to_all(solved, "gx", split_axis=0, concat_axis=1, tiled=True)
            middle_rows = inner + edge_first * boundary[0:1] + edge_last * boundary[1:2]
            field = field.at[component].set(
                jnp.concatenate([boundary[0:1], middle_rows, boundary[1:2]], axis=0).reshape(
                    source.shape
                )
            )
        projection = jnp.sum(field * easy_axes, axis=0)
        padded = with_halo(field, (("gy", 2),), 1)
        neighbours = (
            padded[:, :, 2:] + padded[:, :, :-2] + jnp.roll(field, 1, 3) + jnp.roll(field, -1, 3)
        )
        effective = exchange_rate * (neighbours - 4.0 * field) + projection[None] * easy_axes
        twisted = jnp.cross(field, effective, axis=0)
        rotated = field - torque_rate * twisted
        length = jnp.sqrt(jnp.sum(rotated * rotated, axis=0))
        field = rotated / jnp.maximum(length, norm_floor)[None]
    return field


def solution(mesh):
    in_specs = (P(None, "gx", "gy", None), P(None, "gx", "gy", None), P(None, None, "gy", None))
    out_specs = P(None, "gx", "gy", None)
    return jax.shard_map(
        per_device, mesh=mesh, in_specs=in_specs, out_specs=out_specs, check_vma=False
    )
```

profile of v0, /device:TPU:1, one launch (start us, length us, event | category | flops | bytes accessed | tf_op | source)
XLA Modules:
  0.0 171.0 jit_solution(12533503647062744678)
XLA Ops:
  0.0 1.5 copy.63
  5.2 13.6 %all_to_all.192 = f32[2,16,512]{2,0,1:T(2,128)S(1)} all-to-all(f32[2,16,512]{2,0,1:T(2,128)S(1)} %pad_maximum_fusion.4), channel_id=1, replica_groups=mesh['gx'=16,'gy'=2] {'gx'}, dimensions={1} | all-to-all | bytes 131072 | tf_op jit(solution)/shard_map/all_to_all | solution.py:103
  19.4 9.0 %all_to_all.193 = f32[16,2,512]{2,1,0:T(2,128)S(1)} all-to-all(f32[16,2,512]{2,1,0:T(2,128)S(1)} %all_to_all.147), channel_id=1, replica_groups=mesh['gx'=16,'gy'=2] {'gx'}, dimensions={0} | all-to-all | bytes 131072 | tf_op jit(solution)/shard_map/all_to_all | solution.py:105
  28.4 1.2 multiply_add_fusion.5
  32.7 9.0 %all_to_all.194 = f32[2,16,512]{2,0,1:T(2,128)S(1)} all-to-all(f32[2,16,512]{2,0,1:T(2,128)S(1)} %pad_maximum_fusion.5), channel_id=1, replica_groups=mesh['gx'=16,'gy'=2] {'gx'}, dimensions={1} | all-to-all | bytes 131072 | tf_op jit(solution)/shard_map/all_to_all | solution.py:103
  42.2 9.0 %all_to_all.195 = f32[16,2,512]{2,1,0:T(2,128)S(1)} all-to-all(f32[16,2,512]{2,1,0:T(2,128)S(1)} %all_to_all.153), channel_id=1, replica_groups=mesh['gx'=16,'gy'=2] {'gx'}, dimensions={0} | all-to-all | bytes 131072 | tf_op jit(solution)/shard_map/all_to_all | solution.py:105
  51.2 1.2 multiply_add_fusion.4
  55.4 9.0 %all_to_all.196 = f32[2,16,512]{2,0,1:T(2,128)S(1)} all-to-all(f32[2,16,512]{2,0,1:T(2,128)S(1)} %pad_maximum_fusion.6), channel_id=1, replica_groups=mesh['gx'=16,'gy'=2] {'gx'}, dimensions={1} | all-to-all | bytes 131072 | tf_op jit(solution)/shard_map/all_to_all | solution.py:103
  65.0 9.0 %all_to_all.197 = f32[16,2,512]{2,1,0:T(2,128)S(1)} all-to-all(f32[16,2,512]{2,1,0:T(2,128)S(1)} %all_to_all.159), channel_id=1, replica_groups=mesh['gx'=16,'gy'=2] {'gx'}, dimensions={0} | all-to-all | bytes 131072 | tf_op jit(solution)/shard_map/all_to_all | solution.py:105
  74.0 1.2 multiply_add_fusion.3
  76.6 7.9 %collective-permute-start = (f32[3,16,1,512]{3,2,1,0:T(1,128)S(1)}, f32[3,16,1,512]{3,2,1,0:T(1,128)S(1)}, u32[]{:S(2)}, u32[]{:S(2)}) collective-permute-start(f32[3,16,1,512]{3,2,1,0:T(1,128)S(1)} %get-tuple-element.522), channel_id=1, source_target_pairs={{1,0},{0,1},{3,2},{2,3},{5,4},{4,5},{7,6},{6,7},{9,8},{8,9},{11,10... | collective-permute-start | bytes 294920 | tf_op jit(solution)/shard_map/ppermute | solution.py:26
  85.8 1.4 fusion.13
  91.9 9.0 %all_to_all.198 = f32[2,16,512]{2,0,1:T(2,128)S(1)} all-to-all(f32[2,16,512]{2,0,1:T(2,128)S(1)} %pad_maximum_fusion.7), channel_id=1, replica_groups=mesh['gx'=16,'gy'=2] {'gx'}, dimensions={1} | all-to-all | bytes 131072 | tf_op jit(solution)/shard_map/all_to_all | solution.py:103
  101.4 9.0 %all_to_all.199 = f32[16,2,512]{2,1,0:T(2,128)S(1)} all-to-all(f32[16,2,512]{2,1,0:T(2,128)S(1)} %all_to_all.165), channel_id=1, replica_groups=mesh['gx'=16,'gy'=2] {'gx'}, dimensions={0} | all-to-all | bytes 131072 | tf_op jit(solution)/shard_map/all_to_all | solution.py:105
  110.5 1.3 multiply_add_fusion.2
  114.9 9.0 %all_to_all.200 = f32[2,16,512]{2,0,1:T(2,128)S(1)} all-to-all(f32[2,16,512]{2,0,1:T(2,128)S(1)} %pad_maximum_fusion.8), channel_id=1, replica_groups=mesh['gx'=16,'gy'=2] {'gx'}, dimensions={1} | all-to-all | bytes 131072 | tf_op jit(solution)/shard_map/all_to_all | solution.py:103
  124.4 9.0 %all_to_all.201 = f32[16,2,512]{2,1,0:T(2,128)S(1)} all-to-all(f32[16,2,512]{2,1,0:T(2,128)S(1)} %all_to_all.171), channel_id=1, replica_groups=mesh['gx'=16,'gy'=2] {'gx'}, dimensions={0} | all-to-all | bytes 131072 | tf_op jit(solution)/shard_map/all_to_all | solution.py:105
  133.4 1.2 multiply_add_fusion.1
  137.6 9.0 %all_to_all.202 = f32[2,16,512]{2,0,1:T(2,128)S(1)} all-to-all(f32[2,16,512]{2,0,1:T(2,128)S(1)} %pad_maximum_fusion.9), channel_id=1, replica_groups=mesh['gx'=16,'gy'=2] {'gx'}, dimensions={1} | all-to-all | bytes 131072 | tf_op jit(solution)/shard_map/all_to_all | solution.py:103
  147.1 9.0 %all_to_all.203 = f32[16,2,512]{2,1,0:T(2,128)S(1)} all-to-all(f32[16,2,512]{2,1,0:T(2,128)S(1)} %all_to_all.177), channel_id=1, replica_groups=mesh['gx'=16,'gy'=2] {'gx'}, dimensions={0} | all-to-all | bytes 131072 | tf_op jit(solution)/shard_map/all_to_all | solution.py:105
  156.2 1.2 multiply_add_fusion
  158.8 7.1 %collective-permute-start.2 = (f32[3,16,1,512]{3,2,1,0:T(1,128)S(1)}, f32[3,16,1,512]{3,2,1,0:T(1,128)S(1)}, u32[]{:S(2)}, u32[]{:S(2)}) collective-permute-start(f32[3,16,1,512]{3,2,1,0:T(1,128)S(1)} %get-tuple-element.516), channel_id=1, source_target_pairs={{1,0},{0,1},{3,2},{2,3},{5,4},{4,5},{7,6},{6,7},{9,8},{8,9},{11,10... | collective-permute-start | bytes 294920 | tf_op jit(solution)/shard_map/ppermute | solution.py:26
  167.2 1.4 fusion.6
  169.5 1.6 broadcast_divide_fusion
  (178 shorter events, 29.6 us)
Async XLA Ops:
  0.0 1.9 %copy-start = (f32[3,16,16,512]{3,2,1,0:T(8,128)S(1)}, f32[3,16,16,512]{3,2,1,0:T(8,128)}, u32[]{:S(2)}) copy-start(f32[3,16,16,512]{3,2,1,0:T(8,128)} %param.46) | copy-start | bytes 4718596
  2.3 0.9 copy-start.9
  2.4 1.2 copy-start.10
  3.3 25.1 %copy-start.11 = (f32[14]{0:T(128)S(1)}, f32[14]{0:T(128)}, u32[]{:S(2)}) copy-start(f32[14]{0:T(128)} %constant.664) | copy-start | bytes 172
  3.4 25.1 %copy-start.12 = (f32[14]{0:T(128)S(1)}, f32[14]{0:T(128)}, u32[]{:S(2)}) copy-start(f32[14]{0:T(128)} %constant.661) | copy-start | bytes 172
  4.3 0.8 copy-start.4
  31.7 0.8 copy-start.5
  54.5 0.8 copy-start.6
  76.6 8.9 %collective-permute-start = (f32[3,16,1,512]{3,2,1,0:T(1,128)S(1)}, f32[3,16,1,512]{3,2,1,0:T(1,128)S(1)}, u32[]{:S(2)}, u32[]{:S(2)}) collective-permute-start(f32[3,16,1,512]{3,2,1,0:T(1,128)S(1)} %get-tuple-element.522), channel_id=1, source_target_pairs={{1,0},{0,1},{3,2},{2,3},{5,4},{4,5},{7,6},{6,7},{9,8},{8,9},{11,10... | collective-permute-start | bytes 294920 | tf_op jit(solution)/shard_map/ppermute | solution.py:26
  84.5 1.3 collective-permute-start.1
  88.8 1.1 copy-start.1
  90.9 0.8 copy-start.7
  110.5 1.7 copy-start.2
  113.9 0.8 copy-start.8
  136.7 0.8 copy-start.3
  158.8 8.0 %collective-permute-start.2 = (f32[3,16,1,512]{3,2,1,0:T(1,128)S(1)}, f32[3,16,1,512]{3,2,1,0:T(1,128)S(1)}, u32[]{:S(2)}, u32[]{:S(2)}) collective-permute-start(f32[3,16,1,512]{3,2,1,0:T(1,128)S(1)} %get-tuple-element.516), channel_id=1, source_target_pairs={{1,0},{0,1},{3,2},{2,3},{5,4},{4,5},{7,6},{6,7},{9,8},{8,9},{11,10... | collective-permute-start | bytes 294920 | tf_op jit(solution)/shard_map/ppermute | solution.py:26
  165.9 1.3 collective-permute-start.3
where the time goes:
time: 172 us; the launch traced here: 171 us
  blocking collectives  112 us (65%)
  other arithmetic  20.7 us (12%)
  local copies, waits for them, and re-layouts  16.8 us (10%)
  starting transfers between devices  15.2 us (9%)
  matrix products  3.39 us (2%)
    all_to_all x6, blocking collectives, per_device(): lax.all_to_all(reduced, 'gx', split_axis=1, concat_axis=0, tiled=True)  58.5 us
    all_to_all x6, blocking collectives, per_device(): lax.all_to_all(solved, 'gx', split_axis=0, concat_axis=1, tiled=True)  53.8 us
    ppermute x2, starting transfers between devices, with_halo(): lax.ppermute(lax.slice_in_dim(block, 0, width, axis=dim), axis, backward)  15 us
    unnamed x57, local copies, waits for them, and re-layouts  12.6 us
    add x6, other arithmetic, per_device(): middle_rows = inner + edge_first * boundary[0:1] + edge_last * boundary[1:2]  7.28 us
  transfers between devices with their start and end apart: 4, of which 4 were waited for; matrix products, arithmetic and copies ran while one was open for 0% of the time, Pallas kernels for 0%

commit v1 on v0

v1 whole, which is shorter than its diff:
```python
import functools

import jax
import jax.numpy as jnp
import numpy as np
from jax import lax
from jax.experimental import pallas as pl
from jax.experimental.pallas import tpu as pltpu
from jax.sharding import PartitionSpec as P

STEPS = 2
LANES = 128
RHS = 6
COUPLED = 16

diffusion = 4000.0
anisotropy_rate = 0.3
torque_rate = 0.2
exchange_rate = 0.1
norm_floor = 0.5


class Line:
    def __init__(self, planes):
        leading = 1.0 + 2.0 * diffusion
        pivots = [leading]
        for _ in range(1, planes):
            pivots.append(leading - diffusion * diffusion / pivots[-1])
        self.planes = planes
        self.inverse_pivot = [1.0 / p for p in pivots]
        self.factor = [0.0] + [diffusion / p for p in pivots[:-1]]
        block = (
            leading * np.eye(planes)
            - diffusion * np.eye(planes, k=1)
            - diffusion * np.eye(planes, k=-1)
        )
        self.from_low = diffusion * np.linalg.inv(block)[:, 0]
        self.from_high = self.from_low[::-1]

    def solve(self, source):
        planes = self.planes
        carried = [source[0]]
        for i in range(1, planes):
            carried.append(source[i] + self.factor[i] * carried[-1])
        solved = [None] * planes
        solved[-1] = carried[-1] * self.inverse_pivot[-1]
        for i in range(planes - 2, -1, -1):
            solved[i] = carried[i] * self.inverse_pivot[i] + self.factor[i + 1] * solved[i + 1]
        return solved


def ghost_table(line, groups):
    near, far = line.from_low[0], line.from_low[-1]
    link = np.zeros((2 * groups, 2 * groups))
    pick = np.zeros((2 * groups, 2 * groups))
    for d in range(groups):
        if d > 0:
            link[d, groups + d - 1] = near
            link[groups + d, groups + d - 1] = far
            pick[d, groups + d - 1] = 1.0
        if d < groups - 1:
            link[d, d + 1] = far
            link[groups + d, d + 1] = near
            pick[groups + d, d + 1] = 1.0
    return pick @ np.linalg.inv(np.eye(2 * groups) - link)


def row_window(value, values, units, tile, tiles, rows):
    start = (tile // units) * values * units + value * units + tile % units
    return pl.ds(start, rows, stride=tiles * values)


def pinned(source, pins_ref, component, lanes):
    position = lax.axis_index("gx")
    first = jnp.where(position == 0, diffusion, 0.0).astype(jnp.float32)
    last = jnp.where(position == lax.axis_size("gx") - 1, diffusion, 0.0).astype(jnp.float32)
    source[0] = source[0] + first * pins_ref[0, component, :, lanes]
    source[-1] = source[-1] + last * pins_ref[1, component, :, lanes]
    return source


def solve_components(line, field_ref, axes_ref, pins_ref, lanes, ghosts):
    planes = line.planes
    field = [[field_ref[c, i, :, lanes] for i in range(planes)] for c in range(3)]
    axes = [[axes_ref[c, i, :, lanes] for i in range(planes)] for c in range(3)]
    for component in range(3):
        source = []
        for i in range(planes):
            projection = (
                field[0][i] * axes[0][i] + field[1][i] * axes[1][i] + field[2][i] * axes[2][i]
            )
            source.append(
                field[component][i] + (anisotropy_rate * projection) * axes[component][i]
            )
        source = pinned(source, pins_ref, component, lanes)
        if ghosts is not None:
            source[0] = source[0] + diffusion * ghosts[component][0]
            source[-1] = source[-1] + diffusion * ghosts[component][1]
        field[component] = line.solve(source)
    return field


def couplings(line, axes_ref, lanes):
    planes = line.planes
    low, high = line.from_low, line.from_high
    axes = [[axes_ref[c, i, :, lanes] for i in range(planes)] for c in range(3)]
    scaled = [anisotropy_rate * a for a in axes[1]]
    first_second = [axes[0][i] * scaled[i] for i in range(planes)]
    second_third = [axes[2][i] * scaled[i] for i in range(planes)]
    first_third = [(anisotropy_rate * axes[0][i]) * axes[2][i] for i in range(planes)]

    def weighted(terms, weights):
        total = terms[0] * float(weights[0] / diffusion)
        for i in range(1, planes):
            total = total + terms[i] * float(weights[i] / diffusion)
        return total

    found = []
    for product in (first_second, second_third):
        for weights in (low * low, low * high, high * high):
            found.append(weighted(product, weights))
    for ghost in (low, high):
        moved = line.solve([first_second[i] * float(ghost[i]) for i in range(planes)])
        pushed = [
            second_third[i] * moved[i] + first_third[i] * float(ghost[i]) for i in range(planes)
        ]
        found.append(weighted(pushed, low))
        found.append(weighted(pushed, high))
    return found


def send_edges(line, units, coupled, field_ref, axes_ref, pins_ref, out_ref):
    rows, width = field_ref.shape[2], field_ref.shape[3]
    tiles = width // LANES
    values = COUPLED if coupled else RHS
    for tile in range(tiles):
        lanes = slice(tile * LANES, (tile + 1) * LANES)
        solved = solve_components(line, field_ref, axes_ref, pins_ref, lanes, None)
        sent = []
        for component in range(3):
            sent += [solved[component][0], solved[component][-1]]
        if coupled:
            sent += couplings(line, axes_ref, lanes)
        for value in range(values):
            out_ref[row_window(value, values, units, tile, tiles, rows), :] = sent[value]


def reduced_kernel(groups, units, rhs_values, rhs_ref, coupling_ref, table_ref, out_ref):
    def read(ref, values, value):
        parts = [
            ref[pl.ds(value * units + u, groups, stride=values * units), :] for u in range(units)
        ]
        return jnp.concatenate(parts, axis=1) if units > 1 else parts[0]

    table = table_ref[...]

    def ghosts(first, last):
        found = jnp.dot(
            table,
            jnp.concatenate([first, last], axis=0),
            precision=lax.Precision.HIGHEST,
            preferred_element_type=jnp.float32,
        )
        return found[:groups], found[groups:]

    rhs = [read(rhs_ref, rhs_values, v) for v in range(RHS)]
    c = [read(coupling_ref, COUPLED, v) for v in range(RHS, COUPLED)]
    low1, high1 = ghosts(rhs[0], rhs[1])
    low2, high2 = ghosts(
        rhs[2] + c[0] * low1 + c[1] * high1, rhs[3] + c[1] * low1 + c[2] * high1
    )
    low3, high3 = ghosts(
        rhs[4] + c[3] * low2 + c[4] * high2 + c[6] * low1 + c[8] * high1,
        rhs[5] + c[4] * low2 + c[5] * high2 + c[7] * low1 + c[9] * high1,
    )
    for value, found in enumerate((low1, high1, low2, high2, low3, high3)):
        for u in range(units):
            out_ref[pl.ds(value * units + u, groups, stride=RHS * units), :] = found[
                :, u * LANES : (u + 1) * LANES
            ]


def finish_kernel(line, units, field_ref, axes_ref, pins_ref, ghost_ref, out_ref, low_ref, high_ref):
    planes = line.planes
    rows, width = field_ref.shape[2], field_ref.shape[3]
    tiles = width // LANES
    for tile in range(tiles):
        lanes = slice(tile * LANES, (tile + 1) * LANES)
        ghosts = [
            [
                ghost_ref[row_window(2 * c + side, RHS, units, tile, tiles, rows), :]
                for side in range(2)
            ]
            for c in range(3)
        ]
        solved = solve_components(line, field_ref, axes_ref, pins_ref, lanes, ghosts)
        for c in range(3):
            for i in range(planes):
                out_ref[c, i, :, lanes] = solved[c][i]
                low_ref[c * planes + i : c * planes + i + 1, lanes] = solved[c][i][:1]
                high_ref[c * planes + i : c * planes + i + 1, lanes] = solved[c][i][rows - 1 :]


def rotate(field_ref, below_ref, above_ref, axes_ref, out_ref):
    planes, rows, width = field_ref.shape[1:]
    row = lax.broadcasted_iota(jnp.int32, (rows, width), 0)
    for i in range(planes):
        field = [field_ref[c, i] for c in range(3)]
        axes = [axes_ref[c, i] for c in range(3)]
        projection = field[0] * axes[0] + field[1] * axes[1] + field[2] * axes[2]
        effective = []
        for c in range(3):
            at = c * planes + i
            below = jnp.where(
                row == 0, below_ref[at : at + 1, :], pltpu.roll(field[c], 1, 0)
            )
            above = jnp.where(
                row == rows - 1, above_ref[at : at + 1, :], pltpu.roll(field[c], rows - 1, 0)
            )
            beside = pltpu.roll(field[c], 1, 1) + pltpu.roll(field[c], width - 1, 1)
            effective.append(
                exchange_rate * (((above + below) + beside) - 4.0 * field[c])
                + projection * axes[c]
            )
        rotated = []
        for c in range(3):
            d, e = (c + 1) % 3, (c + 2) % 3
            twisted = field[d] * effective[e] - field[e] * effective[d]
            rotated.append(field[c] - torque_rate * twisted)
        square = rotated[0] * rotated[0] + rotated[1] * rotated[1] + rotated[2] * rotated[2]
        scale = jnp.minimum(lax.rsqrt(square), 1.0 / norm_floor)
        for c in range(3):
            out_ref[c, i] = rotated[c] * scale


def rotate_and_send_kernel(
    line, units, field_ref, below_ref, above_ref, axes_ref, pins_ref, out_ref, sent_ref
):
    rotate(field_ref, below_ref, above_ref, axes_ref, out_ref)
    send_edges(line, units, False, out_ref, axes_ref, pins_ref, sent_ref)


VMEM = pl.BlockSpec(memory_space=pltpu.VMEM)
LIMIT = pltpu.CompilerParams(vmem_limit_bytes=32 * 1024 * 1024)


def call(kernel, shapes, *operands):
    shapes = [jax.ShapeDtypeStruct(shape, jnp.float32) for shape in shapes]
    single = len(shapes) == 1
    return pl.pallas_call(
        kernel,
        out_shape=shapes[0] if single else tuple(shapes),
        in_specs=[VMEM] * len(operands),
        out_specs=VMEM if single else (VMEM,) * len(shapes),
        compiler_params=LIMIT,
    )(*operands)


def exchange(block, groups):
    parts = block.reshape(groups, -1, LANES)
    return lax.all_to_all(parts, "gx", split_axis=0, concat_axis=0, tiled=True).reshape(
        block.shape
    )


def to_neighbours(low, high):
    count = lax.axis_size("gy")
    forward = [(i, (i + 1) % count) for i in range(count)]
    backward = [(target, source) for source, target in forward]
    return lax.ppermute(high, "gy", forward), lax.ppermute(low, "gy", backward)


def per_device(magnetization, easy_axes, pins):
    _, planes, rows, width = magnetization.shape
    groups = lax.axis_size("gx")
    units = rows * (width // LANES) // groups
    line = Line(planes)
    table = jnp.asarray(ghost_table(line, groups), jnp.float32)
    whole = magnetization.shape
    edge = (3 * planes, width)
    sent_shape = (groups * RHS * units, LANES)
    coupled_shape = (groups * COUPLED * units, LANES)

    field = magnetization
    sent = call(
        functools.partial(send_edges, line, units, True),
        [coupled_shape],
        field,
        easy_axes,
        pins,
    )
    coupling = None
    for stepno in range(STEPS):
        gathered = exchange(sent, groups)
        if stepno == 0:
            coupling = gathered
        ghosts = call(
            functools.partial(reduced_kernel, groups, units, RHS if stepno else COUPLED),
            [sent_shape],
            gathered,
            coupling,
            table,
        )
        ghosts = exchange(ghosts, groups)
        solved, low, high = call(
            functools.partial(finish_kernel, line, units),
            [whole, edge, edge],
            field,
            easy_axes,
            pins,
            ghosts,
        )
        below, above = to_neighbours(low, high)
        if stepno < STEPS - 1:
            field, sent = call(
                functools.partial(rotate_and_send_kernel, line, units),
                [whole, sent_shape],
                solved,
                below,
                above,
                easy_axes,
                pins,
            )
        else:
            field = call(rotate, [whole], solved, below, above, easy_axes)
    return field


def solution(mesh):
    in_specs = (P(None, "gx", "gy", None), P(None, "gx", "gy", None), P(None, None, "gy", None))
    out_specs = P(None, "gx", "gy", None)
    return jax.shard_map(
        per_device, mesh=mesh, in_specs=in_specs, out_specs=out_specs, check_vma=False
    )
```

time: 172 us -> 75.7 us (0.44)
  blocking collectives: 112 us -> 53.6 us
  other arithmetic: 20.7 us -> 0 us
  local copies, waits for them, and re-layouts: 16.8 us -> 3.76 us
  Pallas kernels: 0 us -> 9.82 us
  starting transfers between devices: 15.2 us -> 5.55 us
  matrix products: 3.39 us -> 0 us
    all_to_all x12 -> x4, blocking collectives: 112 us -> 53.6 us  [exchange(): lax.all_to_all(parts, 'gx', split_axis=0, concat_axis=0, tiled=True)]
    pallas_call x0 -> x7, Pallas kernels: none -> 9.82 us  [call(): pl.pallas_call(kernel, out_shape=shapes[0] if single else tuple(shapes),...]
    ppermute x4, starting transfers between devices: 15.2 us -> 5.55 us  [the longest x2 5.39 us: to_neighbours(): lax.ppermute(high, 'gy', forward)]
    add x18 -> x0, other arithmetic: 8.89 us -> none  [the longest x6 7.28 us: per_device(): middle_rows = inner + edge_first * boundary[0:1] + edge_last * boundary[1:2]]
    unnamed x57 -> x14, local copies, waits for them, and re-layouts: 12.6 us -> 3.76 us
    reduce_sum x10 -> x0, other arithmetic: 4.14 us -> none  [the longest x8 3.33 us: per_device(): projection = jnp.sum(field * easy_axes, axis=0)]
    dot_general x6 -> x0, matrix products: 3.39 us -> none  [per_device(): jnp.dot(inverse_here, columns[1:-1], precision=lax.Precision.HIGHEST, pre...]
    transpose x2 -> x0, other arithmetic: 2.74 us -> none  [per_device(): twisted = jnp.cross(field, effective, axis=0)]
where the time goes in v1:
time: 75.7 us; the launch traced here: 75.2 us
  blocking collectives  53.6 us (71%)
  Pallas kernels  9.82 us (13%)
  starting transfers between devices  5.55 us (7%)
  local copies, waits for them, and re-layouts  3.76 us (5%)
  waiting for transfers between devices  2.44 us (3%)
    all_to_all x4, blocking collectives, exchange(): lax.all_to_all(parts, 'gx', split_axis=0, concat_axis=0, tiled=True)  53.6 us
    pallas_call x7, Pallas kernels, call(): pl.pallas_call(kernel, out_shape=shapes[0] if single else tuple(shapes),...  9.82 us
    ppermute x2, starting transfers between devices, to_neighbours(): lax.ppermute(high, 'gy', forward)  5.39 us
    unnamed x14, local copies, waits for them, and re-layouts  3.76 us
    ppermute x2, waiting for transfers between devices, to_neighbours(): lax.ppermute(high, 'gy', forward)  1.73 us
  transfers between devices with their start and end apart: 4, of which 4 were waited for; matrix products, arithmetic and copies ran while one was open for 0% of the time, Pallas kernels for 0%

profile of v1, /device:TPU:1, one launch (start us, length us, event | category | flops | bytes accessed | tf_op | source)
XLA Modules:
  0.0 75.2 jit_solution(16367466130761009351)
XLA Ops:
  0.0 1.4 %copy-done = f32[3,16,16,512]{3,2,1,0:T(8,128)S(1)} copy-done((f32[3,16,16,512]{3,2,1,0:T(8,128)S(1)}, f32[3,16,16,512]{3,2,1,0:T(8,128)}, u32[]{:S(2)}) %copy-start) | copy-done | bytes 1572888
  1.4 1.4 %copy-done.2 = f32[3,16,16,512]{3,2,1,0:T(8,128)S(1)} copy-done((f32[3,16,16,512]{3,2,1,0:T(8,128)S(1)}, f32[3,16,16,512]{3,2,1,0:T(8,128)}, u32[]{:S(2)}) %copy-start.2) | copy-done | bytes 1572888
  2.8 0.9 %copy-done.4 = f32[2,3,16,512]{3,2,1,0:T(8,128)S(1)} copy-done((f32[2,3,16,512]{3,2,1,0:T(8,128)S(1)}, f32[2,3,16,512]{3,2,1,0:T(8,128)}, u32[]{:S(2)}) %copy-start.4) | copy-done | bytes 196632
  3.7 1.9 %shard_map.46 = f32[1024,128]{1,0:T(8,128)S(1)} custom-call(f32[3,16,16,512]{3,2,1,0:T(8,128)S(1)} %copy-done.2, f32[3,16,16,512]{3,2,1,0:T(8,128)S(1)} %copy-done, f32[2,3,16,512]{3,2,1,0:T(8,128)S(1)} %copy-done.4), custom_call_target="tpu_custom_call" | custom-call | tf_op jit(solution)/shard_map/pallas_call | solution.py:250
  5.7 0.0 copy-start.3
  5.7 19.6 %all_to_all.20 = f32[16,64,128]{2,1,0:T(8,128)S(1)} all-to-all(f32[16,64,128]{2,1,0:T(8,128)S(1)} %bitcast.11), channel_id=1, replica_groups=mesh['gx'=16,'gy'=2] {'gx'}, dimensions={0} | all-to-all | bytes 1048576 | tf_op jit(solution)/shard_map/all_to_all | solution.py:261
  25.3 0.0 copy-done.6
  25.3 0.7 shard_map.47
  26.0 12.8 %all_to_all.21 = f32[16,24,128]{2,1,0:T(8,128)S(1)} all-to-all(f32[16,24,128]{2,1,0:T(8,128)S(1)} %bitcast.16), channel_id=1, replica_groups=mesh['gx'=16,'gy'=2] {'gx'}, dimensions={0} | all-to-all | bytes 393216 | tf_op jit(solution)/shard_map/all_to_all | solution.py:261
  38.9 1.0 %shard_map.48 = (f32[3,16,16,512]{3,2,1,0:T(8,128)S(1)}, f32[48,512]{1,0:T(8,128)S(1)}, f32[48,512]{1,0:T(8,128)S(1)}) custom-call(f32[3,16,16,512]{3,2,1,0:T(8,128)S(1)} %copy-done.3, f32[3,16,16,512]{3,2,1,0:T(8,128)S(1)} %copy-done, f32[2,3,16,512]{3,2,1,0:T(8,128)S(1)} %copy-done.4, f32[384,128]{1,0:T(8,128)S(1)} %bitcast.13), custom_call_target="tpu_custom_call" | custom-call | tf_op jit(solution)/shard_map/pallas_call | solution.py:250
  39.8 2.8 %collective-permute-start = (f32[48,512]{1,0:T(8,128)S(1)}, f32[48,512]{1,0:T(8,128)S(1)}, u32[]{:S(2)}, u32[]{:S(2)}) collective-permute-start(f32[48,512]{1,0:T(8,128)S(1)} %get-tuple-element.14), channel_id=1, source_target_pairs={{0,1},{1,0},{2,3},{3,2},{4,5},{5,4},{6,7},{7,6},{8,9},{9,8},{10,11... | collective-permute-start | bytes 294920 | tf_op jit(solution)/shard_map/ppermute | solution.py:270
  42.6 0.1 collective-permute-start.1
  42.7 0.9 %collective-permute-done.below_ref = f32[48,512]{1,0:T(8,128)S(1)} collective-permute-done((f32[48,512]{1,0:T(8,128)S(1)}, f32[48,512]{1,0:T(8,128)S(1)}, u32[]{:S(2)}, u32[]{:S(2)}) %collective-permute-start) | collective-permute-done | bytes 98336 | tf_op jit(solution)/shard_map/ppermute | solution.py:270
  43.6 0.4 collective-permute-done.1.above_ref
  44.0 2.1 %shard_map.49 = (f32[3,16,16,512]{3,2,1,0:T(8,128)S(1)}, f32[384,128]{1,0:T(8,128)S(1)}) custom-call(f32[3,16,16,512]{3,2,1,0:T(8,128)S(1)} %get-tuple-element.13.field_ref, f32[48,512]{1,0:T(8,128)S(1)} %collective-permute-done.below_ref, f32[48,512]{1,0:T(8,128)S(1)} %collective-permute-done.1.above_ref, f32[3,16,16,512]{3,2,1,0:T(8,128)S(1)} %copy-done.1, ...), custom_call_target="tpu_custom_call" | custom-call | tf_op jit(solution)/shard_map/pallas_call | solution.py:250
  46.1 10.2 %all_to_all.22 = f32[16,24,128]{2,1,0:T(8,128)S(1)} all-to-all(f32[16,24,128]{2,1,0:T(8,128)S(1)} %bitcast.17), channel_id=1, replica_groups=mesh['gx'=16,'gy'=2] {'gx'}, dimensions={0} | all-to-all | bytes 393216 | tf_op jit(solution)/shard_map/all_to_all | solution.py:261
  56.3 0.6 shard_map.50
  56.9 10.9 %all_to_all.23 = f32[16,24,128]{2,1,0:T(8,128)S(1)} all-to-all(f32[16,24,128]{2,1,0:T(8,128)S(1)} %bitcast.15), channel_id=1, replica_groups=mesh['gx'=16,'gy'=2] {'gx'}, dimensions={0} | all-to-all | bytes 393216 | tf_op jit(solution)/shard_map/all_to_all | solution.py:261
  67.8 1.0 %shard_map.51 = (f32[3,16,16,512]{3,2,1,0:T(8,128)S(1)}, f32[48,512]{1,0:T(8,128)S(1)}, f32[48,512]{1,0:T(8,128)S(1)}) custom-call(f32[3,16,16,512]{3,2,1,0:T(8,128)S(1)} %get-tuple-element.16.field_ref, f32[3,16,16,512]{3,2,1,0:T(8,128)S(1)} %copy-done.1, f32[2,3,16,512]{3,2,1,0:T(8,128)S(1)} %copy-done.5, f32[384,128]{1,0:T(8,128)S(1)} %bitcast.12), custom_call_target="tpu_custom_call" | custom-call | tf_op jit(solution)/shard_map/pallas_call | solution.py:250
  68.8 2.6 %collective-permute-start.2 = (f32[48,512]{1,0:T(8,128)S(1)}, f32[48,512]{1,0:T(8,128)S(1)}, u32[]{:S(2)}, u32[]{:S(2)}) collective-permute-start(f32[48,512]{1,0:T(8,128)S(1)} %get-tuple-element.19), channel_id=1, source_target_pairs={{0,1},{1,0},{2,3},{3,2},{4,5},{5,4},{6,7},{7,6},{8,9},{9,8},{10,11... | collective-permute-start | bytes 294920 | tf_op jit(solution)/shard_map/ppermute | solution.py:270
  71.4 0.1 collective-permute-start.3
  71.5 0.9 %collective-permute-done.2.below_ref = f32[48,512]{1,0:T(8,128)S(1)} collective-permute-done((f32[48,512]{1,0:T(8,128)S(1)}, f32[48,512]{1,0:T(8,128)S(1)}, u32[]{:S(2)}, u32[]{:S(2)}) %collective-permute-start.2) | collective-permute-done | bytes 98336 | tf_op jit(solution)/shard_map/ppermute | solution.py:270
  72.3 0.4 collective-permute-done.3.above_ref
  72.7 2.5 %shard_map.52 = f32[3,16,16,512]{3,2,1,0:T(8,128)} custom-call(f32[3,16,16,512]{3,2,1,0:T(8,128)S(1)} %get-tuple-element.18.field_ref, f32[48,512]{1,0:T(8,128)S(1)} %collective-permute-done.2.below_ref, f32[48,512]{1,0:T(8,128)S(1)} %collective-permute-done.3.above_ref, f32[3,16,16,512]{3,2,1,0:T(8,128)S(1)} %copy-done.1), custom_call_target="tpu_custom_call" | custom-call | tf_op jit(solution)/shard_map/pallas_call | solution.py:250
  (9 shorter events, 0.0 us)
Async XLA Ops:
  0.0 1.4 %copy-start = (f32[3,16,16,512]{3,2,1,0:T(8,128)S(1)}, f32[3,16,16,512]{3,2,1,0:T(8,128)}, u32[]{:S(2)}) copy-start(f32[3,16,16,512]{3,2,1,0:T(8,128)} %axes_ref.9) | copy-start | bytes 4718596
  1.4 1.4 %copy-start.2 = (f32[3,16,16,512]{3,2,1,0:T(8,128)S(1)}, f32[3,16,16,512]{3,2,1,0:T(8,128)}, u32[]{:S(2)}) copy-start(f32[3,16,16,512]{3,2,1,0:T(8,128)} %field_ref.3) | copy-start | bytes 4718596
  2.8 0.9 %copy-start.4 = (f32[2,3,16,512]{3,2,1,0:T(8,128)S(1)}, f32[2,3,16,512]{3,2,1,0:T(8,128)}, u32[]{:S(2)}) copy-start(f32[2,3,16,512]{3,2,1,0:T(8,128)} %pins_ref.7) | copy-start | bytes 589828
  3.7 21.6 %copy-start.6 = (f32[32,32]{1,0:T(8,128)S(1)}, f32[32,32]{1,0:T(8,128)}, u32[]{:S(2)}) copy-start(f32[32,32]{1,0:T(8,128)} %constant.2.clone.table_ref) | copy-start | bytes 12292
  5.7 33.2 %copy-start.3 = (f32[3,16,16,512]{3,2,1,0:T(8,128)S(1)}, f32[3,16,16,512]{3,2,1,0:T(8,128)}, u32[]{:S(2)}) copy-start(f32[3,16,16,512]{3,2,1,0:T(8,128)} %field_ref.3) | copy-start | bytes 4718596
  38.8 5.1 %copy-start.1 = (f32[3,16,16,512]{3,2,1,0:T(8,128)S(1)}, f32[3,16,16,512]{3,2,1,0:T(8,128)}, u32[]{:S(2)}) copy-start(f32[3,16,16,512]{3,2,1,0:T(8,128)} %axes_ref.9) | copy-start | bytes 4718596
  38.9 5.1 %copy-start.5 = (f32[2,3,16,512]{3,2,1,0:T(8,128)S(1)}, f32[2,3,16,512]{3,2,1,0:T(8,128)}, u32[]{:S(2)}) copy-start(f32[2,3,16,512]{3,2,1,0:T(8,128)} %pins_ref.7) | copy-start | bytes 589828
  39.8 3.8 %collective-permute-start = (f32[48,512]{1,0:T(8,128)S(1)}, f32[48,512]{1,0:T(8,128)S(1)}, u32[]{:S(2)}, u32[]{:S(2)}) collective-permute-start(f32[48,512]{1,0:T(8,128)S(1)} %get-tuple-element.14), channel_id=1, source_target_pairs={{0,1},{1,0},{2,3},{3,2},{4,5},{5,4},{6,7},{7,6},{8,9},{9,8},{10,11... | collective-permute-start | bytes 294920 | tf_op jit(solution)/shard_map/ppermute | solution.py:270
  42.6 1.3 %collective-permute-start.1 = (f32[48,512]{1,0:T(8,128)S(1)}, f32[48,512]{1,0:T(8,128)S(1)}, u32[]{:S(2)}, u32[]{:S(2)}) collective-permute-start(f32[48,512]{1,0:T(8,128)S(1)} %get-tuple-element.15), channel_id=1, source_target_pairs={{1,0},{0,1},{3,2},{2,3},{5,4},{4,5},{7,6},{6,7},{9,8},{8,9},{11,10... | collective-permute-start | bytes 294920 | tf_op jit(solution)/shard_map/ppermute | solution.py:270
  68.8 3.5 %collective-permute-start.2 = (f32[48,512]{1,0:T(8,128)S(1)}, f32[48,512]{1,0:T(8,128)S(1)}, u32[]{:S(2)}, u32[]{:S(2)}) collective-permute-start(f32[48,512]{1,0:T(8,128)S(1)} %get-tuple-element.19), channel_id=1, source_target_pairs={{0,1},{1,0},{2,3},{3,2},{4,5},{5,4},{6,7},{7,6},{8,9},{9,8},{10,11... | collective-permute-start | bytes 294920 | tf_op jit(solution)/shard_map/ppermute | solution.py:270
  71.4 1.3 %collective-permute-start.3 = (f32[48,512]{1,0:T(8,128)S(1)}, f32[48,512]{1,0:T(8,128)S(1)}, u32[]{:S(2)}, u32[]{:S(2)}) collective-permute-start(f32[48,512]{1,0:T(8,128)S(1)} %get-tuple-element.20), channel_id=1, source_target_pairs={{1,0},{0,1},{3,2},{2,3},{5,4},{4,5},{7,6},{6,7},{9,8},{8,9},{11,10... | collective-permute-start | bytes 294920 | tf_op jit(solution)/shard_map/ppermute | solution.py:270

commit v2 on v1

--- a/solution.py
+++ b/solution.py
@@ -49,25 +49,252 @@
         return solved
 
 
-def ghost_table(line, groups):
-    near, far = line.from_low[0], line.from_low[-1]
-    link = np.zeros((2 * groups, 2 * groups))
-    pick = np.zeros((2 * groups, 2 * groups))
-    for d in range(groups):
-        if d > 0:
-            link[d, groups + d - 1] = near
-            link[groups + d, groups + d - 1] = far
-            pick[d, groups + d - 1] = 1.0
-        if d < groups - 1:
-            link[d, d + 1] = far
-            link[groups + d, d + 1] = near
-            pick[groups + d, d + 1] = 1.0
-    return pick @ np.linalg.inv(np.eye(2 * groups) - link)
-
-
-def row_window(value, values, units, tile, tiles, rows):
-    start = (tile // units) * values * units + value * units + tile % units
-    return pl.ds(start, rows, stride=tiles * values)
+class Level:
+    def __init__(self, length, radix, shift, rows):
+        self.radix, self.shift, self.rows = radix, shift, rows
+        line = Line(length)
+        near, far = line.from_low[0], line.from_low[-1]
+        count = 2 * radix
+        inside = np.kron(np.eye(radix), np.array([[near, far], [far, near]]))
+        pick = np.zeros((count, count))
+        for r in range(radix):
+            if r > 0:
+                pick[2 * r, 2 * r - 1] = 1.0
+            if r < radix - 1:
+                pick[2 * r + 1, 2 * r + 2] = 1.0
+        outer = np.zeros((count, 2))
+        outer[0, 0] = outer[count - 1, 1] = 1.0
+        settle = np.linalg.inv(np.eye(count) - pick @ inside)
+        self.ghosts = settle @ pick
+        self.passed = settle @ outer
+        ends = (np.eye(count) + inside @ self.ghosts)[[0, count - 1]]
+        self.ends = ends
+
+
+def radices_of(groups):
+    found = []
+    while groups > 1:
+        radix = 4 if groups % 4 == 0 else 2
+        assert groups % radix == 0
+        found.append(radix)
+        groups //= radix
+    return found
+
+
+def digit(level):
+    return (lax.axis_index("gx") >> level.shift) & (level.radix - 1)
+
+
+def combine(weights, terms):
+    total = None
+    for weight, term in zip(weights, terms):
+        if weight == 0.0 or term is None:
+            continue
+        part = term * float(weight)
+        total = part if total is None else total + part
+    return total
+
+
+def add(*terms):
+    kept = [t for t in terms if t is not None]
+    total = kept[0] if kept else None
+    for term in kept[1:]:
+        total = total + term
+    return total
+
+
+def times(left, right):
+    return None if right is None else left * right
+
+
+def solve_children(level, rhs, coupling, outer):
+    radix = level.radix
+
+    def settle(values, component):
+        found = []
+        for k in range(2 * radix):
+            own = combine(level.ghosts[k], values)
+            if outer is not None:
+                own = add(own, combine(level.passed[k], outer[component]))
+            found.append(own)
+        return found
+
+    first = rhs[0]
+    ghosts1 = settle(first, 0)
+    second = []
+    for r in range(radix):
+        c, low, high = coupling[r], ghosts1[2 * r], ghosts1[2 * r + 1]
+        second.append(add(rhs[1][2 * r], times(c[0], low), times(c[1], high)))
+        second.append(add(rhs[1][2 * r + 1], times(c[1], low), times(c[2], high)))
+    ghosts2 = settle(second, 1)
+    third = []
+    for r in range(radix):
+        c, low1, high1 = coupling[r], ghosts1[2 * r], ghosts1[2 * r + 1]
+        low2, high2 = ghosts2[2 * r], ghosts2[2 * r + 1]
+        third.append(
+            add(
+                rhs[2][2 * r],
+                times(c[3], low2),
+                times(c[4], high2),
+                times(c[6], low1),
+                times(c[8], high1),
+            )
+        )
+        third.append(
+            add(
+                rhs[2][2 * r + 1],
+                times(c[4], low2),
+                times(c[5], high2),
+                times(c[7], low1),
+                times(c[9], high1),
+            )
+        )
+    return (first, second, third), (ghosts1, ghosts2, third)
+
+
+def merged_coupling(level, coupling):
+    radix = level.radix
+    from_first, from_second, across = [], [], []
+    for side in range(2):
+        passed = level.passed[:, side]
+        moved2, moved3 = [], []
+        for r in range(radix):
+            c, low, high = coupling[r], float(passed[2 * r]), float(passed[2 * r + 1])
+            moved2 += [c[0] * low + c[1] * high, c[1] * low + c[2] * high]
+            moved3 += [c[3] * low + c[4] * high, c[4] * low + c[5] * high]
+        inner = [combine(level.ghosts[k], moved2) for k in range(2 * radix)]
+        through = []
+        for r in range(radix):
+            c, low, high = coupling[r], float(passed[2 * r]), float(passed[2 * r + 1])
+            k_low, k_high = inner[2 * r], inner[2 * r + 1]
+            through.append(
+                add(c[6] * low + c[8] * high, times(c[3], k_low), times(c[4], k_high))
+            )
+            through.append(
+                add(c[7] * low + c[9] * high, times(c[4], k_low), times(c[5], k_high))
+            )
+        for end in range(2):
+            if side <= end:
+                from_first.append(combine(level.ends[end], moved2))
+                from_second.append(combine(level.ends[end], moved3))
+            across.append(combine(level.ends[end], through))
+    return from_first + from_second + across
+
+
+def gather_children(level, received, ordered_ref):
+    position = digit(level)
+    for s in range(level.radix):
+        ordered_ref[position ^ s] = received[s][...]
+
+
+def read_children(level, rhs_ref, coupling_ref):
+    rows, radix = level.rows, level.radix
+
+    def value(ref, r, v):
+        return ref[r, v * rows : (v + 1) * rows, :]
+
+    rhs = [
+        [value(rhs_ref, k // 2, 2 * component + k % 2) for k in range(2 * radix)]
+        for component in range(3)
+    ]
+    coupling = [
+        [value(coupling_ref, r, v) for v in range(RHS, COUPLED)] for r in range(radix)
+    ]
+    return rhs, coupling
+
+
+def up_kernel(level, above, coupled, *refs):
+    radix, rows = level.radix, above.rows
+    received, refs = refs[:radix], refs[radix:]
+    if coupled:
+        outs, (ordered_ref, staged_ref) = refs[:-2], refs[-2:]
+        coupling_ref = ordered_ref
+    else:
+        coupling_ref, refs = refs[0], refs[1:]
+        outs, (ordered_ref, staged_ref) = refs[:-2], refs[-2:]
+    gather_children(level, received, ordered_ref)
+    rhs, coupling = read_children(level, ordered_ref, coupling_ref)
+    seen, _ = solve_children(level, rhs, coupling, None)
+    sent = []
+    for component in range(3):
+        for end in range(2):
+            sent.append(combine(level.ends[end], seen[component]))
+    if coupled:
+        sent += merged_coupling(level, coupling)
+    for v, value in enumerate(sent):
+        for chunk in range(above.radix):
+            staged_ref[chunk, v * rows : (v + 1) * rows, :] = value[
+                chunk * rows : (chunk + 1) * rows
+            ]
+    position = digit(above)
+    for s in range(above.radix):
+        outs[s][...] = staged_ref[position ^ s]
+
+
+def send_down(level, rhs, coupling, outer, outs, staged_ref):
+    rows = level.rows
+    _, (ghosts1, ghosts2, third) = solve_children(level, rhs, coupling, outer)
+    ghosts3 = []
+    for k in range(2 * level.radix):
+        own = combine(level.ghosts[k], third)
+        if outer is not None:
+            own = add(own, combine(level.passed[k], outer[2]))
+        ghosts3.append(own)
+    for component, ghosts in enumerate((ghosts1, ghosts2, ghosts3)):
+        for k, ghost in enumerate(ghosts):
+            v = 2 * component + k % 2
+            if ghost is None:
+                ghost = jnp.zeros((rows, LANES), jnp.float32)
+            staged_ref[k // 2, v * rows : (v + 1) * rows, :] = ghost
+    position = digit(level)
+    for s in range(level.radix):
+        outs[s][...] = staged_ref[position ^ s]
+
+
+def top_kernel(level, coupled, *refs):
+    radix = level.radix
+    received, refs = refs[:radix], refs[radix:]
+    if coupled:
+        outs, (ordered_ref, staged_ref) = refs[:-2], refs[-2:]
+        coupling_ref = ordered_ref
+    else:
+        coupling_ref, refs = refs[0], refs[1:]
+        outs, (ordered_ref, staged_ref) = refs[:-2], refs[-2:]
+    gather_children(level, received, ordered_ref)
+    rhs, coupling = read_children(level, ordered_ref, coupling_ref)
+    send_down(level, rhs, coupling, None, outs, staged_ref)
+
+
+def down_kernel(level, above, *refs):
+    radix, rows = above.radix, above.rows
+    received, refs = refs[:radix], refs[radix:]
+    rhs_ref, coupling_ref, refs = refs[0], refs[1], refs[2:]
+    outs, (ordered_ref, staged_ref) = refs[:-2], refs[-2:]
+    gather_children(above, received, ordered_ref)
+    outer = [
+        [
+            jnp.concatenate(
+                [
+                    ordered_ref[chunk, v * rows : (v + 1) * rows, :]
+                    for chunk in range(above.radix)
+                ],
+                axis=0,
+            )
+            for v in (2 * component, 2 * component + 1)
+        ]
+        for component in range(3)
+    ]
+    rhs, coupling = read_children(level, rhs_ref, coupling_ref)
+    send_down(level, rhs, coupling, outer, outs, staged_ref)
+
+
+def chunk_tiles(level, width):
+    per = width // LANES // level.radix
+    position = digit(level)
+    for s in range(level.radix):
+        for k in range(per):
+            tile = (position ^ s) * per + k
+            yield s, k, pl.ds(pl.multiple_of(tile * LANES, LANES), LANES)
 
 
 def pinned(source, pins_ref, component, lanes):
@@ -129,76 +356,41 @@
     return found
 
 
-def send_edges(line, units, coupled, field_ref, axes_ref, pins_ref, out_ref):
-    rows, width = field_ref.shape[2], field_ref.shape[3]
-    tiles = width // LANES
-    values = COUPLED if coupled else RHS
-    for tile in range(tiles):
-        lanes = slice(tile * LANES, (tile + 1) * LANES)
+def send_edges(line, level, coupled, field_ref, axes_ref, pins_ref, outs):
+    rows, width = field_ref.shape[2:]
+    for s, k, lanes in chunk_tiles(level, width):
         solved = solve_components(line, field_ref, axes_ref, pins_ref, lanes, None)
         sent = []
         for component in range(3):
             sent += [solved[component][0], solved[component][-1]]
         if coupled:
             sent += couplings(line, axes_ref, lanes)
-        for value in range(values):
-            out_ref[row_window(value, values, units, tile, tiles, rows), :] = sent[value]
-
-
-def reduced_kernel(groups, units, rhs_values, rhs_ref, coupling_ref, table_ref, out_ref):
-    def read(ref, values, value):
-        parts = [
-            ref[pl.ds(value * units + u, groups, stride=values * units), :] for u in range(units)
-        ]
-        return jnp.concatenate(parts, axis=1) if units > 1 else parts[0]
-
-    table = table_ref[...]
-
-    def ghosts(first, last):
-        found = jnp.dot(
-            table,
-            jnp.concatenate([first, last], axis=0),
-            precision=lax.Precision.HIGHEST,
-            preferred_element_type=jnp.float32,
-        )
-        return found[:groups], found[groups:]
-
-    rhs = [read(rhs_ref, rhs_values, v) for v in range(RHS)]
-    c = [read(coupling_ref, COUPLED, v) for v in range(RHS, COUPLED)]
-    low1, high1 = ghosts(rhs[0], rhs[1])
-    low2, high2 = ghosts(
-        rhs[2] + c[0] * low1 + c[1] * high1, rhs[3] + c[1] * low1 + c[2] * high1
-    )
-    low3, high3 = ghosts(
-        rhs[4] + c[3] * low2 + c[4] * high2 + c[6] * low1 + c[8] * high1,
-        rhs[5] + c[4] * low2 + c[5] * high2 + c[7] * low1 + c[9] * high1,
-    )
-    for value, found in enumerate((low1, high1, low2, high2, low3, high3)):
-        for u in range(units):
-            out_ref[pl.ds(value * units + u, groups, stride=RHS * units), :] = found[
-                :, u * LANES : (u + 1) * LANES
-            ]
-
-
-def finish_kernel(line, units, field_ref, axes_ref, pins_ref, ghost_ref, out_ref, low_ref, high_ref):
-    planes = line.planes
-    rows, width = field_ref.shape[2], field_ref.shape[3]
-    tiles = width // LANES
-    for tile in range(tiles):
-        lanes = slice(tile * LANES, (tile + 1) * LANES)
-        ghosts = [
-            [
-                ghost_ref[row_window(2 * c + side, RHS, units, tile, tiles, rows), :]
-                for side in range(2)
-            ]
-            for c in range(3)
-        ]
+        for v, value in enumerate(sent):
+            start = v * level.rows + k * rows
+            outs[s][start : start + rows, :] = value
+
+
+def send_kernel(line, level, field_ref, axes_ref, pins_ref, *outs):
+    send_edges(line, level, True, field_ref, axes_ref, pins_ref, outs)
+
+
+def finish_kernel(line, level, *refs):
+    radix, planes = level.radix, line.planes
+    received, refs = refs[:radix], refs[radix:]
+    field_ref, axes_ref, pins_ref, out_ref, low_ref, high_ref = refs
+    rows, width = field_ref.shape[2:]
+    for s, k, lanes in chunk_tiles(level, width):
+        ghosts = []
+        for component in range(3):
+            starts = [(2 * component + side) * level.rows + k * rows for side in range(2)]
+            ghosts.append([received[s][start : start + rows, :] for start in starts])
         solved = solve_components(line, field_ref, axes_ref, pins_ref, lanes, ghosts)
         for c in range(3):
             for i in range(planes):
+                at = c * planes + i
                 out_ref[c, i, :, lanes] = solved[c][i]
-                low_ref[c * planes + i : c * planes + i + 1, lanes] = solved[c][i][:1]
-                high_ref[c * planes + i : c * planes + i + 1, lanes] = solved[c][i][rows - 1 :]
+                low_ref[at : at + 1, lanes] = solved[c][i][:1]
+                high_ref[at : at + 1, lanes] = solved[c][i][rows - 1 :]
 
 
 def rotate(field_ref, below_ref, above_ref, axes_ref, out_ref):
@@ -234,33 +426,35 @@
 
 
 def rotate_and_send_kernel(
-    line, units, field_ref, below_ref, above_ref, axes_ref, pins_ref, out_ref, sent_ref
+    line, level, field_ref, below_ref, above_ref, axes_ref, pins_ref, out_ref, *outs
 ):
     rotate(field_ref, below_ref, above_ref, axes_ref, out_ref)
-    send_edges(line, units, False, out_ref, axes_ref, pins_ref, sent_ref)
+    send_edges(line, level, False, out_ref, axes_ref, pins_ref, outs)
 
 
 VMEM = pl.BlockSpec(memory_space=pltpu.VMEM)
 LIMIT = pltpu.CompilerParams(vmem_limit_bytes=32 * 1024 * 1024)
 
 
-def call(kernel, shapes, *operands):
+def call(kernel, shapes, *operands, scratch=()):
     shapes = [jax.ShapeDtypeStruct(shape, jnp.float32) for shape in shapes]
-    single = len(shapes) == 1
     return pl.pallas_call(
         kernel,
-        out_shape=shapes[0] if single else tuple(shapes),
+        out_shape=tuple(shapes),
         in_specs=[VMEM] * len(operands),
-        out_specs=VMEM if single else (VMEM,) * len(shapes),
+        out_specs=(VMEM,) * len(shapes),
+        scratch_shapes=[pltpu.VMEM(shape, jnp.float32) for shape in scratch],
         compiler_params=LIMIT,
     )(*operands)
 
 
-def exchange(block, groups):
-    parts = block.reshape(groups, -1, LANES)
-    return lax.all_to_all(parts, "gx", split_axis=0, concat_axis=0, tiled=True).reshape(
-        block.shape
-    )
+def exchange(level, blocks):
+    groups = lax.axis_size("gx")
+    received = [blocks[0]]
+    for s in range(1, level.radix):
+        pairs = [(i, i ^ (s << level.shift)) for i in range(groups)]
+        received.append(lax.ppermute(blocks[s], "gx", pairs))
+    return received
 
 
 def to_neighbours(low, high):
@@ -270,51 +464,99 @@
     return lax.ppermute(high, "gy", forward), lax.ppermute(low, "gy", backward)
 
 
+def make_levels(planes, lines, groups):
+    found = []
+    length, rows, shift = planes, lines // LANES, 0
+    for radix in radices_of(groups):
+        rows //= radix
+        found.append(Level(length, radix, shift, rows))
+        length *= radix
+        shift += radix.bit_length() - 1
+    return found
+
+
+def settle_ghosts(levels, blocks, coupled, kept):
+    values = COUPLED if coupled else RHS
+    orders = []
+    for at, level in enumerate(levels):
+        received = exchange(level, blocks)
+        extra = [] if coupled else [kept[at]]
+        ordered = (level.radix, values * level.rows, LANES)
+        down = (RHS * level.rows, LANES)
+        if at + 1 < len(levels):
+            above = levels[at + 1]
+            up = (values * above.rows, LANES)
+            found = call(
+                functools.partial(up_kernel, level, above, coupled),
+                [up] * above.radix + [ordered],
+                *received,
+                *extra,
+                scratch=[(above.radix, values * above.rows, LANES)],
+            )
+        else:
+            found = call(
+                functools.partial(top_kernel, level, coupled),
+                [down] * level.radix + [ordered],
+                *received,
+                *extra,
+                scratch=[(level.radix, RHS * level.rows, LANES)],
+            )
+        blocks, ordered = found[:-1], found[-1]
+        orders.append(ordered)
+    if coupled:
+        kept = orders
+    for at in range(len(levels) - 1, -1, -1):
+        received = exchange(levels[at], blocks)
+        if at == 0:
+            return received, kept
+        level, above = levels[at - 1], levels[at]
+        down = (RHS * level.rows, LANES)
+        blocks = call(
+            functools.partial(down_kernel, level, above),
+            [down] * level.radix,
+            *received,
+            orders[at - 1],
+            kept[at - 1],
+            scratch=[
+                (above.radix, RHS * above.rows, LANES),
+                (level.radix, RHS * level.rows, LANES),
+            ],
+        )
+
+
 def per_device(magnetization, easy_axes, pins):
     _, planes, rows, width = magnetization.shape
     groups = lax.axis_size("gx")
-    units = rows * (width // LANES) // groups
     line = Line(planes)
-    table = jnp.asarray(ghost_table(line, groups), jnp.float32)
+    levels = make_levels(planes, rows * width, groups)
+    lowest = levels[0]
     whole = magnetization.shape
     edge = (3 * planes, width)
-    sent_shape = (groups * RHS * units, LANES)
-    coupled_shape = (groups * COUPLED * units, LANES)
 
     field = magnetization
-    sent = call(
-        functools.partial(send_edges, line, units, True),
-        [coupled_shape],
+    blocks = call(
+        functools.partial(send_kernel, line, lowest),
+        [(COUPLED * lowest.rows, LANES)] * lowest.radix,
         field,
         easy_axes,
         pins,
     )
-    coupling = None
+    kept = None
     for stepno in range(STEPS):
-        gathered = exchange(sent, groups)
-        if stepno == 0:
-            coupling = gathered
-        ghosts = call(
-            functools.partial(reduced_kernel, groups, units, RHS if stepno else COUPLED),
-            [sent_shape],
-            gathered,
-            coupling,
-            table,
-        )
-        ghosts = exchange(ghosts, groups)
+        ghosts, kept = settle_ghosts(levels, blocks, stepno == 0, kept)
         solved, low, high = call(
-            functools.partial(finish_kernel, line, units),
+            functools.partial(finish_kernel, line, lowest),
             [whole, edge, edge],
+            *ghosts,
             field,
             easy_axes,
             pins,
-            ghosts,
         )
         below, above = to_neighbours(low, high)
         if stepno < STEPS - 1:
-            field, sent = call(
-                functools.partial(rotate_and_send_kernel, line, units),
-                [whole, sent_shape],
+            field, *blocks = call(
+                functools.partial(rotate_and_send_kernel, line, lowest),
+                [whole] + [(RHS * lowest.rows, LANES)] * lowest.radix,
                 solved,
                 below,
                 above,
@@ -322,7 +564,7 @@
                 pins,
             )
         else:
-            field = call(rotate, [whole], solved, below, above, easy_axes)
+            (field,) = call(rotate, [whole], solved, below, above, easy_axes)
     return field
 
 

time: 75.7 us -> 82.4 us (1.089)
  blocking collectives: 53.6 us -> 0 us
  starting transfers between devices: 5.55 us -> 39.5 us
  waiting for transfers between devices: 2.44 us -> 27.9 us
  Pallas kernels: 9.82 us -> 10.8 us
    all_to_all x4 -> x0, blocking collectives: 53.6 us -> none  [exchange(): lax.all_to_all(parts, 'gx', split_axis=0, concat_axis=0, tiled=True)]
    ppermute x0 -> x24, starting transfers between devices: none -> 25.9 us  [exchange(): received.append(lax.ppermute(blocks[s], 'gx', pairs))]
    ppermute x0 -> x24, waiting for transfers between devices: none -> 25.5 us  [exchange(): received.append(lax.ppermute(blocks[s], 'gx', pairs))]
    ppermute x2, starting transfers between devices: 5.39 us -> 13.4 us  [to_neighbours(): lax.ppermute(high, 'gy', forward)]
    pallas_call x7 -> x11, Pallas kernels: 9.82 us -> 10.8 us  [call(): pl.pallas_call(kernel, out_shape=tuple(shapes), in_specs=[VMEM] * len(ope...]
    unnamed x14 -> x12, local copies, waits for them, and re-layouts: 3.76 us -> 3.75 us
  transfers between devices with their start and end apart: 4 -> 28, of which waited for: 4 -> 22; matrix products, arithmetic and copies ran while one was open for 0% -> 0% of each run, Pallas kernels for 0% -> 0%
where the time goes in v2:
time: 82.4 us; the launch traced here: 82.1 us
  starting transfers between devices  39.5 us (48%)
  waiting for transfers between devices  27.9 us (34%)
  Pallas kernels  10.8 us (13%)
  local copies, waits for them, and re-layouts  3.75 us (5%)
    ppermute x24, starting transfers between devices, exchange(): received.append(lax.ppermute(blocks[s], 'gx', pairs))  25.9 us
    ppermute x24, waiting for transfers between devices, exchange(): received.append(lax.ppermute(blocks[s], 'gx', pairs))  25.5 us
    ppermute x2, starting transfers between devices, to_neighbours(): lax.ppermute(high, 'gy', forward)  13.4 us
    pallas_call x11, Pallas kernels, call(): pl.pallas_call(kernel, out_shape=tuple(shapes), in_specs=[VMEM] * len(ope...  10.8 us
    unnamed x12, local copies, waits for them, and re-layouts  3.75 us
    ppermute x2, waiting for transfers between devices, to_neighbours(): lax.ppermute(high, 'gy', forward)  1.73 us
  transfers between devices with their start and end apart: 28, of which 22 were waited for; matrix products, arithmetic and copies ran while one was open for 0% of the time, Pallas kernels for 0%

profile of v2, /device:TPU:1, one launch (start us, length us, event | category | flops | bytes accessed | tf_op | source)
XLA Modules:
  0.0 82.1 jit_solution(18222609480201322463)
XLA Ops:
  0.0 1.4 %copy-done = f32[3,16,16,512]{3,2,1,0:T(8,128)S(1)} copy-done((f32[3,16,16,512]{3,2,1,0:T(8,128)S(1)}, f32[3,16,16,512]{3,2,1,0:T(8,128)}, u32[]{:S(2)}) %copy-start) | copy-done | bytes 1572888
  1.4 1.4 %copy-done.2 = f32[3,16,16,512]{3,2,1,0:T(8,128)S(1)} copy-done((f32[3,16,16,512]{3,2,1,0:T(8,128)S(1)}, f32[3,16,16,512]{3,2,1,0:T(8,128)}, u32[]{:S(2)}) %copy-start.2) | copy-done | bytes 1572888
  3.7 1.8 %shard_map.37 = (f32[256,128]{1,0:T(8,128)S(1)}, f32[256,128]{1,0:T(8,128)S(1)}, f32[256,128]{1,0:T(8,128)S(1)}, f32[256,128]{1,0:T(8,128)S(1)}) custom-call(f32[3,16,16,512]{3,2,1,0:T(8,128)S(1)} %copy-done.2, f32[3,16,16,512]{3,2,1,0:T(8,128)S(1)} %copy-done, f32[2,3,16,512]{3,2,1,0:T(8,128)S(1)} %copy-done.4), custom_call_target="tpu_custom_call" | custom-call | tf_op jit(solution)/shard_map/pallas_call | solution.py:441
  5.6 2.1 %collective-permute-start = (f32[256,128]{1,0:T(8,128)S(1)}, f32[256,128]{1,0:T(8,128)S(1)}, u32[]{:S(2)}, u32[]{:S(2)}) collective-permute-start(f32[256,128]{1,0:T(8,128)S(1)} %get-tuple-element.48), channel_id=1, source_target_pairs={{0,2},{2,0},{4,6},{6,4},{8,10},{10,8},{12,14},{14,12},{16,18},{18,... | collective-permute-start | bytes 393224 | tf_op jit(solution)/shard_map/ppermute | solution.py:456
  8.9 2.0 %collective-permute-done.refs_1_ = f32[256,128]{1,0:T(8,128)S(1)} collective-permute-done((f32[256,128]{1,0:T(8,128)S(1)}, f32[256,128]{1,0:T(8,128)S(1)}, u32[]{:S(2)}, u32[]{:S(2)}) %collective-permute-start) | collective-permute-done | bytes 131104 | tf_op jit(solution)/shard_map/ppermute | solution.py:456
  11.8 2.7 %collective-permute-done.2.refs_3_ = f32[256,128]{1,0:T(8,128)S(1)} collective-permute-done((f32[256,128]{1,0:T(8,128)S(1)}, f32[256,128]{1,0:T(8,128)S(1)}, u32[]{:S(2)}, u32[]{:S(2)}) %collective-permute-start.2) | collective-permute-done | bytes 131104 | tf_op jit(solution)/shard_map/ppermute | solution.py:456
  14.7 1.4 %collective-permute-start.3 = (f32[64,128]{1,0:T(8,128)S(1)}, f32[64,128]{1,0:T(8,128)S(1)}, u32[]{:S(2)}, u32[]{:S(2)}) collective-permute-start(f32[64,128]{1,0:T(8,128)S(1)} %get-tuple-element.52), channel_id=1, source_target_pairs={{0,8},{2,10},{4,12},{6,14},{8,0},{10,2},{12,4},{14,6},{16,24},{18,... | collective-permute-start | bytes 98312 | tf_op jit(solution)/shard_map/ppermute | solution.py:456
  16.0 2.3 %collective-permute-start.4 = (f32[64,128]{1,0:T(8,128)S(1)}, f32[64,128]{1,0:T(8,128)S(1)}, u32[]{:S(2)}, u32[]{:S(2)}) collective-permute-start(f32[64,128]{1,0:T(8,128)S(1)} %get-tuple-element.53), channel_id=1, source_target_pairs={{0,16},{2,18},{4,20},{6,22},{8,24},{10,26},{12,28},{14,30},{16,0},... | collective-permute-start | bytes 98312 | tf_op jit(solution)/shard_map/ppermute | solution.py:456
  18.4 1.7 %collective-permute-done.4.refs_2_ = f32[64,128]{1,0:T(8,128)S(1)} collective-permute-done((f32[64,128]{1,0:T(8,128)S(1)}, f32[64,128]{1,0:T(8,128)S(1)}, u32[]{:S(2)}, u32[]{:S(2)}) %collective-permute-start.4) | collective-permute-done | bytes 32800 | tf_op jit(solution)/shard_map/ppermute | solution.py:456
  20.1 2.9 %collective-permute-done.5.refs_3_ = f32[64,128]{1,0:T(8,128)S(1)} collective-permute-done((f32[64,128]{1,0:T(8,128)S(1)}, f32[64,128]{1,0:T(8,128)S(1)}, u32[]{:S(2)}, u32[]{:S(2)}) %collective-permute-start.5) | collective-permute-done | bytes 32800 | tf_op jit(solution)/shard_map/ppermute | solution.py:456
  24.0 2.6 %collective-permute-start.8 = (f32[24,128]{1,0:T(8,128)S(1)}, f32[24,128]{1,0:T(8,128)S(1)}, u32[]{:S(2)}, u32[]{:S(2)}) collective-permute-start(f32[24,128]{1,0:T(8,128)S(1)} %get-tuple-element.58), channel_id=1, source_target_pairs={{0,24},{2,26},{4,28},{6,30},{8,16},{10,18},{12,20},{14,22},{16,8},... | collective-permute-start | bytes 36872 | tf_op jit(solution)/shard_map/ppermute | solution.py:456
  26.6 1.8 %collective-permute-done.8.refs_3_ = f32[24,128]{1,0:T(8,128)S(1)} collective-permute-done((f32[24,128]{1,0:T(8,128)S(1)}, f32[24,128]{1,0:T(8,128)S(1)}, u32[]{:S(2)}, u32[]{:S(2)}) %collective-permute-start.8) | collective-permute-done | bytes 12320 | tf_op jit(solution)/shard_map/ppermute | solution.py:456
  32.7 1.3 %collective-permute-done.11.refs_3_ = f32[96,128]{1,0:T(8,128)S(1)} collective-permute-done((f32[96,128]{1,0:T(8,128)S(1)}, f32[96,128]{1,0:T(8,128)S(1)}, u32[]{:S(2)}, u32[]{:S(2)}) %collective-permute-start.11) | collective-permute-done | bytes 49184 | tf_op jit(solution)/shard_map/ppermute | solution.py:456
  34.0 1.4 %shard_map.41 = (f32[3,16,16,512]{3,2,1,0:T(8,128)S(1)}, f32[48,512]{1,0:T(8,128)S(1)}, f32[48,512]{1,0:T(8,128)S(1)}) custom-call(f32[96,128]{1,0:T(8,128)S(1)} %get-tuple-element.60.refs_0_, f32[96,128]{1,0:T(8,128)S(1)} %collective-permute-done.9.refs_1_, f32[96,128]{1,0:T(8,128)S(1)} %collective-permute-done.10.refs_2_, ...), custom_call_target="tpu_custom_call" | custom-call | tf_op jit(solution)/shard_map/pallas_call | solution.py:441
  35.4 6.4 %collective-permute-start.12 = (f32[48,512]{1,0:T(8,128)S(1)}, f32[48,512]{1,0:T(8,128)S(1)}, u32[]{:S(2)}, u32[]{:S(2)}) collective-permute-start(f32[48,512]{1,0:T(8,128)S(1)} %get-tuple-element.65), channel_id=1, source_target_pairs={{0,1},{1,0},{2,3},{3,2},{4,5},{5,4},{6,7},{7,6},{8,9},{9,8},{10,11... | collective-permute-start | bytes 294920 | tf_op jit(solution)/shard_map/ppermute | solution.py:464
  43.1 2.5 %shard_map.42 = (f32[3,16,16,512]{3,2,1,0:T(8,128)S(1)}, f32[96,128]{1,0:T(8,128)S(1)}, f32[96,128]{1,0:T(8,128)S(1)}, f32[96,128]{1,0:T(8,128)S(1)}, f32[96,128]{1,0:T(8,128)S(1)}) custom-call(f32[3,16,16,512]{3,2,1,0:T(8,128)S(1)} %get-tuple-element.64.field_ref, f32[48,512]{1,0:T(8,128)S(1)} %collective-permute-done.12.below_ref, ...), custom_call_target="tpu_custom_call" | custom-call | tf_op jit(solution)/shard_map/pallas_call | solution.py:441
  45.6 1.3 %collective-permute-start.14 = (f32[96,128]{1,0:T(8,128)S(1)}, f32[96,128]{1,0:T(8,128)S(1)}, u32[]{:S(2)}, u32[]{:S(2)}) collective-permute-start(f32[96,128]{1,0:T(8,128)S(1)} %get-tuple-element.68), channel_id=1, source_target_pairs={{0,2},{2,0},{4,6},{6,4},{8,10},{10,8},{12,14},{14,12},{16,18},{18,... | collective-permute-start | bytes 147464 | tf_op jit(solution)/shard_map/ppermute | solution.py:456
  51.2 3.5 %collective-permute-start.18 = (f32[24,128]{1,0:T(8,128)S(1)}, f32[24,128]{1,0:T(8,128)S(1)}, u32[]{:S(2)}, u32[]{:S(2)}) collective-permute-start(f32[24,128]{1,0:T(8,128)S(1)} %get-tuple-element.73), channel_id=1, source_target_pairs={{0,16},{2,18},{4,20},{6,22},{8,24},{10,26},{12,28},{14,30},{16,0},... | collective-permute-start | bytes 36872 | tf_op jit(solution)/shard_map/ppermute | solution.py:456
  55.8 3.2 %collective-permute-done.19.refs_3_ = f32[24,128]{1,0:T(8,128)S(1)} collective-permute-done((f32[24,128]{1,0:T(8,128)S(1)}, f32[24,128]{1,0:T(8,128)S(1)}, u32[]{:S(2)}, u32[]{:S(2)}) %collective-permute-start.19) | collective-permute-done | bytes 12320 | tf_op jit(solution)/shard_map/ppermute | solution.py:456
  60.1 3.1 %collective-permute-start.22 = (f32[24,128]{1,0:T(8,128)S(1)}, f32[24,128]{1,0:T(8,128)S(1)}, u32[]{:S(2)}, u32[]{:S(2)}) collective-permute-start(f32[24,128]{1,0:T(8,128)S(1)} %get-tuple-element.79), channel_id=1, source_target_pairs={{0,24},{2,26},{4,28},{6,30},{8,16},{10,18},{12,20},{14,22},{16,8},... | collective-permute-start | bytes 36872 | tf_op jit(solution)/shard_map/ppermute | solution.py:456
  66.1 1.3 %collective-permute-start.25 = (f32[96,128]{1,0:T(8,128)S(1)}, f32[96,128]{1,0:T(8,128)S(1)}, u32[]{:S(2)}, u32[]{:S(2)}) collective-permute-start(f32[96,128]{1,0:T(8,128)S(1)} %get-tuple-element.84), channel_id=1, source_target_pairs={{0,6},{2,4},{4,2},{6,0},{8,14},{10,12},{12,10},{14,8},{16,22},{18,... | collective-permute-start | bytes 147464 | tf_op jit(solution)/shard_map/ppermute | solution.py:456
  69.9 1.4 %shard_map.46 = (f32[3,16,16,512]{3,2,1,0:T(8,128)S(1)}, f32[48,512]{1,0:T(8,128)S(1)}, f32[48,512]{1,0:T(8,128)S(1)}) custom-call(f32[96,128]{1,0:T(8,128)S(1)} %get-tuple-element.81.refs_0_, f32[96,128]{1,0:T(8,128)S(1)} %collective-permute-done.23.refs_1_, f32[96,128]{1,0:T(8,128)S(1)} %collective-permute-done.24.refs_2_, ...), custom_call_target="tpu_custom_call" | custom-call | tf_op jit(solution)/shard_map/pallas_call | solution.py:441
  71.3 7.0 %collective-permute-start.26 = (f32[48,512]{1,0:T(8,128)S(1)}, f32[48,512]{1,0:T(8,128)S(1)}, u32[]{:S(2)}, u32[]{:S(2)}) collective-permute-start(f32[48,512]{1,0:T(8,128)S(1)} %get-tuple-element.87), channel_id=1, source_target_pairs={{0,1},{1,0},{2,3},{3,2},{4,5},{5,4},{6,7},{7,6},{8,9},{9,8},{10,11... | collective-permute-start | bytes 294920 | tf_op jit(solution)/shard_map/ppermute | solution.py:464
  79.5 2.5 %shard_map.47 = f32[3,16,16,512]{3,2,1,0:T(8,128)} custom-call(f32[3,16,16,512]{3,2,1,0:T(8,128)S(1)} %get-tuple-element.86.field_ref, f32[48,512]{1,0:T(8,128)S(1)} %collective-permute-done.26.below_ref, f32[48,512]{1,0:T(8,128)S(1)} %collective-permute-done.27.above_ref, f32[3,16,16,512]{3,2,1,0:T(8,128)S(1)} %copy-done.1), custom_call_target="tpu_custom_call" | custom-call | tf_op jit(solution)/shard_map/pallas_call | solution.py:441
  (55 shorter events, 23.3 us)
Async XLA Ops:
  5.6 5.3 %collective-permute-start = (f32[256,128]{1,0:T(8,128)S(1)}, f32[256,128]{1,0:T(8,128)S(1)}, u32[]{:S(2)}, u32[]{:S(2)}) collective-permute-start(f32[256,128]{1,0:T(8,128)S(1)} %get-tuple-element.48), channel_id=1, source_target_pairs={{0,2},{2,0},{4,6},{6,4},{8,10},{10,8},{12,14},{14,12},{16,18},{18,... | collective-permute-start | bytes 393224 | tf_op jit(solution)/shard_map/ppermute | solution.py:456
  7.6 4.1 %collective-permute-start.1 = (f32[256,128]{1,0:T(8,128)S(1)}, f32[256,128]{1,0:T(8,128)S(1)}, u32[]{:S(2)}, u32[]{:S(2)}) collective-permute-start(f32[256,128]{1,0:T(8,128)S(1)} %get-tuple-element.49), channel_id=1, source_target_pairs={{0,4},{2,6},{4,0},{6,2},{8,12},{10,14},{12,8},{14,10},{16,20},{18,... | collective-permute-start | bytes 393224 | tf_op jit(solution)/shard_map/ppermute | solution.py:456
  8.9 5.5 %collective-permute-start.2 = (f32[256,128]{1,0:T(8,128)S(1)}, f32[256,128]{1,0:T(8,128)S(1)}, u32[]{:S(2)}, u32[]{:S(2)}) collective-permute-start(f32[256,128]{1,0:T(8,128)S(1)} %get-tuple-element.50), channel_id=1, source_target_pairs={{0,6},{2,4},{4,2},{6,0},{8,14},{10,12},{12,10},{14,8},{16,22},{18,... | collective-permute-start | bytes 393224 | tf_op jit(solution)/shard_map/ppermute | solution.py:456
  14.7 3.7 %collective-permute-start.3 = (f32[64,128]{1,0:T(8,128)S(1)}, f32[64,128]{1,0:T(8,128)S(1)}, u32[]{:S(2)}, u32[]{:S(2)}) collective-permute-start(f32[64,128]{1,0:T(8,128)S(1)} %get-tuple-element.52), channel_id=1, source_target_pairs={{0,8},{2,10},{4,12},{6,14},{8,0},{10,2},{12,4},{14,6},{16,24},{18,... | collective-permute-start | bytes 98312 | tf_op jit(solution)/shard_map/ppermute | solution.py:456
  16.0 4.0 %collective-permute-start.4 = (f32[64,128]{1,0:T(8,128)S(1)}, f32[64,128]{1,0:T(8,128)S(1)}, u32[]{:S(2)}, u32[]{:S(2)}) collective-permute-start(f32[64,128]{1,0:T(8,128)S(1)} %get-tuple-element.53), channel_id=1, source_target_pairs={{0,16},{2,18},{4,20},{6,22},{8,24},{10,26},{12,28},{14,30},{16,0},... | collective-permute-start | bytes 98312 | tf_op jit(solution)/shard_map/ppermute | solution.py:456
  18.3 4.6 %collective-permute-start.5 = (f32[64,128]{1,0:T(8,128)S(1)}, f32[64,128]{1,0:T(8,128)S(1)}, u32[]{:S(2)}, u32[]{:S(2)}) collective-permute-start(f32[64,128]{1,0:T(8,128)S(1)} %get-tuple-element.54), channel_id=1, source_target_pairs={{0,24},{2,26},{4,28},{6,30},{8,16},{10,18},{12,20},{14,22},{16,8},... | collective-permute-start | bytes 98312 | tf_op jit(solution)/shard_map/ppermute | solution.py:456
  23.0 3.6 %collective-permute-start.6 = (f32[24,128]{1,0:T(8,128)S(1)}, f32[24,128]{1,0:T(8,128)S(1)}, u32[]{:S(2)}, u32[]{:S(2)}) collective-permute-start(f32[24,128]{1,0:T(8,128)S(1)} %get-tuple-element.56), channel_id=1, source_target_pairs={{0,8},{2,10},{4,12},{6,14},{8,0},{10,2},{12,4},{14,6},{16,24},{18,... | collective-permute-start | bytes 36872 | tf_op jit(solution)/shard_map/ppermute | solution.py:456
  23.1 3.5 %collective-permute-start.7 = (f32[24,128]{1,0:T(8,128)S(1)}, f32[24,128]{1,0:T(8,128)S(1)}, u32[]{:S(2)}, u32[]{:S(2)}) collective-permute-start(f32[24,128]{1,0:T(8,128)S(1)} %get-tuple-element.57), channel_id=1, source_target_pairs={{0,16},{2,18},{4,20},{6,22},{8,24},{10,26},{12,28},{14,30},{16,0},... | collective-permute-start | bytes 36872 | tf_op jit(solution)/shard_map/ppermute | solution.py:456
  24.0 4.4 %collective-permute-start.8 = (f32[24,128]{1,0:T(8,128)S(1)}, f32[24,128]{1,0:T(8,128)S(1)}, u32[]{:S(2)}, u32[]{:S(2)}) collective-permute-start(f32[24,128]{1,0:T(8,128)S(1)} %get-tuple-element.58), channel_id=1, source_target_pairs={{0,24},{2,26},{4,28},{6,30},{8,16},{10,18},{12,20},{14,22},{16,8},... | collective-permute-start | bytes 36872 | tf_op jit(solution)/shard_map/ppermute | solution.py:456
  28.5 3.0 %collective-permute-start.9 = (f32[96,128]{1,0:T(8,128)S(1)}, f32[96,128]{1,0:T(8,128)S(1)}, u32[]{:S(2)}, u32[]{:S(2)}) collective-permute-start(f32[96,128]{1,0:T(8,128)S(1)} %get-tuple-element.61), channel_id=1, source_target_pairs={{0,2},{2,0},{4,6},{6,4},{8,10},{10,8},{12,14},{14,12},{16,18},{18,... | collective-permute-start | bytes 147464 | tf_op jit(solution)/shard_map/ppermute | solution.py:456
  29.6 3.1 %collective-permute-start.10 = (f32[96,128]{1,0:T(8,128)S(1)}, f32[96,128]{1,0:T(8,128)S(1)}, u32[]{:S(2)}, u32[]{:S(2)}) collective-permute-start(f32[96,128]{1,0:T(8,128)S(1)} %get-tuple-element.62), channel_id=1, source_target_pairs={{0,4},{2,6},{4,0},{6,2},{8,12},{10,14},{12,8},{14,10},{16,20},{18,... | collective-permute-start | bytes 147464 | tf_op jit(solution)/shard_map/ppermute | solution.py:456
  30.2 3.8 %collective-permute-start.11 = (f32[96,128]{1,0:T(8,128)S(1)}, f32[96,128]{1,0:T(8,128)S(1)}, u32[]{:S(2)}, u32[]{:S(2)}) collective-permute-start(f32[96,128]{1,0:T(8,128)S(1)} %get-tuple-element.63), channel_id=1, source_target_pairs={{0,6},{2,4},{4,2},{6,0},{8,14},{10,12},{12,10},{14,8},{16,22},{18,... | collective-permute-start | bytes 147464 | tf_op jit(solution)/shard_map/ppermute | solution.py:456
  35.4 7.4 %collective-permute-start.12 = (f32[48,512]{1,0:T(8,128)S(1)}, f32[48,512]{1,0:T(8,128)S(1)}, u32[]{:S(2)}, u32[]{:S(2)}) collective-permute-start(f32[48,512]{1,0:T(8,128)S(1)} %get-tuple-element.65), channel_id=1, source_target_pairs={{0,1},{1,0},{2,3},{3,2},{4,5},{5,4},{6,7},{7,6},{8,9},{9,8},{10,11... | collective-permute-start | bytes 294920 | tf_op jit(solution)/shard_map/ppermute | solution.py:464
  47.1 3.9 %collective-permute-start.16 = (f32[96,128]{1,0:T(8,128)S(1)}, f32[96,128]{1,0:T(8,128)S(1)}, u32[]{:S(2)}, u32[]{:S(2)}) collective-permute-start(f32[96,128]{1,0:T(8,128)S(1)} %get-tuple-element.70), channel_id=1, source_target_pairs={{0,6},{2,4},{4,2},{6,0},{8,14},{10,12},{12,10},{14,8},{16,22},{18,... | collective-permute-start | bytes 147464 | tf_op jit(solution)/shard_map/ppermute | solution.py:456
  51.2 3.6 %collective-permute-start.17 = (f32[24,128]{1,0:T(8,128)S(1)}, f32[24,128]{1,0:T(8,128)S(1)}, u32[]{:S(2)}, u32[]{:S(2)}) collective-permute-start(f32[24,128]{1,0:T(8,128)S(1)} %get-tuple-element.72), channel_id=1, source_target_pairs={{0,8},{2,10},{4,12},{6,14},{8,0},{10,2},{12,4},{14,6},{16,24},{18,... | collective-permute-start | bytes 36872 | tf_op jit(solution)/shard_map/ppermute | solution.py:456
  51.2 4.6 %collective-permute-start.18 = (f32[24,128]{1,0:T(8,128)S(1)}, f32[24,128]{1,0:T(8,128)S(1)}, u32[]{:S(2)}, u32[]{:S(2)}) collective-permute-start(f32[24,128]{1,0:T(8,128)S(1)} %get-tuple-element.73), channel_id=1, source_target_pairs={{0,16},{2,18},{4,20},{6,22},{8,24},{10,26},{12,28},{14,30},{16,0},... | collective-permute-start | bytes 36872 | tf_op jit(solution)/shard_map/ppermute | solution.py:456
  54.7 4.3 %collective-permute-start.19 = (f32[24,128]{1,0:T(8,128)S(1)}, f32[24,128]{1,0:T(8,128)S(1)}, u32[]{:S(2)}, u32[]{:S(2)}) collective-permute-start(f32[24,128]{1,0:T(8,128)S(1)} %get-tuple-element.74), channel_id=1, source_target_pairs={{0,24},{2,26},{4,28},{6,30},{8,16},{10,18},{12,20},{14,22},{16,8},... | collective-permute-start | bytes 36872 | tf_op jit(solution)/shard_map/ppermute | solution.py:456
  59.7 3.6 %collective-permute-start.20 = (f32[24,128]{1,0:T(8,128)S(1)}, f32[24,128]{1,0:T(8,128)S(1)}, u32[]{:S(2)}, u32[]{:S(2)}) collective-permute-start(f32[24,128]{1,0:T(8,128)S(1)} %get-tuple-element.77), channel_id=1, source_target_pairs={{0,8},{2,10},{4,12},{6,14},{8,0},{10,2},{12,4},{14,6},{16,24},{18,... | collective-permute-start | bytes 36872 | tf_op jit(solution)/shard_map/ppermute | solution.py:456
  59.7 3.6 %collective-permute-start.21 = (f32[24,128]{1,0:T(8,128)S(1)}, f32[24,128]{1,0:T(8,128)S(1)}, u32[]{:S(2)}, u32[]{:S(2)}) collective-permute-start(f32[24,128]{1,0:T(8,128)S(1)} %get-tuple-element.78), channel_id=1, source_target_pairs={{0,16},{2,18},{4,20},{6,22},{8,24},{10,26},{12,28},{14,30},{16,0},... | collective-permute-start | bytes 36872 | tf_op jit(solution)/shard_map/ppermute | solution.py:456
  60.1 4.3 %collective-permute-start.22 = (f32[24,128]{1,0:T(8,128)S(1)}, f32[24,128]{1,0:T(8,128)S(1)}, u32[]{:S(2)}, u32[]{:S(2)}) collective-permute-start(f32[24,128]{1,0:T(8,128)S(1)} %get-tuple-element.79), channel_id=1, source_target_pairs={{0,24},{2,26},{4,28},{6,30},{8,16},{10,18},{12,20},{14,22},{16,8},... | collective-permute-start | bytes 36872 | tf_op jit(solution)/shard_map/ppermute | solution.py:456
  64.6 3.0 %collective-permute-start.23 = (f32[96,128]{1,0:T(8,128)S(1)}, f32[96,128]{1,0:T(8,128)S(1)}, u32[]{:S(2)}, u32[]{:S(2)}) collective-permute-start(f32[96,128]{1,0:T(8,128)S(1)} %get-tuple-element.82), channel_id=1, source_target_pairs={{0,2},{2,0},{4,6},{6,4},{8,10},{10,8},{12,14},{14,12},{16,18},{18,... | collective-permute-start | bytes 147464 | tf_op jit(solution)/shard_map/ppermute | solution.py:456
  65.5 3.2 %collective-permute-start.24 = (f32[96,128]{1,0:T(8,128)S(1)}, f32[96,128]{1,0:T(8,128)S(1)}, u32[]{:S(2)}, u32[]{:S(2)}) collective-permute-start(f32[96,128]{1,0:T(8,128)S(1)} %get-tuple-element.83), channel_id=1, source_target_pairs={{0,4},{2,6},{4,0},{6,2},{8,12},{10,14},{12,8},{14,10},{16,20},{18,... | collective-permute-start | bytes 147464 | tf_op jit(solution)/shard_map/ppermute | solution.py:456
  66.1 3.8 %collective-permute-start.25 = (f32[96,128]{1,0:T(8,128)S(1)}, f32[96,128]{1,0:T(8,128)S(1)}, u32[]{:S(2)}, u32[]{:S(2)}) collective-permute-start(f32[96,128]{1,0:T(8,128)S(1)} %get-tuple-element.84), channel_id=1, source_target_pairs={{0,6},{2,4},{4,2},{6,0},{8,14},{10,12},{12,10},{14,8},{16,22},{18,... | collective-permute-start | bytes 147464 | tf_op jit(solution)/shard_map/ppermute | solution.py:456
  71.3 7.9 %collective-permute-start.26 = (f32[48,512]{1,0:T(8,128)S(1)}, f32[48,512]{1,0:T(8,128)S(1)}, u32[]{:S(2)}, u32[]{:S(2)}) collective-permute-start(f32[48,512]{1,0:T(8,128)S(1)} %get-tuple-element.87), channel_id=1, source_target_pairs={{0,1},{1,0},{2,3},{3,2},{4,5},{5,4},{6,7},{7,6},{8,9},{9,8},{10,11... | collective-permute-start | bytes 294920 | tf_op jit(solution)/shard_map/ppermute | solution.py:464
  (10 other events, 59.0 us)

commit v3 on v2

--- a/solution.py
+++ b/solution.py
@@ -81,10 +81,6 @@
     return found
 
 
-def digit(level):
-    return (lax.axis_index("gx") >> level.shift) & (level.radix - 1)
-
-
 def combine(weights, terms):
     total = None
     for weight, term in zip(weights, terms):
@@ -181,12 +177,6 @@
     return from_first + from_second + across
 
 
-def gather_children(level, received, ordered_ref):
-    position = digit(level)
-    for s in range(level.radix):
-        ordered_ref[position ^ s] = received[s][...]
-
-
 def read_children(level, rhs_ref, coupling_ref):
     rows, radix = level.rows, level.radix
 
@@ -203,17 +193,9 @@
     return rhs, coupling
 
 
-def up_kernel(level, above, coupled, *refs):
-    radix, rows = level.radix, above.rows
-    received, refs = refs[:radix], refs[radix:]
-    if coupled:
-        outs, (ordered_ref, staged_ref) = refs[:-2], refs[-2:]
-        coupling_ref = ordered_ref
-    else:
-        coupling_ref, refs = refs[0], refs[1:]
-        outs, (ordered_ref, staged_ref) = refs[:-2], refs[-2:]
-    gather_children(level, received, ordered_ref)
-    rhs, coupling = read_children(level, ordered_ref, coupling_ref)
+def up_kernel(level, above, coupled, rhs_ref, coupling_ref, out_ref):
+    rows = above.rows
+    rhs, coupling = read_children(level, rhs_ref, coupling_ref)
     seen, _ = solve_children(level, rhs, coupling, None)
     sent = []
     for component in range(3):
@@ -223,15 +205,12 @@
         sent += merged_coupling(level, coupling)
     for v, value in enumerate(sent):
         for chunk in range(above.radix):
-            staged_ref[chunk, v * rows : (v + 1) * rows, :] = value[
+            out_ref[chunk, v * rows : (v + 1) * rows, :] = value[
                 chunk * rows : (chunk + 1) * rows
             ]
-    position = digit(above)
-    for s in range(above.radix):
-        outs[s][...] = staged_ref[position ^ s]
-
-
-def send_down(level, rhs, coupling, outer, outs, staged_ref):
+
+
+def send_down(level, rhs, coupling, outer, out_ref):
     rows = level.rows
     _, (ghosts1, ghosts2, third) = solve_children(level, rhs, coupling, outer)
     ghosts3 = []
@@ -245,37 +224,21 @@
             v = 2 * component + k % 2
             if ghost is None:
                 ghost = jnp.zeros((rows, LANES), jnp.float32)
-            staged_ref[k // 2, v * rows : (v + 1) * rows, :] = ghost
-    position = digit(level)
-    for s in range(level.radix):
-        outs[s][...] = staged_ref[position ^ s]
-
-
-def top_kernel(level, coupled, *refs):
-    radix = level.radix
-    received, refs = refs[:radix], refs[radix:]
-    if coupled:
-        outs, (ordered_ref, staged_ref) = refs[:-2], refs[-2:]
-        coupling_ref = ordered_ref
-    else:
-        coupling_ref, refs = refs[0], refs[1:]
-        outs, (ordered_ref, staged_ref) = refs[:-2], refs[-2:]
-    gather_children(level, received, ordered_ref)
-    rhs, coupling = read_children(level, ordered_ref, coupling_ref)
-    send_down(level, rhs, coupling, None, outs, staged_ref)
-
-
-def down_kernel(level, above, *refs):
-    radix, rows = above.radix, above.rows
-    received, refs = refs[:radix], refs[radix:]
-    rhs_ref, coupling_ref, refs = refs[0], refs[1], refs[2:]
-    outs, (ordered_ref, staged_ref) = refs[:-2], refs[-2:]
-    gather_children(above, received, ordered_ref)
+            out_ref[k // 2, v * rows : (v + 1) * rows, :] = ghost
+
+
+def top_kernel(level, rhs_ref, coupling_ref, out_ref):
+    rhs, coupling = read_children(level, rhs_ref, coupling_ref)
+    send_down(level, rhs, coupling, None, out_ref)
+
+
+def down_kernel(level, above, outer_ref, rhs_ref, coupling_ref, out_ref):
+    rows = above.rows
     outer = [
         [
             jnp.concatenate(
                 [
-                    ordered_ref[chunk, v * rows : (v + 1) * rows, :]
+                    outer_ref[chunk, v * rows : (v + 1) * rows, :]
                     for chunk in range(above.radix)
                 ],
                 axis=0,
@@ -285,16 +248,15 @@
         for component in range(3)
     ]
     rhs, coupling = read_children(level, rhs_ref, coupling_ref)
-    send_down(level, rhs, coupling, outer, outs, staged_ref)
+    send_down(level, rhs, coupling, outer, out_ref)
 
 
 def chunk_tiles(level, width):
     per = width // LANES // level.radix
-    position = digit(level)
-    for s in range(level.radix):
+    for chunk in range(level.radix):
         for k in range(per):
-            tile = (position ^ s) * per + k
-            yield s, k, pl.ds(pl.multiple_of(tile * LANES, LANES), LANES)
+            tile = chunk * per + k
+            yield chunk, k, slice(tile * LANES, (tile + 1) * LANES)
 
 
 def pinned(source, pins_ref, component, lanes):
@@ -356,9 +318,9 @@
     return found
 
 
-def send_edges(line, level, coupled, field_ref, axes_ref, pins_ref, outs):
+def send_edges(line, level, coupled, field_ref, axes_ref, pins_ref, out_ref):
     rows, width = field_ref.shape[2:]
-    for s, k, lanes in chunk_tiles(level, width):
+    for chunk, k, lanes in chunk_tiles(level, width):
         solved = solve_components(line, field_ref, axes_ref, pins_ref, lanes, None)
         sent = []
         for component in range(3):
@@ -367,23 +329,23 @@
             sent += couplings(line, axes_ref, lanes)
         for v, value in enumerate(sent):
             start = v * level.rows + k * rows
-            outs[s][start : start + rows, :] = value
-
-
-def send_kernel(line, level, field_ref, axes_ref, pins_ref, *outs):
-    send_edges(line, level, True, field_ref, axes_ref, pins_ref, outs)
-
-
-def finish_kernel(line, level, *refs):
-    radix, planes = level.radix, line.planes
-    received, refs = refs[:radix], refs[radix:]
-    field_ref, axes_ref, pins_ref, out_ref, low_ref, high_ref = refs
+            out_ref[chunk, start : start + rows, :] = value
+
+
+def send_kernel(line, level, field_ref, axes_ref, pins_ref, out_ref):
+    send_edges(line, level, True, field_ref, axes_ref, pins_ref, out_ref)
+
+
+def finish_kernel(
+    line, level, ghost_ref, field_ref, axes_ref, pins_ref, out_ref, low_ref, high_ref
+):
+    planes = line.planes
     rows, width = field_ref.shape[2:]
-    for s, k, lanes in chunk_tiles(level, width):
+    for chunk, k, lanes in chunk_tiles(level, width):
         ghosts = []
         for component in range(3):
             starts = [(2 * component + side) * level.rows + k * rows for side in range(2)]
-            ghosts.append([received[s][start : start + rows, :] for start in starts])
+            ghosts.append([ghost_ref[chunk, start : start + rows, :] for start in starts])
         solved = solve_components(line, field_ref, axes_ref, pins_ref, lanes, ghosts)
         for c in range(3):
             for i in range(planes):
@@ -426,10 +388,10 @@
 
 
 def rotate_and_send_kernel(
-    line, level, field_ref, below_ref, above_ref, axes_ref, pins_ref, out_ref, *outs
+    line, level, field_ref, below_ref, above_ref, axes_ref, pins_ref, out_ref, sent_ref
 ):
     rotate(field_ref, below_ref, above_ref, axes_ref, out_ref)
-    send_edges(line, level, False, out_ref, axes_ref, pins_ref, outs)
+    send_edges(line, level, False, out_ref, axes_ref, pins_ref, sent_ref)
 
 
 VMEM = pl.BlockSpec(memory_space=pltpu.VMEM)
@@ -448,13 +410,17 @@
     )(*operands)
 
 
-def exchange(level, blocks):
-    groups = lax.axis_size("gx")
-    received = [blocks[0]]
-    for s in range(1, level.radix):
-        pairs = [(i, i ^ (s << level.shift)) for i in range(groups)]
-        received.append(lax.ppermute(blocks[s], "gx", pairs))
-    return received
+def exchange(level, block):
+    count = lax.axis_size("gx")
+    step, span = 1 << level.shift, level.radix << level.shift
+    members = [
+        [start + low + step * r for r in range(level.radix)]
+        for start in range(0, count, span)
+        for low in range(step)
+    ]
+    return lax.all_to_all(
+        block, "gx", split_axis=0, concat_axis=0, axis_index_groups=members, tiled=True
+    )
 
 
 def to_neighbours(low, high):
@@ -475,52 +441,41 @@
     return found
 
 
-def settle_ghosts(levels, blocks, coupled, kept):
+def settle_ghosts(levels, block, coupled, kept):
     values = COUPLED if coupled else RHS
     orders = []
     for at, level in enumerate(levels):
-        received = exchange(level, blocks)
-        extra = [] if coupled else [kept[at]]
-        ordered = (level.radix, values * level.rows, LANES)
-        down = (RHS * level.rows, LANES)
+        ordered = exchange(level, block)
+        orders.append(ordered)
+        coupling = ordered if coupled else kept[at]
         if at + 1 < len(levels):
             above = levels[at + 1]
-            up = (values * above.rows, LANES)
-            found = call(
+            (block,) = call(
                 functools.partial(up_kernel, level, above, coupled),
-                [up] * above.radix + [ordered],
-                *received,
-                *extra,
-                scratch=[(above.radix, values * above.rows, LANES)],
+                [(above.radix, values * above.rows, LANES)],
+                ordered,
+                coupling,
             )
         else:
-            found = call(
-                functools.partial(top_kernel, level, coupled),
-                [down] * level.radix + [ordered],
-                *received,
-                *extra,
-                scratch=[(level.radix, RHS * level.rows, LANES)],
-            )
-        blocks, ordered = found[:-1], found[-1]
-        orders.append(ordered)
+            (block,) = call(
+                functools.partial(top_kernel, level),
+                [(level.radix, RHS * level.rows, LANES)],
+                ordered,
+                coupling,
+            )
     if coupled:
         kept = orders
     for at in range(len(levels) - 1, -1, -1):
-        received = exchange(levels[at], blocks)
+        received = exchange(levels[at], block)
         if at == 0:
             return received, kept
         level, above = levels[at - 1], levels[at]
-        down = (RHS * level.rows, LANES)
-        blocks = call(
+        (block,) = call(
             functools.partial(down_kernel, level, above),
-            [down] * level.radix,
-            *received,
+            [(level.radix, RHS * level.rows, LANES)],
+            received,
             orders[at - 1],
             kept[at - 1],
-            scratch=[
-                (above.radix, RHS * above.rows, LANES),
-                (level.radix, RHS * level.rows, LANES),
-            ],
         )
 
 
@@ -534,29 +489,29 @@
     edge = (3 * planes, width)
 
     field = magnetization
-    blocks = call(
+    (block,) = call(
         functools.partial(send_kernel, line, lowest),
-        [(COUPLED * lowest.rows, LANES)] * lowest.radix,
+        [(lowest.radix, COUPLED * lowest.rows, LANES)],
         field,
         easy_axes,
         pins,
     )
     kept = None
     for stepno in range(STEPS):
-        ghosts, kept = settle_ghosts(levels, blocks, stepno == 0, kept)
+        ghosts, kept = settle_ghosts(levels, block, stepno == 0, kept)
         solved, low, high = call(
             functools.partial(finish_kernel, line, lowest),
             [whole, edge, edge],
-            *ghosts,
+            ghosts,
             field,
             easy_axes,
             pins,
         )
         below, above = to_neighbours(low, high)
         if stepno < STEPS - 1:
-            field, *blocks = call(
+            field, block = call(
                 functools.partial(rotate_and_send_kernel, line, lowest),
-                [whole] + [(RHS * lowest.rows, LANES)] * lowest.radix,
+                [whole, (lowest.radix, RHS * lowest.rows, LANES)],
                 solved,
                 below,
                 above,

time: 82.4 us -> 88.7 us (1.076)
  blocking collectives: 0 us -> 62.3 us
  starting transfers between devices: 39.5 us -> 10.9 us
  waiting for transfers between devices: 27.9 us -> 2.44 us
  Pallas kernels: 10.8 us -> 8.73 us
    all_to_all x0 -> x8, blocking collectives: none -> 62.3 us  [exchange(): lax.all_to_all(block, 'gx', split_axis=0, concat_axis=0, axis_index_group...]
    ppermute x24 -> x0, starting transfers between devices: 25.9 us -> none  [exchange(): received.append(lax.ppermute(blocks[s], 'gx', pairs))]
    ppermute x24 -> x0, waiting for transfers between devices: 25.5 us -> none  [exchange(): received.append(lax.ppermute(blocks[s], 'gx', pairs))]
    ppermute x2, starting transfers between devices: 13.4 us -> 10.7 us  [to_neighbours(): lax.ppermute(high, 'gy', forward)]
    pallas_call x11, Pallas kernels: 10.8 us -> 8.73 us  [call(): pl.pallas_call(kernel, out_shape=tuple(shapes), in_specs=[VMEM] * len(ope...]
  transfers between devices with their start and end apart: 28 -> 4, of which waited for: 22 -> 4; matrix products, arithmetic and copies ran while one was open for 0% -> 0% of each run, Pallas kernels for 0% -> 0%
where the time goes in v3:
time: 88.7 us; the launch traced here: 88.2 us
  blocking collectives  62.3 us (70%)
  starting transfers between devices  10.9 us (12%)
  Pallas kernels  8.73 us (10%)
  local copies, waits for them, and re-layouts  3.75 us (4%)
  waiting for transfers between devices  2.44 us (3%)
    all_to_all x8, blocking collectives, exchange(): lax.all_to_all(block, 'gx', split_axis=0, concat_axis=0, axis_index_group...  62.3 us
    ppermute x2, starting transfers between devices, to_neighbours(): lax.ppermute(high, 'gy', forward)  10.7 us
    pallas_call x11, Pallas kernels, call(): pl.pallas_call(kernel, out_shape=tuple(shapes), in_specs=[VMEM] * len(ope...  8.73 us
    unnamed x12, local copies, waits for them, and re-layouts  3.75 us
  transfers between devices with their start and end apart: 4, of which 4 were waited for; matrix products, arithmetic and copies ran while one was open for 0% of the time, Pallas kernels for 0%

profile of v3, /device:TPU:1, one launch (start us, length us, event | category | flops | bytes accessed | tf_op | source)
XLA Modules:
  0.0 88.2 jit_solution(6197807988370730599)
XLA Ops:
  0.0 1.4 %copy-done = f32[3,16,16,512]{3,2,1,0:T(8,128)S(1)} copy-done((f32[3,16,16,512]{3,2,1,0:T(8,128)S(1)}, f32[3,16,16,512]{3,2,1,0:T(8,128)}, u32[]{:S(2)}) %copy-start) | copy-done | bytes 1572888
  1.4 1.4 %copy-done.2 = f32[3,16,16,512]{3,2,1,0:T(8,128)S(1)} copy-done((f32[3,16,16,512]{3,2,1,0:T(8,128)S(1)}, f32[3,16,16,512]{3,2,1,0:T(8,128)}, u32[]{:S(2)}) %copy-start.2) | copy-done | bytes 1572888
  2.8 0.9 %copy-done.4 = f32[2,3,16,512]{3,2,1,0:T(8,128)S(1)} copy-done((f32[2,3,16,512]{3,2,1,0:T(8,128)S(1)}, f32[2,3,16,512]{3,2,1,0:T(8,128)}, u32[]{:S(2)}) %copy-start.4) | copy-done | bytes 196632
  3.7 1.6 %shard_map.37 = f32[4,256,128]{2,1,0:T(8,128)S(1)} custom-call(f32[3,16,16,512]{3,2,1,0:T(8,128)S(1)} %copy-done.2, f32[3,16,16,512]{3,2,1,0:T(8,128)S(1)} %copy-done, f32[2,3,16,512]{3,2,1,0:T(8,128)S(1)} %copy-done.4), custom_call_target="tpu_custom_call" | custom-call | tf_op jit(solution)/shard_map/pallas_call | solution.py:403
  5.4 11.3 %all_to_all.40.rhs_ref.coupling_ref = f32[4,256,128]{2,1,0:T(8,128)S(1)} all-to-all(f32[4,256,128]{2,1,0:T(8,128)S(1)} %shard_map.37), channel_id=1, replica_groups={{0,2,4,6},{8,10,12,14},{16,18,20,22},{24,26,28,30},{1,3,5,7},{9,11,13,1..., dimensions={0} | all-to-all | bytes 1048576 | tf_op jit(solution)/shard_map/all_to_all | solution.py:421
  16.7 0.2 shard_map.38
  16.9 9.3 %all_to_all.41.rhs_ref.coupling_ref = f32[4,64,128]{2,1,0:T(8,128)S(1)} all-to-all(f32[4,64,128]{2,1,0:T(8,128)S(1)} %shard_map.38), channel_id=1, replica_groups={{0,8,16,24},{2,10,18,26},{4,12,20,28},{6,14,22,30},{1,9,17,25},{3,11,19..., dimensions={0} | all-to-all | bytes 262144 | tf_op jit(solution)/shard_map/all_to_all | solution.py:421
  26.3 7.0 %all_to_all.42.outer_ref = f32[4,24,128]{2,1,0:T(8,128)S(1)} all-to-all(f32[4,24,128]{2,1,0:T(8,128)S(1)} %shard_map.39), channel_id=1, replica_groups={{0,8,16,24},{2,10,18,26},{4,12,20,28},{6,14,22,30},{1,9,17,25},{3,11,19..., dimensions={0} | all-to-all | bytes 98304 | tf_op jit(solution)/shard_map/all_to_all | solution.py:421
  33.2 0.1 shard_map.40
  33.3 6.8 %all_to_all.43.ghost_ref = f32[4,96,128]{2,1,0:T(8,128)S(1)} all-to-all(f32[4,96,128]{2,1,0:T(8,128)S(1)} %shard_map.40), channel_id=1, replica_groups={{0,2,4,6},{8,10,12,14},{16,18,20,22},{24,26,28,30},{1,3,5,7},{9,11,13,1..., dimensions={0} | all-to-all | bytes 393216 | tf_op jit(solution)/shard_map/all_to_all | solution.py:421
  40.1 0.9 %shard_map.41 = (f32[3,16,16,512]{3,2,1,0:T(8,128)S(1)}, f32[48,512]{1,0:T(8,128)S(1)}, f32[48,512]{1,0:T(8,128)S(1)}) custom-call(f32[4,96,128]{2,1,0:T(8,128)S(1)} %all_to_all.43.ghost_ref, f32[3,16,16,512]{3,2,1,0:T(8,128)S(1)} %copy-done.3, f32[3,16,16,512]{3,2,1,0:T(8,128)S(1)} %copy-done, f32[2,3,16,512]{3,2,1,0:T(8,128)S(1)} %copy-done.4), custom_call_target="tpu_custom_call" | custom-call | tf_op jit(solution)/shard_map/pallas_call | solution.py:403
  41.0 6.1 %collective-permute-start = (f32[48,512]{1,0:T(8,128)S(1)}, f32[48,512]{1,0:T(8,128)S(1)}, u32[]{:S(2)}, u32[]{:S(2)}) collective-permute-start(f32[48,512]{1,0:T(8,128)S(1)} %get-tuple-element.14), channel_id=1, source_target_pairs={{0,1},{1,0},{2,3},{3,2},{4,5},{5,4},{6,7},{7,6},{8,9},{9,8},{10,11... | collective-permute-start | bytes 294920 | tf_op jit(solution)/shard_map/ppermute | solution.py:430
  47.2 0.9 collective-permute-done.below_ref
  48.1 0.4 collective-permute-done.1.above_ref
  48.4 2.1 %shard_map.42 = (f32[3,16,16,512]{3,2,1,0:T(8,128)S(1)}, f32[4,96,128]{2,1,0:T(8,128)S(1)}) custom-call(f32[3,16,16,512]{3,2,1,0:T(8,128)S(1)} %get-tuple-element.13.field_ref, f32[48,512]{1,0:T(8,128)S(1)} %collective-permute-done.below_ref, f32[48,512]{1,0:T(8,128)S(1)} %collective-permute-done.1.above_ref, f32[3,16,16,512]{3,2,1,0:T(8,128)S(1)} %copy-done.1, ...), custom_call_target="tpu_custom_call" | custom-call | tf_op jit(solution)/shard_map/pallas_call | solution.py:403
  50.5 7.4 %all_to_all.44.rhs_ref = f32[4,96,128]{2,1,0:T(8,128)S(1)} all-to-all(f32[4,96,128]{2,1,0:T(8,128)S(1)} %get-tuple-element.16), channel_id=1, replica_groups={{0,2,4,6},{8,10,12,14},{16,18,20,22},{24,26,28,30},{1,3,5,7},{9,11,13,1..., dimensions={0} | all-to-all | bytes 393216 | tf_op jit(solution)/shard_map/all_to_all | solution.py:421
  58.0 6.9 %all_to_all.45.rhs_ref = f32[4,24,128]{2,1,0:T(8,128)S(1)} all-to-all(f32[4,24,128]{2,1,0:T(8,128)S(1)} %shard_map.43), channel_id=1, replica_groups={{0,8,16,24},{2,10,18,26},{4,12,20,28},{6,14,22,30},{1,9,17,25},{3,11,19..., dimensions={0} | all-to-all | bytes 98304 | tf_op jit(solution)/shard_map/all_to_all | solution.py:421
  64.9 6.9 %all_to_all.46.outer_ref = f32[4,24,128]{2,1,0:T(8,128)S(1)} all-to-all(f32[4,24,128]{2,1,0:T(8,128)S(1)} %shard_map.44), channel_id=1, replica_groups={{0,8,16,24},{2,10,18,26},{4,12,20,28},{6,14,22,30},{1,9,17,25},{3,11,19..., dimensions={0} | all-to-all | bytes 98304 | tf_op jit(solution)/shard_map/all_to_all | solution.py:421
  72.0 6.8 %all_to_all.47.ghost_ref = f32[4,96,128]{2,1,0:T(8,128)S(1)} all-to-all(f32[4,96,128]{2,1,0:T(8,128)S(1)} %shard_map.45), channel_id=1, replica_groups={{0,2,4,6},{8,10,12,14},{16,18,20,22},{24,26,28,30},{1,3,5,7},{9,11,13,1..., dimensions={0} | all-to-all | bytes 393216 | tf_op jit(solution)/shard_map/all_to_all | solution.py:421
  78.7 0.9 %shard_map.46 = (f32[3,16,16,512]{3,2,1,0:T(8,128)S(1)}, f32[48,512]{1,0:T(8,128)S(1)}, f32[48,512]{1,0:T(8,128)S(1)}) custom-call(f32[4,96,128]{2,1,0:T(8,128)S(1)} %all_to_all.47.ghost_ref, f32[3,16,16,512]{3,2,1,0:T(8,128)S(1)} %get-tuple-element.17.field_ref, f32[3,16,16,512]{3,2,1,0:T(8,128)S(1)} %copy-done.1, f32[2,3,16,512]{3,2,1,0:T(8,128)S(1)} %copy-done.5), custom_call_target="tpu_custom_call" | custom-call | tf_op jit(solution)/shard_map/pallas_call | solution.py:403
  79.7 4.7 %collective-permute-start.2 = (f32[48,512]{1,0:T(8,128)S(1)}, f32[48,512]{1,0:T(8,128)S(1)}, u32[]{:S(2)}, u32[]{:S(2)}) collective-permute-start(f32[48,512]{1,0:T(8,128)S(1)} %get-tuple-element.19), channel_id=1, source_target_pairs={{0,1},{1,0},{2,3},{3,2},{4,5},{5,4},{6,7},{7,6},{8,9},{9,8},{10,11... | collective-permute-start | bytes 294920 | tf_op jit(solution)/shard_map/ppermute | solution.py:430
  84.4 0.9 collective-permute-done.2.below_ref
  85.3 0.4 collective-permute-done.3.above_ref
  85.6 2.5 %shard_map.47 = f32[3,16,16,512]{3,2,1,0:T(8,128)} custom-call(f32[3,16,16,512]{3,2,1,0:T(8,128)S(1)} %get-tuple-element.18.field_ref, f32[48,512]{1,0:T(8,128)S(1)} %collective-permute-done.2.below_ref, f32[48,512]{1,0:T(8,128)S(1)} %collective-permute-done.3.above_ref, f32[3,16,16,512]{3,2,1,0:T(8,128)S(1)} %copy-done.1), custom_call_target="tpu_custom_call" | custom-call | tf_op jit(solution)/shard_map/pallas_call | solution.py:403
  (15 shorter events, 0.4 us)
Async XLA Ops:
  0.0 1.4 %copy-start = (f32[3,16,16,512]{3,2,1,0:T(8,128)S(1)}, f32[3,16,16,512]{3,2,1,0:T(8,128)}, u32[]{:S(2)}) copy-start(f32[3,16,16,512]{3,2,1,0:T(8,128)} %axes_ref.9) | copy-start | bytes 4718596
  1.4 1.4 %copy-start.2 = (f32[3,16,16,512]{3,2,1,0:T(8,128)S(1)}, f32[3,16,16,512]{3,2,1,0:T(8,128)}, u32[]{:S(2)}) copy-start(f32[3,16,16,512]{3,2,1,0:T(8,128)} %field_ref.3) | copy-start | bytes 4718596
  2.8 0.9 %copy-start.4 = (f32[2,3,16,512]{3,2,1,0:T(8,128)S(1)}, f32[2,3,16,512]{3,2,1,0:T(8,128)}, u32[]{:S(2)}) copy-start(f32[2,3,16,512]{3,2,1,0:T(8,128)} %pins_ref.7) | copy-start | bytes 589828
  16.7 23.4 %copy-start.3 = (f32[3,16,16,512]{3,2,1,0:T(8,128)S(1)}, f32[3,16,16,512]{3,2,1,0:T(8,128)}, u32[]{:S(2)}) copy-start(f32[3,16,16,512]{3,2,1,0:T(8,128)} %field_ref.3) | copy-start | bytes 4718596
  40.1 8.3 %copy-start.1 = (f32[3,16,16,512]{3,2,1,0:T(8,128)S(1)}, f32[3,16,16,512]{3,2,1,0:T(8,128)}, u32[]{:S(2)}) copy-start(f32[3,16,16,512]{3,2,1,0:T(8,128)} %axes_ref.9) | copy-start | bytes 4718596
  40.1 8.3 %copy-start.5 = (f32[2,3,16,512]{3,2,1,0:T(8,128)S(1)}, f32[2,3,16,512]{3,2,1,0:T(8,128)}, u32[]{:S(2)}) copy-start(f32[2,3,16,512]{3,2,1,0:T(8,128)} %pins_ref.7) | copy-start | bytes 589828
  41.0 7.0 %collective-permute-start = (f32[48,512]{1,0:T(8,128)S(1)}, f32[48,512]{1,0:T(8,128)S(1)}, u32[]{:S(2)}, u32[]{:S(2)}) collective-permute-start(f32[48,512]{1,0:T(8,128)S(1)} %get-tuple-element.14), channel_id=1, source_target_pairs={{0,1},{1,0},{2,3},{3,2},{4,5},{5,4},{6,7},{7,6},{8,9},{9,8},{10,11... | collective-permute-start | bytes 294920 | tf_op jit(solution)/shard_map/ppermute | solution.py:430
  47.1 1.3 %collective-permute-start.1 = (f32[48,512]{1,0:T(8,128)S(1)}, f32[48,512]{1,0:T(8,128)S(1)}, u32[]{:S(2)}, u32[]{:S(2)}) collective-permute-start(f32[48,512]{1,0:T(8,128)S(1)} %get-tuple-element.15), channel_id=1, source_target_pairs={{1,0},{0,1},{3,2},{2,3},{5,4},{4,5},{7,6},{6,7},{9,8},{8,9},{11,10... | collective-permute-start | bytes 294920 | tf_op jit(solution)/shard_map/ppermute | solution.py:430
  79.7 5.6 %collective-permute-start.2 = (f32[48,512]{1,0:T(8,128)S(1)}, f32[48,512]{1,0:T(8,128)S(1)}, u32[]{:S(2)}, u32[]{:S(2)}) collective-permute-start(f32[48,512]{1,0:T(8,128)S(1)} %get-tuple-element.19), channel_id=1, source_target_pairs={{0,1},{1,0},{2,3},{3,2},{4,5},{5,4},{6,7},{7,6},{8,9},{9,8},{10,11... | collective-permute-start | bytes 294920 | tf_op jit(solution)/shard_map/ppermute | solution.py:430
  84.3 1.3 %collective-permute-start.3 = (f32[48,512]{1,0:T(8,128)S(1)}, f32[48,512]{1,0:T(8,128)S(1)}, u32[]{:S(2)}, u32[]{:S(2)}) collective-permute-start(f32[48,512]{1,0:T(8,128)S(1)} %get-tuple-element.20), channel_id=1, source_target_pairs={{1,0},{0,1},{3,2},{2,3},{5,4},{4,5},{7,6},{6,7},{9,8},{8,9},{11,10... | collective-permute-start | bytes 294920 | tf_op jit(solution)/shard_map/ppermute | solution.py:430

commit v4 on v1

--- a/solution.py
+++ b/solution.py
@@ -49,20 +49,75 @@
         return solved
 
 
-def ghost_table(line, groups):
-    near, far = line.from_low[0], line.from_low[-1]
-    link = np.zeros((2 * groups, 2 * groups))
-    pick = np.zeros((2 * groups, 2 * groups))
-    for d in range(groups):
-        if d > 0:
-            link[d, groups + d - 1] = near
-            link[groups + d, groups + d - 1] = far
-            pick[d, groups + d - 1] = 1.0
-        if d < groups - 1:
-            link[d, d + 1] = far
-            link[groups + d, d + 1] = near
-            pick[groups + d, d + 1] = 1.0
-    return pick @ np.linalg.inv(np.eye(2 * groups) - link)
+class Level:
+    def __init__(self, length, radix):
+        self.radix = radix
+        line = Line(length)
+        near, far = line.from_low[0], line.from_low[-1]
+        count = 2 * radix
+        inside = np.kron(np.eye(radix), np.array([[near, far], [far, near]]))
+        pick = np.zeros((count, count))
+        for r in range(radix):
+            if r > 0:
+                pick[2 * r, 2 * r - 1] = 1.0
+            if r < radix - 1:
+                pick[2 * r + 1, 2 * r + 2] = 1.0
+        outer = np.zeros((count, 2))
+        outer[0, 0] = outer[count - 1, 1] = 1.0
+        settle = np.linalg.inv(np.eye(count) - pick @ inside)
+        self.ghosts = settle @ pick
+        self.passed = settle @ outer
+        ends = (np.eye(count) + inside @ self.ghosts)[[0, count - 1]]
+        self.ends = ends
+
+
+def radices_of(groups):
+    found = []
+    while groups > 1:
+        radix = 4 if groups % 4 == 0 else 2
+        assert groups % radix == 0
+        found.append(radix)
+        groups //= radix
+    return found
+
+
+def combine(weights, terms):
+    total = None
+    for weight, term in zip(weights, terms):
+        if weight == 0.0 or term is None:
+            continue
+        part = term * float(weight)
+        total = part if total is None else total + part
+    return total
+
+
+def make_levels(planes, groups):
+    found = []
+    for radix in radices_of(groups):
+        found.append(Level(planes, radix))
+        planes *= radix
+    return found
+
+
+def settle(levels, ends):
+    level, count = levels[0], 2 * levels[0].radix
+    if len(levels) == 1:
+        return [combine(weights, ends) for weights in level.ghosts]
+    joined = []
+    for start in range(0, len(ends), count):
+        part = ends[start : start + count]
+        joined += [combine(weights, part) for weights in level.ends]
+    outer = settle(levels[1:], joined)
+    found = []
+    for at, start in enumerate(range(0, len(ends), count)):
+        part = list(ends[start : start + count]) + [outer[2 * at], outer[2 * at + 1]]
+        for inside, passed in zip(level.ghosts, level.passed):
+            found.append(combine(list(inside) + list(passed), part))
+    return found
+
+
+def plus(total, weight, term):
+    return total if term is None else total + weight * term
 
 
 def row_window(value, values, units, tile, tiles, rows):
@@ -129,58 +184,86 @@
     return found
 
 
-def send_edges(line, units, coupled, field_ref, axes_ref, pins_ref, out_ref):
+def send_tile(line, units, coupled, field_ref, axes_ref, pins_ref, out_ref, tile):
     rows, width = field_ref.shape[2], field_ref.shape[3]
     tiles = width // LANES
     values = COUPLED if coupled else RHS
+    lanes = slice(tile * LANES, (tile + 1) * LANES)
+    solved = solve_components(line, field_ref, axes_ref, pins_ref, lanes, None)
+    sent = []
+    for component in range(3):
+        sent += [solved[component][0], solved[component][-1]]
+    if coupled:
+        sent += couplings(line, axes_ref, lanes)
+    for value in range(values):
+        out_ref[row_window(value, values, units, tile, tiles, rows), :] = sent[value]
+
+
+def first_kernel(
+    line, units, field_hbm, axes_hbm, pins_hbm, out_ref, field_ref, axes_ref, pins_ref, sems, pin_sem
+):
+    tiles = field_ref.shape[3] // LANES
+    pin_copy = pltpu.make_async_copy(pins_hbm, pins_ref, pin_sem)
+    copies = []
     for tile in range(tiles):
-        lanes = slice(tile * LANES, (tile + 1) * LANES)
-        solved = solve_components(line, field_ref, axes_ref, pins_ref, lanes, None)
-        sent = []
-        for component in range(3):
-            sent += [solved[component][0], solved[component][-1]]
-        if coupled:
-            sent += couplings(line, axes_ref, lanes)
-        for value in range(values):
-            out_ref[row_window(value, values, units, tile, tiles, rows), :] = sent[value]
-
-
-def reduced_kernel(groups, units, rhs_values, rhs_ref, coupling_ref, table_ref, out_ref):
-    def read(ref, values, value):
-        parts = [
-            ref[pl.ds(value * units + u, groups, stride=values * units), :] for u in range(units)
-        ]
-        return jnp.concatenate(parts, axis=1) if units > 1 else parts[0]
-
-    table = table_ref[...]
-
-    def ghosts(first, last):
-        found = jnp.dot(
-            table,
-            jnp.concatenate([first, last], axis=0),
-            precision=lax.Precision.HIGHEST,
-            preferred_element_type=jnp.float32,
+        lanes = pl.ds(tile * LANES, LANES)
+        at = (slice(None), slice(None), slice(None), lanes)
+        copies.append(
+            (
+                pltpu.make_async_copy(axes_hbm.at[at], axes_ref.at[at], sems.at[0, tile]),
+                pltpu.make_async_copy(field_hbm.at[at], field_ref.at[at], sems.at[1, tile]),
+            )
         )
-        return found[:groups], found[groups:]
-
-    rhs = [read(rhs_ref, rhs_values, v) for v in range(RHS)]
-    c = [read(coupling_ref, COUPLED, v) for v in range(RHS, COUPLED)]
-    low1, high1 = ghosts(rhs[0], rhs[1])
-    low2, high2 = ghosts(
-        rhs[2] + c[0] * low1 + c[1] * high1, rhs[3] + c[1] * low1 + c[2] * high1
-    )
-    low3, high3 = ghosts(
-        rhs[4] + c[3] * low2 + c[4] * high2 + c[6] * low1 + c[8] * high1,
-        rhs[5] + c[4] * low2 + c[5] * high2 + c[7] * low1 + c[9] * high1,
-    )
-    for value, found in enumerate((low1, high1, low2, high2, low3, high3)):
-        for u in range(units):
-            out_ref[pl.ds(value * units + u, groups, stride=RHS * units), :] = found[
-                :, u * LANES : (u + 1) * LANES
-            ]
-
-
-def finish_kernel(line, units, field_ref, axes_ref, pins_ref, ghost_ref, out_ref, low_ref, high_ref):
+        for copy in copies[-1]:
+            copy.start()
+        if tile == 0:
+            pin_copy.start()
+    for tile in range(tiles):
+        for copy in copies[tile]:
+            copy.wait()
+        if tile == 0:
+            pin_copy.wait()
+        send_tile(line, units, True, field_ref, axes_ref, pins_ref, out_ref, tile)
+
+
+def reduced_kernel(levels, groups, units, rhs_values, rhs_ref, coupling_ref, out_ref):
+    def read(ref, values, d, value):
+        start = (d * values + value) * units
+        return ref[start : start + units, :]
+
+    rhs = [
+        [read(rhs_ref, rhs_values, k // 2, 2 * c + k % 2) for k in range(2 * groups)]
+        for c in range(3)
+    ]
+
+    def coupling(d, value):
+        return read(coupling_ref, COUPLED, d, RHS + value)
+
+    first = settle(levels, rhs[0])
+    for d in range(groups):
+        low, high = first[2 * d], first[2 * d + 1]
+        mixed = coupling(d, 1)
+        rhs[1][2 * d] = plus(plus(rhs[1][2 * d], coupling(d, 0), low), mixed, high)
+        rhs[1][2 * d + 1] = plus(plus(rhs[1][2 * d + 1], mixed, low), coupling(d, 2), high)
+    second = settle(levels, rhs[1])
+    for d in range(groups):
+        low1, high1 = first[2 * d], first[2 * d + 1]
+        low2, high2 = second[2 * d], second[2 * d + 1]
+        mixed = coupling(d, 4)
+        total = plus(plus(rhs[2][2 * d], coupling(d, 3), low2), mixed, high2)
+        rhs[2][2 * d] = plus(plus(total, coupling(d, 6), low1), coupling(d, 8), high1)
+        total = plus(plus(rhs[2][2 * d + 1], mixed, low2), coupling(d, 5), high2)
+        rhs[2][2 * d + 1] = plus(plus(total, coupling(d, 7), low1), coupling(d, 9), high1)
+    third = settle(levels, rhs[2])
+    for c, ghosts in enumerate((first, second, third)):
+        for k, ghost in enumerate(ghosts):
+            start = (k // 2 * RHS + 2 * c + k % 2) * units
+            if ghost is None:
+                ghost = jnp.zeros((units, LANES), jnp.float32)
+            out_ref[start : start + units, :] = ghost
+
+
+def finish_kernel(line, units, field_ref, axes_ref, pins_ref, ghost_ref, out_ref, edge_ref):
     planes = line.planes
     rows, width = field_ref.shape[2], field_ref.shape[3]
     tiles = width // LANES
@@ -197,11 +280,12 @@
         for c in range(3):
             for i in range(planes):
                 out_ref[c, i, :, lanes] = solved[c][i]
-                low_ref[c * planes + i : c * planes + i + 1, lanes] = solved[c][i][:1]
-                high_ref[c * planes + i : c * planes + i + 1, lanes] = solved[c][i][rows - 1 :]
-
-
-def rotate(field_ref, below_ref, above_ref, axes_ref, out_ref):
+                at = c * planes + i
+                edge_ref[0, at : at + 1, lanes] = solved[c][i][:1]
+                edge_ref[1, at : at + 1, lanes] = solved[c][i][rows - 1 :]
+
+
+def rotate(field_ref, beyond_ref, axes_ref, out_ref, finished=None):
     planes, rows, width = field_ref.shape[1:]
     row = lax.broadcasted_iota(jnp.int32, (rows, width), 0)
     for i in range(planes):
@@ -212,10 +296,10 @@
         for c in range(3):
             at = c * planes + i
             below = jnp.where(
-                row == 0, below_ref[at : at + 1, :], pltpu.roll(field[c], 1, 0)
+                row == 0, beyond_ref[1, at : at + 1, :], pltpu.roll(field[c], 1, 0)
             )
             above = jnp.where(
-                row == rows - 1, above_ref[at : at + 1, :], pltpu.roll(field[c], rows - 1, 0)
+                row == rows - 1, beyond_ref[0, at : at + 1, :], pltpu.roll(field[c], rows - 1, 0)
             )
             beside = pltpu.roll(field[c], 1, 1) + pltpu.roll(field[c], width - 1, 1)
             effective.append(
@@ -231,28 +315,42 @@
         scale = jnp.minimum(lax.rsqrt(square), 1.0 / norm_floor)
         for c in range(3):
             out_ref[c, i] = rotated[c] * scale
+        if finished is not None:
+            finished(i)
 
 
 def rotate_and_send_kernel(
-    line, units, field_ref, below_ref, above_ref, axes_ref, pins_ref, out_ref, sent_ref
+    line, units, field_ref, beyond_ref, axes_ref, pins_ref, out_ref, sent_ref
 ):
-    rotate(field_ref, below_ref, above_ref, axes_ref, out_ref)
-    send_edges(line, units, False, out_ref, axes_ref, pins_ref, sent_ref)
+    rotate(field_ref, beyond_ref, axes_ref, out_ref)
+    for tile in range(field_ref.shape[3] // LANES):
+        send_tile(line, units, False, out_ref, axes_ref, pins_ref, sent_ref, tile)
+
+
+def last_kernel(field_ref, beyond_ref, axes_ref, out_hbm, out_ref, sems):
+    def copy(i):
+        return pltpu.make_async_copy(out_ref.at[:, i], out_hbm.at[:, i], sems.at[i])
+
+    rotate(field_ref, beyond_ref, axes_ref, out_ref, lambda i: copy(i).start())
+    for i in range(field_ref.shape[1]):
+        copy(i).wait()
 
 
 VMEM = pl.BlockSpec(memory_space=pltpu.VMEM)
-LIMIT = pltpu.CompilerParams(vmem_limit_bytes=32 * 1024 * 1024)
-
-
-def call(kernel, shapes, *operands):
+HBM = pl.BlockSpec(memory_space=pltpu.HBM)
+SMALL = 32 * 1024 * 1024
+LARGE = 63 * 1024 * 1024
+
+
+def call(kernel, shapes, *operands, read=VMEM, written=VMEM, scratch=(), limit=SMALL):
     shapes = [jax.ShapeDtypeStruct(shape, jnp.float32) for shape in shapes]
-    single = len(shapes) == 1
     return pl.pallas_call(
         kernel,
-        out_shape=shapes[0] if single else tuple(shapes),
-        in_specs=[VMEM] * len(operands),
-        out_specs=VMEM if single else (VMEM,) * len(shapes),
-        compiler_params=LIMIT,
+        out_shape=tuple(shapes),
+        in_specs=[read] * len(operands),
+        out_specs=(written,) * len(shapes),
+        scratch_shapes=scratch,
+        compiler_params=pltpu.CompilerParams(vmem_limit_bytes=limit),
     )(*operands)
 
 
@@ -263,66 +361,84 @@
     )
 
 
-def to_neighbours(low, high):
+def from_neighbours(edges):
     count = lax.axis_size("gy")
     forward = [(i, (i + 1) % count) for i in range(count)]
+    if count == 2:
+        return lax.ppermute(edges, "gy", forward)
     backward = [(target, source) for source, target in forward]
-    return lax.ppermute(high, "gy", forward), lax.ppermute(low, "gy", backward)
+    return jnp.stack(
+        [lax.ppermute(edges[0], "gy", backward), lax.ppermute(edges[1], "gy", forward)]
+    )
 
 
 def per_device(magnetization, easy_axes, pins):
     _, planes, rows, width = magnetization.shape
     groups = lax.axis_size("gx")
-    units = rows * (width // LANES) // groups
+    tiles = width // LANES
+    units = rows * tiles // groups
     line = Line(planes)
-    table = jnp.asarray(ghost_table(line, groups), jnp.float32)
+    levels = make_levels(planes, groups)
     whole = magnetization.shape
-    edge = (3 * planes, width)
     sent_shape = (groups * RHS * units, LANES)
-    coupled_shape = (groups * COUPLED * units, LANES)
 
     field = magnetization
-    sent = call(
-        functools.partial(send_edges, line, units, True),
-        [coupled_shape],
+    (sent,) = call(
+        functools.partial(first_kernel, line, units),
+        [(groups * COUPLED * units, LANES)],
         field,
         easy_axes,
         pins,
+        read=HBM,
+        scratch=[
+            pltpu.VMEM(whole, jnp.float32),
+            pltpu.VMEM(whole, jnp.float32),
+            pltpu.VMEM(pins.shape, jnp.float32),
+            pltpu.SemaphoreType.DMA((2, tiles)),
+            pltpu.SemaphoreType.DMA,
+        ],
+        limit=LARGE,
     )
     coupling = None
     for stepno in range(STEPS):
         gathered = exchange(sent, groups)
         if stepno == 0:
             coupling = gathered
-        ghosts = call(
-            functools.partial(reduced_kernel, groups, units, RHS if stepno else COUPLED),
+        (ghosts,) = call(
+            functools.partial(reduced_kernel, levels, groups, units, RHS if stepno else COUPLED),
             [sent_shape],
             gathered,
             coupling,
-            table,
         )
         ghosts = exchange(ghosts, groups)
-        solved, low, high = call(
+        solved, edges = call(
             functools.partial(finish_kernel, line, units),
-            [whole, edge, edge],
+            [whole, (2, 3 * planes, width)],
             field,
             easy_axes,
             pins,
             ghosts,
         )
-        below, above = to_neighbours(low, high)
+        beyond = from_neighbours(edges)
         if stepno < STEPS - 1:
             field, sent = call(
                 functools.partial(rotate_and_send_kernel, line, units),
                 [whole, sent_shape],
                 solved,
-                below,
-                above,
+                beyond,
                 easy_axes,
                 pins,
             )
         else:
-            field = call(rotate, [whole], solved, below, above, easy_axes)
+            (field,) = call(
+                last_kernel,
+                [whole],
+                solved,
+                beyond,
+                easy_axes,
+                written=HBM,
+                scratch=[pltpu.VMEM(whole, jnp.float32), pltpu.SemaphoreType.DMA((planes,))],
+            )
     return field
 
 

time: 75.7 us -> 75.1 us (level)
  local copies, waits for them, and re-layouts: 3.76 us -> 1.42 us
  Pallas kernels: 9.82 us -> 11.6 us
    unnamed x14 -> x6, local copies, waits for them, and re-layouts: 3.76 us -> 1.42 us
    pallas_call x7, Pallas kernels: 9.82 us -> 11.6 us  [call(): pl.pallas_call(kernel, out_shape=tuple(shapes), in_specs=[read] * len(ope...]
    ppermute x4 -> x2, waiting for transfers between devices: 2.44 us -> 2.14 us  [from_neighbours(): return lax.ppermute(edges, 'gy', forward)]
    ppermute x4 -> x2, starting transfers between devices: 5.55 us -> 5.39 us  [from_neighbours(): return lax.ppermute(edges, 'gy', forward)]
  transfers between devices with their start and end apart: 4 -> 2, of which waited for: 4 -> 2; matrix products, arithmetic and copies ran while one was open for 0% -> 0% of each run, Pallas kernels for 0% -> 0%
where the time goes in v4:
time: 75.1 us; the launch traced here: 74.4 us
  blocking collectives  53.8 us (72%)
  Pallas kernels  11.6 us (15%)
  starting transfers between devices  5.39 us (7%)
  waiting for transfers between devices  2.14 us (3%)
  local copies, waits for them, and re-layouts  1.42 us (2%)
    all_to_all x4, blocking collectives, exchange(): lax.all_to_all(parts, 'gx', split_axis=0, concat_axis=0, tiled=True)  53.8 us
    pallas_call x7, Pallas kernels, call(): pl.pallas_call(kernel, out_shape=tuple(shapes), in_specs=[read] * len(ope...  11.6 us
    ppermute x2, starting transfers between devices, from_neighbours(): return lax.ppermute(edges, 'gy', forward)  5.39 us
    ppermute x2, waiting for transfers between devices, from_neighbours(): return lax.ppermute(edges, 'gy', forward)  2.14 us
  transfers between devices with their start and end apart: 2, of which 2 were waited for; matrix products, arithmetic and copies ran while one was open for 0% of the time, Pallas kernels for 0%

profile of v4, /device:TPU:1, one launch (start us, length us, event | category | flops | bytes accessed | tf_op | source)
XLA Modules:
  0.0 74.4 jit_solution(12360907453771944661)
XLA Ops:
  0.0 4.9 %shard_map.37 = f32[1024,128]{1,0:T(8,128)} custom-call(f32[3,16,16,512]{3,2,1,0:T(8,128)} %field_ref.1, f32[3,16,16,512]{3,2,1,0:T(8,128)} %axes_ref.7, f32[2,3,16,512]{3,2,1,0:T(8,128)} %pins_ref.5), custom_call_target="tpu_custom_call" | custom-call | tf_op jit(solution)/shard_map/pallas_call | solution.py:347
  4.9 0.0 copy-start
  4.9 0.0 copy-start.2
  4.9 19.8 %all_to_all.20 = f32[16,64,128]{2,1,0:T(8,128)S(1)} all-to-all(f32[16,64,128]{2,1,0:T(8,128)} %bitcast.17), channel_id=1, replica_groups=mesh['gx'=16,'gy'=2] {'gx'}, dimensions={0} | all-to-all | bytes 1048576 | tf_op jit(solution)/shard_map/all_to_all | solution.py:359
  24.7 0.2 shard_map.38
  25.0 12.8 %all_to_all.21 = f32[16,24,128]{2,1,0:T(8,128)S(1)} all-to-all(f32[16,24,128]{2,1,0:T(8,128)S(1)} %bitcast.15), channel_id=1, replica_groups=mesh['gx'=16,'gy'=2] {'gx'}, dimensions={0} | all-to-all | bytes 393216 | tf_op jit(solution)/shard_map/all_to_all | solution.py:359
  37.8 0.0 copy-done
  37.8 0.0 copy-done.2
  37.8 0.0 copy-start.1
  37.8 1.4 %copy-done.1 = f32[3,16,16,512]{3,2,1,0:T(8,128)S(1)} copy-done((f32[3,16,16,512]{3,2,1,0:T(8,128)S(1)}, f32[3,16,16,512]{3,2,1,0:T(8,128)}, u32[]{:S(2)}) %copy-start.1) | copy-done | bytes 1572888
  39.2 1.0 %shard_map.39 = (f32[3,16,16,512]{3,2,1,0:T(8,128)S(1)}, f32[2,48,512]{2,1,0:T(8,128)S(1)}) custom-call(f32[3,16,16,512]{3,2,1,0:T(8,128)S(1)} %copy-done.1, f32[3,16,16,512]{3,2,1,0:T(8,128)S(1)} %copy-done, f32[2,3,16,512]{3,2,1,0:T(8,128)S(1)} %copy-done.2, f32[384,128]{1,0:T(8,128)S(1)} %bitcast.12), custom_call_target="tpu_custom_call" | custom-call | tf_op jit(solution)/shard_map/pallas_call | solution.py:347
  40.2 2.8 %collective-permute-start = (f32[2,48,512]{2,1,0:T(8,128)S(1)}, f32[2,48,512]{2,1,0:T(8,128)S(1)}, u32[]{:S(2)}, u32[]{:S(2)}) collective-permute-start(f32[2,48,512]{2,1,0:T(8,128)S(1)} %get-tuple-element.12), channel_id=1, source_target_pairs={{0,1},{1,0},{2,3},{3,2},{4,5},{5,4},{6,7},{7,6},{8,9},{9,8},{10,11... | collective-permute-start | bytes 589832 | tf_op jit(solution)/shard_map/ppermute | solution.py:368
  43.0 1.1 %collective-permute-done.beyond_ref = f32[2,48,512]{2,1,0:T(8,128)S(1)} collective-permute-done((f32[2,48,512]{2,1,0:T(8,128)S(1)}, f32[2,48,512]{2,1,0:T(8,128)S(1)}, u32[]{:S(2)}, u32[]{:S(2)}) %collective-permute-start) | collective-permute-done | bytes 196640 | tf_op jit(solution)/shard_map/ppermute | solution.py:368
  44.1 2.1 %shard_map.40 = (f32[3,16,16,512]{3,2,1,0:T(8,128)S(1)}, f32[384,128]{1,0:T(8,128)S(1)}) custom-call(f32[3,16,16,512]{3,2,1,0:T(8,128)S(1)} %get-tuple-element.11.field_ref, f32[2,48,512]{2,1,0:T(8,128)S(1)} %collective-permute-done.beyond_ref, f32[3,16,16,512]{3,2,1,0:T(8,128)S(1)} %copy-done, f32[2,3,16,512]{3,2,1,0:T(8,128)S(1)} %copy-done.2), custom_call_target="tpu_custom_call" | custom-call | tf_op jit(solution)/shard_map/pallas_call | solution.py:347
  46.2 10.0 %all_to_all.22 = f32[16,24,128]{2,1,0:T(8,128)S(1)} all-to-all(f32[16,24,128]{2,1,0:T(8,128)S(1)} %bitcast.16), channel_id=1, replica_groups=mesh['gx'=16,'gy'=2] {'gx'}, dimensions={0} | all-to-all | bytes 393216 | tf_op jit(solution)/shard_map/all_to_all | solution.py:359
  56.2 0.2 shard_map.41
  56.5 11.1 %all_to_all.23 = f32[16,24,128]{2,1,0:T(8,128)S(1)} all-to-all(f32[16,24,128]{2,1,0:T(8,128)S(1)} %bitcast.14), channel_id=1, replica_groups=mesh['gx'=16,'gy'=2] {'gx'}, dimensions={0} | all-to-all | bytes 393216 | tf_op jit(solution)/shard_map/all_to_all | solution.py:359
  67.6 1.0 %shard_map.42 = (f32[3,16,16,512]{3,2,1,0:T(8,128)S(1)}, f32[2,48,512]{2,1,0:T(8,128)S(1)}) custom-call(f32[3,16,16,512]{3,2,1,0:T(8,128)S(1)} %get-tuple-element.13.field_ref, f32[3,16,16,512]{3,2,1,0:T(8,128)S(1)} %copy-done, f32[2,3,16,512]{3,2,1,0:T(8,128)S(1)} %copy-done.2, f32[384,128]{1,0:T(8,128)S(1)} %bitcast.11), custom_call_target="tpu_custom_call" | custom-call | tf_op jit(solution)/shard_map/pallas_call | solution.py:347
  68.6 2.6 %collective-permute-start.1 = (f32[2,48,512]{2,1,0:T(8,128)S(1)}, f32[2,48,512]{2,1,0:T(8,128)S(1)}, u32[]{:S(2)}, u32[]{:S(2)}) collective-permute-start(f32[2,48,512]{2,1,0:T(8,128)S(1)} %get-tuple-element.16), channel_id=1, source_target_pairs={{0,1},{1,0},{2,3},{3,2},{4,5},{5,4},{6,7},{7,6},{8,9},{9,8},{10,11... | collective-permute-start | bytes 589832 | tf_op jit(solution)/shard_map/ppermute | solution.py:368
  71.1 1.1 %collective-permute-done.1.beyond_ref = f32[2,48,512]{2,1,0:T(8,128)S(1)} collective-permute-done((f32[2,48,512]{2,1,0:T(8,128)S(1)}, f32[2,48,512]{2,1,0:T(8,128)S(1)}, u32[]{:S(2)}, u32[]{:S(2)}) %collective-permute-start.1) | collective-permute-done | bytes 196640 | tf_op jit(solution)/shard_map/ppermute | solution.py:368
  72.2 2.2 %shard_map.43 = f32[3,16,16,512]{3,2,1,0:T(8,128)} custom-call(f32[3,16,16,512]{3,2,1,0:T(8,128)S(1)} %get-tuple-element.15.field_ref, f32[2,48,512]{2,1,0:T(8,128)S(1)} %collective-permute-done.1.beyond_ref, f32[3,16,16,512]{3,2,1,0:T(8,128)S(1)} %copy-done), custom_call_target="tpu_custom_call" | custom-call | tf_op jit(solution)/shard_map/pallas_call | solution.py:347
Async XLA Ops:
  4.9 33.0 %copy-start = (f32[3,16,16,512]{3,2,1,0:T(8,128)S(1)}, f32[3,16,16,512]{3,2,1,0:T(8,128)}, u32[]{:S(2)}) copy-start(f32[3,16,16,512]{3,2,1,0:T(8,128)} %axes_ref.7) | copy-start | bytes 4718596
  4.9 32.9 %copy-start.2 = (f32[2,3,16,512]{3,2,1,0:T(8,128)S(1)}, f32[2,3,16,512]{3,2,1,0:T(8,128)}, u32[]{:S(2)}) copy-start(f32[2,3,16,512]{3,2,1,0:T(8,128)} %pins_ref.5) | copy-start | bytes 589828
  37.8 1.4 %copy-start.1 = (f32[3,16,16,512]{3,2,1,0:T(8,128)S(1)}, f32[3,16,16,512]{3,2,1,0:T(8,128)}, u32[]{:S(2)}) copy-start(f32[3,16,16,512]{3,2,1,0:T(8,128)} %field_ref.1) | copy-start | bytes 4718596
  40.2 3.9 %collective-permute-start = (f32[2,48,512]{2,1,0:T(8,128)S(1)}, f32[2,48,512]{2,1,0:T(8,128)S(1)}, u32[]{:S(2)}, u32[]{:S(2)}) collective-permute-start(f32[2,48,512]{2,1,0:T(8,128)S(1)} %get-tuple-element.12), channel_id=1, source_target_pairs={{0,1},{1,0},{2,3},{3,2},{4,5},{5,4},{6,7},{7,6},{8,9},{9,8},{10,11... | collective-permute-start | bytes 589832 | tf_op jit(solution)/shard_map/ppermute | solution.py:368
  68.6 3.6 %collective-permute-start.1 = (f32[2,48,512]{2,1,0:T(8,128)S(1)}, f32[2,48,512]{2,1,0:T(8,128)S(1)}, u32[]{:S(2)}, u32[]{:S(2)}) collective-permute-start(f32[2,48,512]{2,1,0:T(8,128)S(1)} %get-tuple-element.16), channel_id=1, source_target_pairs={{0,1},{1,0},{2,3},{3,2},{4,5},{5,4},{6,7},{7,6},{8,9},{9,8},{10,11... | collective-permute-start | bytes 589832 | tf_op jit(solution)/shard_map/ppermute | solution.py:368

commit v5 on v4

--- a/solution.py
+++ b/solution.py
@@ -184,46 +184,33 @@
     return found
 
 
-def send_tile(line, units, coupled, field_ref, axes_ref, pins_ref, out_ref, tile):
+def send_tile(line, units, values, field_ref, axes_ref, pins_ref, out_ref, tile):
     rows, width = field_ref.shape[2], field_ref.shape[3]
     tiles = width // LANES
-    values = COUPLED if coupled else RHS
     lanes = slice(tile * LANES, (tile + 1) * LANES)
     solved = solve_components(line, field_ref, axes_ref, pins_ref, lanes, None)
-    sent = []
     for component in range(3):
-        sent += [solved[component][0], solved[component][-1]]
-    if coupled:
-        sent += couplings(line, axes_ref, lanes)
-    for value in range(values):
-        out_ref[row_window(value, values, units, tile, tiles, rows), :] = sent[value]
-
-
-def first_kernel(
-    line, units, field_hbm, axes_hbm, pins_hbm, out_ref, field_ref, axes_ref, pins_ref, sems, pin_sem
-):
-    tiles = field_ref.shape[3] // LANES
-    pin_copy = pltpu.make_async_copy(pins_hbm, pins_ref, pin_sem)
-    copies = []
+        for side, end in enumerate((0, -1)):
+            at = row_window(2 * component + side, values, units, tile, tiles, rows)
+            out_ref[at, :] = solved[component][end]
+
+
+def coupling_kernel(line, units, axes_ref, out_ref):
+    rows, width = axes_ref.shape[2:]
+    tiles = width // LANES
     for tile in range(tiles):
-        lanes = pl.ds(tile * LANES, LANES)
-        at = (slice(None), slice(None), slice(None), lanes)
-        copies.append(
-            (
-                pltpu.make_async_copy(axes_hbm.at[at], axes_ref.at[at], sems.at[0, tile]),
-                pltpu.make_async_copy(field_hbm.at[at], field_ref.at[at], sems.at[1, tile]),
-            )
-        )
-        for copy in copies[-1]:
-            copy.start()
-        if tile == 0:
-            pin_copy.start()
-    for tile in range(tiles):
-        for copy in copies[tile]:
-            copy.wait()
-        if tile == 0:
-            pin_copy.wait()
-        send_tile(line, units, True, field_ref, axes_ref, pins_ref, out_ref, tile)
+        found = couplings(line, axes_ref, slice(tile * LANES, (tile + 1) * LANES))
+        for value, one in enumerate(found):
+            out_ref[row_window(value, COUPLED - RHS, units, tile, tiles, rows), :] = one
+
+
+def first_kernel(line, groups, units, coupling_ref, field_ref, axes_ref, pins_ref, out_ref):
+    extra = (COUPLED - RHS) * units
+    for d in range(groups):
+        start = (d * COUPLED + RHS) * units
+        out_ref[start : start + extra, :] = coupling_ref[d * extra : (d + 1) * extra, :]
+    for tile in range(field_ref.shape[3] // LANES):
+        send_tile(line, units, COUPLED, field_ref, axes_ref, pins_ref, out_ref, tile)
 
 
 def reduced_kernel(levels, groups, units, rhs_values, rhs_ref, coupling_ref, out_ref):
@@ -324,7 +311,7 @@
 ):
     rotate(field_ref, beyond_ref, axes_ref, out_ref)
     for tile in range(field_ref.shape[3] // LANES):
-        send_tile(line, units, False, out_ref, axes_ref, pins_ref, sent_ref, tile)
+        send_tile(line, units, RHS, out_ref, axes_ref, pins_ref, sent_ref, tile)
 
 
 def last_kernel(field_ref, beyond_ref, axes_ref, out_hbm, out_ref, sems):
@@ -338,19 +325,18 @@
 
 VMEM = pl.BlockSpec(memory_space=pltpu.VMEM)
 HBM = pl.BlockSpec(memory_space=pltpu.HBM)
-SMALL = 32 * 1024 * 1024
-LARGE = 63 * 1024 * 1024
-
-
-def call(kernel, shapes, *operands, read=VMEM, written=VMEM, scratch=(), limit=SMALL):
+LIMIT = 32 * 1024 * 1024
+
+
+def call(kernel, shapes, *operands, written=VMEM, scratch=()):
     shapes = [jax.ShapeDtypeStruct(shape, jnp.float32) for shape in shapes]
     return pl.pallas_call(
         kernel,
         out_shape=tuple(shapes),
-        in_specs=[read] * len(operands),
+        in_specs=[VMEM] * len(operands),
         out_specs=(written,) * len(shapes),
         scratch_shapes=scratch,
-        compiler_params=pltpu.CompilerParams(vmem_limit_bytes=limit),
+        compiler_params=pltpu.CompilerParams(vmem_limit_bytes=LIMIT),
     )(*operands)
 
 
@@ -383,21 +369,18 @@
     sent_shape = (groups * RHS * units, LANES)
 
     field = magnetization
+    (coupling,) = call(
+        functools.partial(coupling_kernel, line, units),
+        [(groups * (COUPLED - RHS) * units, LANES)],
+        easy_axes,
+    )
     (sent,) = call(
-        functools.partial(first_kernel, line, units),
+        functools.partial(first_kernel, line, groups, units),
         [(groups * COUPLED * units, LANES)],
+        coupling,
         field,
         easy_axes,
         pins,
-        read=HBM,
-        scratch=[
-            pltpu.VMEM(whole, jnp.float32),
-            pltpu.VMEM(whole, jnp.float32),
-            pltpu.VMEM(pins.shape, jnp.float32),
-            pltpu.SemaphoreType.DMA((2, tiles)),
-            pltpu.SemaphoreType.DMA,
-        ],
-        limit=LARGE,
     )
     coupling = None
     for stepno in range(STEPS):

time: 75.1 us -> 72.3 us (0.963)
  Pallas kernels: 11.6 us -> 8.67 us
    pallas_call x7 -> x8, Pallas kernels: 11.6 us -> 8.67 us  [call(): pl.pallas_call(kernel, out_shape=tuple(shapes), in_specs=[VMEM] * len(ope...]
    unnamed x6 -> x8, local copies, waits for them, and re-layouts: 1.42 us -> 1.89 us
where the time goes in v5:
time: 72.3 us; the launch traced here: 71.7 us
  blocking collectives  53.6 us (74%)
  Pallas kernels  8.67 us (12%)
  starting transfers between devices  5.39 us (7%)
  waiting for transfers between devices  2.14 us (3%)
  local copies, waits for them, and re-layouts  1.89 us (3%)
    all_to_all x4, blocking collectives, exchange(): lax.all_to_all(parts, 'gx', split_axis=0, concat_axis=0, tiled=True)  53.6 us
    pallas_call x8, Pallas kernels, call(): pl.pallas_call(kernel, out_shape=tuple(shapes), in_specs=[VMEM] * len(ope...  8.67 us
    ppermute x2, starting transfers between devices, from_neighbours(): return lax.ppermute(edges, 'gy', forward)  5.39 us
    ppermute x2, waiting for transfers between devices, from_neighbours(): return lax.ppermute(edges, 'gy', forward)  2.14 us
    unnamed x8, local copies, waits for them, and re-layouts  1.89 us
  transfers between devices with their start and end apart: 2, of which 2 were waited for; matrix products, arithmetic and copies ran while one was open for 0% of the time, Pallas kernels for 0%

profile of v5, /device:TPU:1, one launch (start us, length us, event | category | flops | bytes accessed | tf_op | source)
XLA Modules:
  0.0 71.7 jit_solution(13291081140136836714)
XLA Ops:
  0.0 0.0 copy-start
  0.0 1.4 %copy-done = f32[3,16,16,512]{3,2,1,0:T(8,128)S(1)} copy-done((f32[3,16,16,512]{3,2,1,0:T(8,128)S(1)}, f32[3,16,16,512]{3,2,1,0:T(8,128)}, u32[]{:S(2)}) %copy-start) | copy-done | bytes 1572888
  1.4 0.0 copy-start.2
  1.4 0.0 copy-start.3
  1.4 0.9 %shard_map.37.coupling_ref = f32[640,128]{1,0:T(8,128)S(1)} custom-call(f32[3,16,16,512]{3,2,1,0:T(8,128)S(1)} %copy-done), custom_call_target="tpu_custom_call" | custom-call | tf_op jit(solution)/shard_map/pallas_call | solution.py:333
  2.3 0.5 copy-done.2
  2.8 0.0 copy-done.3
  2.8 1.0 %shard_map.38 = f32[1024,128]{1,0:T(8,128)S(1)} custom-call(f32[640,128]{1,0:T(8,128)S(1)} %shard_map.37.coupling_ref, f32[3,16,16,512]{3,2,1,0:T(8,128)S(1)} %copy-done.2, f32[3,16,16,512]{3,2,1,0:T(8,128)S(1)} %copy-done, f32[2,3,16,512]{3,2,1,0:T(8,128)S(1)} %copy-done.3), custom_call_target="tpu_custom_call" | custom-call | tf_op jit(solution)/shard_map/pallas_call | solution.py:333
  3.8 0.0 copy-start.1
  3.8 19.6 %all_to_all.20 = f32[16,64,128]{2,1,0:T(8,128)S(1)} all-to-all(f32[16,64,128]{2,1,0:T(8,128)S(1)} %bitcast.11), channel_id=1, replica_groups=mesh['gx'=16,'gy'=2] {'gx'}, dimensions={0} | all-to-all | bytes 1048576 | tf_op jit(solution)/shard_map/all_to_all | solution.py:345
  23.4 0.2 shard_map.39
  23.7 12.8 %all_to_all.21 = f32[16,24,128]{2,1,0:T(8,128)S(1)} all-to-all(f32[16,24,128]{2,1,0:T(8,128)S(1)} %bitcast.16), channel_id=1, replica_groups=mesh['gx'=16,'gy'=2] {'gx'}, dimensions={0} | all-to-all | bytes 393216 | tf_op jit(solution)/shard_map/all_to_all | solution.py:345
  36.5 0.0 copy-done.1
  36.5 1.0 %shard_map.40 = (f32[3,16,16,512]{3,2,1,0:T(8,128)S(1)}, f32[2,48,512]{2,1,0:T(8,128)S(1)}) custom-call(f32[3,16,16,512]{3,2,1,0:T(8,128)S(1)} %copy-done.2, f32[3,16,16,512]{3,2,1,0:T(8,128)S(1)} %copy-done.1, f32[2,3,16,512]{3,2,1,0:T(8,128)S(1)} %copy-done.3, f32[384,128]{1,0:T(8,128)S(1)} %bitcast.13), custom_call_target="tpu_custom_call" | custom-call | tf_op jit(solution)/shard_map/pallas_call | solution.py:333
  37.5 2.8 %collective-permute-start = (f32[2,48,512]{2,1,0:T(8,128)S(1)}, f32[2,48,512]{2,1,0:T(8,128)S(1)}, u32[]{:S(2)}, u32[]{:S(2)}) collective-permute-start(f32[2,48,512]{2,1,0:T(8,128)S(1)} %get-tuple-element.12), channel_id=1, source_target_pairs={{0,1},{1,0},{2,3},{3,2},{4,5},{5,4},{6,7},{7,6},{8,9},{9,8},{10,11... | collective-permute-start | bytes 589832 | tf_op jit(solution)/shard_map/ppermute | solution.py:354
  40.3 1.1 %collective-permute-done.beyond_ref = f32[2,48,512]{2,1,0:T(8,128)S(1)} collective-permute-done((f32[2,48,512]{2,1,0:T(8,128)S(1)}, f32[2,48,512]{2,1,0:T(8,128)S(1)}, u32[]{:S(2)}, u32[]{:S(2)}) %collective-permute-start) | collective-permute-done | bytes 196640 | tf_op jit(solution)/shard_map/ppermute | solution.py:354
  41.4 2.1 %shard_map.41 = (f32[3,16,16,512]{3,2,1,0:T(8,128)S(1)}, f32[384,128]{1,0:T(8,128)S(1)}) custom-call(f32[3,16,16,512]{3,2,1,0:T(8,128)S(1)} %get-tuple-element.11.field_ref, f32[2,48,512]{2,1,0:T(8,128)S(1)} %collective-permute-done.beyond_ref, f32[3,16,16,512]{3,2,1,0:T(8,128)S(1)} %copy-done.1, f32[2,3,16,512]{3,2,1,0:T(8,128)S(1)} %copy-done.3), custom_call_target="tpu_custom_call" | custom-call | tf_op jit(solution)/shard_map/pallas_call | solution.py:333
  43.5 10.0 %all_to_all.22 = f32[16,24,128]{2,1,0:T(8,128)S(1)} all-to-all(f32[16,24,128]{2,1,0:T(8,128)S(1)} %bitcast.17), channel_id=1, replica_groups=mesh['gx'=16,'gy'=2] {'gx'}, dimensions={0} | all-to-all | bytes 393216 | tf_op jit(solution)/shard_map/all_to_all | solution.py:345
  53.5 0.2 shard_map.42
  53.8 11.1 %all_to_all.23 = f32[16,24,128]{2,1,0:T(8,128)S(1)} all-to-all(f32[16,24,128]{2,1,0:T(8,128)S(1)} %bitcast.15), channel_id=1, replica_groups=mesh['gx'=16,'gy'=2] {'gx'}, dimensions={0} | all-to-all | bytes 393216 | tf_op jit(solution)/shard_map/all_to_all | solution.py:345
  64.9 1.0 %shard_map.43 = (f32[3,16,16,512]{3,2,1,0:T(8,128)S(1)}, f32[2,48,512]{2,1,0:T(8,128)S(1)}) custom-call(f32[3,16,16,512]{3,2,1,0:T(8,128)S(1)} %get-tuple-element.13.field_ref, f32[3,16,16,512]{3,2,1,0:T(8,128)S(1)} %copy-done.1, f32[2,3,16,512]{3,2,1,0:T(8,128)S(1)} %copy-done.3, f32[384,128]{1,0:T(8,128)S(1)} %bitcast.12), custom_call_target="tpu_custom_call" | custom-call | tf_op jit(solution)/shard_map/pallas_call | solution.py:333
  65.9 2.6 %collective-permute-start.1 = (f32[2,48,512]{2,1,0:T(8,128)S(1)}, f32[2,48,512]{2,1,0:T(8,128)S(1)}, u32[]{:S(2)}, u32[]{:S(2)}) collective-permute-start(f32[2,48,512]{2,1,0:T(8,128)S(1)} %get-tuple-element.16), channel_id=1, source_target_pairs={{0,1},{1,0},{2,3},{3,2},{4,5},{5,4},{6,7},{7,6},{8,9},{9,8},{10,11... | collective-permute-start | bytes 589832 | tf_op jit(solution)/shard_map/ppermute | solution.py:354
  68.4 1.1 %collective-permute-done.1.beyond_ref = f32[2,48,512]{2,1,0:T(8,128)S(1)} collective-permute-done((f32[2,48,512]{2,1,0:T(8,128)S(1)}, f32[2,48,512]{2,1,0:T(8,128)S(1)}, u32[]{:S(2)}, u32[]{:S(2)}) %collective-permute-start.1) | collective-permute-done | bytes 196640 | tf_op jit(solution)/shard_map/ppermute | solution.py:354
  69.5 2.2 %shard_map.44 = f32[3,16,16,512]{3,2,1,0:T(8,128)} custom-call(f32[3,16,16,512]{3,2,1,0:T(8,128)S(1)} %get-tuple-element.15.field_ref, f32[2,48,512]{2,1,0:T(8,128)S(1)} %collective-permute-done.1.beyond_ref, f32[3,16,16,512]{3,2,1,0:T(8,128)S(1)} %copy-done.1), custom_call_target="tpu_custom_call" | custom-call | tf_op jit(solution)/shard_map/pallas_call | solution.py:333
Async XLA Ops:
  0.0 1.4 %copy-start = (f32[3,16,16,512]{3,2,1,0:T(8,128)S(1)}, f32[3,16,16,512]{3,2,1,0:T(8,128)}, u32[]{:S(2)}) copy-start(f32[3,16,16,512]{3,2,1,0:T(8,128)} %axes_ref.11) | copy-start | bytes 4718596
  1.4 1.4 %copy-start.2 = (f32[3,16,16,512]{3,2,1,0:T(8,128)S(1)}, f32[3,16,16,512]{3,2,1,0:T(8,128)}, u32[]{:S(2)}) copy-start(f32[3,16,16,512]{3,2,1,0:T(8,128)} %field_ref.3) | copy-start | bytes 4718596
  1.4 1.4 %copy-start.3 = (f32[2,3,16,512]{3,2,1,0:T(8,128)S(1)}, f32[2,3,16,512]{3,2,1,0:T(8,128)}, u32[]{:S(2)}) copy-start(f32[2,3,16,512]{3,2,1,0:T(8,128)} %pins_ref.7) | copy-start | bytes 589828
  3.8 32.7 %copy-start.1 = (f32[3,16,16,512]{3,2,1,0:T(8,128)S(1)}, f32[3,16,16,512]{3,2,1,0:T(8,128)}, u32[]{:S(2)}) copy-start(f32[3,16,16,512]{3,2,1,0:T(8,128)} %axes_ref.11) | copy-start | bytes 4718596
  37.5 3.9 %collective-permute-start = (f32[2,48,512]{2,1,0:T(8,128)S(1)}, f32[2,48,512]{2,1,0:T(8,128)S(1)}, u32[]{:S(2)}, u32[]{:S(2)}) collective-permute-start(f32[2,48,512]{2,1,0:T(8,128)S(1)} %get-tuple-element.12), channel_id=1, source_target_pairs={{0,1},{1,0},{2,3},{3,2},{4,5},{5,4},{6,7},{7,6},{8,9},{9,8},{10,11... | collective-permute-start | bytes 589832 | tf_op jit(solution)/shard_map/ppermute | solution.py:354
  65.9 3.6 %collective-permute-start.1 = (f32[2,48,512]{2,1,0:T(8,128)S(1)}, f32[2,48,512]{2,1,0:T(8,128)S(1)}, u32[]{:S(2)}, u32[]{:S(2)}) collective-permute-start(f32[2,48,512]{2,1,0:T(8,128)S(1)} %get-tuple-element.16), channel_id=1, source_target_pairs={{0,1},{1,0},{2,3},{3,2},{4,5},{5,4},{6,7},{7,6},{8,9},{9,8},{10,11... | collective-permute-start | bytes 589832 | tf_op jit(solution)/shard_map/ppermute | solution.py:354

commit v6 on v5

--- a/solution.py
+++ b/solution.py
@@ -134,9 +134,13 @@
     return source
 
 
-def solve_components(line, field_ref, axes_ref, pins_ref, lanes, ghosts):
+def read_field(field_ref, lanes):
+    planes = field_ref.shape[1]
+    return [[field_ref[c, i, :, lanes] for i in range(planes)] for c in range(3)]
+
+
+def solve_components(line, field, axes_ref, pins_ref, lanes, ghosts):
     planes = line.planes
-    field = [[field_ref[c, i, :, lanes] for i in range(planes)] for c in range(3)]
     axes = [[axes_ref[c, i, :, lanes] for i in range(planes)] for c in range(3)]
     for component in range(3):
         source = []
@@ -184,11 +188,11 @@
     return found
 
 
-def send_tile(line, units, values, field_ref, axes_ref, pins_ref, out_ref, tile):
-    rows, width = field_ref.shape[2], field_ref.shape[3]
+def send_tile(line, units, values, field, axes_ref, pins_ref, out_ref, tile):
+    rows, width = axes_ref.shape[2:]
     tiles = width // LANES
     lanes = slice(tile * LANES, (tile + 1) * LANES)
-    solved = solve_components(line, field_ref, axes_ref, pins_ref, lanes, None)
+    solved = solve_components(line, field, axes_ref, pins_ref, lanes, None)
     for component in range(3):
         for side, end in enumerate((0, -1)):
             at = row_window(2 * component + side, values, units, tile, tiles, rows)
@@ -210,7 +214,8 @@
         start = (d * COUPLED + RHS) * units
         out_ref[start : start + extra, :] = coupling_ref[d * extra : (d + 1) * extra, :]
     for tile in range(field_ref.shape[3] // LANES):
-        send_tile(line, units, COUPLED, field_ref, axes_ref, pins_ref, out_ref, tile)
+        field = read_field(field_ref, slice(tile * LANES, (tile + 1) * LANES))
+        send_tile(line, units, COUPLED, field, axes_ref, pins_ref, out_ref, tile)
 
 
 def reduced_kernel(levels, groups, units, rhs_values, rhs_ref, coupling_ref, out_ref):
@@ -263,7 +268,8 @@
             ]
             for c in range(3)
         ]
-        solved = solve_components(line, field_ref, axes_ref, pins_ref, lanes, ghosts)
+        field = read_field(field_ref, lanes)
+        solved = solve_components(line, field, axes_ref, pins_ref, lanes, ghosts)
         for c in range(3):
             for i in range(planes):
                 out_ref[c, i, :, lanes] = solved[c][i]
@@ -272,7 +278,12 @@
                 edge_ref[1, at : at + 1, lanes] = solved[c][i][rows - 1 :]
 
 
-def rotate(field_ref, beyond_ref, axes_ref, out_ref, finished=None):
+def unit_scale(parts):
+    square = parts[0] * parts[0] + parts[1] * parts[1] + parts[2] * parts[2]
+    return jnp.minimum(lax.rsqrt(square), 1.0 / norm_floor)
+
+
+def turn_kernel(field_ref, axes_ref, out_ref, raw_ref):
     planes, rows, width = field_ref.shape[1:]
     row = lax.broadcasted_iota(jnp.int32, (rows, width), 0)
     for i in range(planes):
@@ -281,13 +292,8 @@
         projection = field[0] * axes[0] + field[1] * axes[1] + field[2] * axes[2]
         effective = []
         for c in range(3):
-            at = c * planes + i
-            below = jnp.where(
-                row == 0, beyond_ref[1, at : at + 1, :], pltpu.roll(field[c], 1, 0)
-            )
-            above = jnp.where(
-                row == rows - 1, beyond_ref[0, at : at + 1, :], pltpu.roll(field[c], rows - 1, 0)
-            )
+            below = jnp.where(row == 0, 0.0, pltpu.roll(field[c], 1, 0))
+            above = jnp.where(row == rows - 1, 0.0, pltpu.roll(field[c], rows - 1, 0))
             beside = pltpu.roll(field[c], 1, 1) + pltpu.roll(field[c], width - 1, 1)
             effective.append(
                 exchange_rate * (((above + below) + beside) - 4.0 * field[c])
@@ -298,28 +304,74 @@
             d, e = (c + 1) % 3, (c + 2) % 3
             twisted = field[d] * effective[e] - field[e] * effective[d]
             rotated.append(field[c] - torque_rate * twisted)
-        square = rotated[0] * rotated[0] + rotated[1] * rotated[1] + rotated[2] * rotated[2]
-        scale = jnp.minimum(lax.rsqrt(square), 1.0 / norm_floor)
-        for c in range(3):
+        scale = unit_scale(rotated)
+        for c in range(3):
+            at = c * planes + i
             out_ref[c, i] = rotated[c] * scale
-        if finished is not None:
-            finished(i)
-
-
-def rotate_and_send_kernel(
-    line, units, field_ref, beyond_ref, axes_ref, pins_ref, out_ref, sent_ref
+            raw_ref[0, at : at + 1, :] = rotated[c][:1]
+            raw_ref[1, at : at + 1, :] = rotated[c][rows - 1 :]
+
+
+def mend_edges(edge_ref, raw_ref, beyond_ref, mended_ref):
+    planes = edge_ref.shape[1] // 3
+    for side in range(2):
+        parts = [slice(c * planes, (c + 1) * planes) for c in range(3)]
+        field = [edge_ref[side, part, :] for part in parts]
+        beyond = [beyond_ref[1 - side, part, :] for part in parts]
+        rotated = []
+        for c in range(3):
+            d, e = (c + 1) % 3, (c + 2) % 3
+            twisted = field[d] * beyond[e] - field[e] * beyond[d]
+            rotated.append(raw_ref[side, parts[c], :] - (torque_rate * exchange_rate) * twisted)
+        scale = unit_scale(rotated)
+        for c in range(3):
+            mended_ref[side, parts[c], :] = rotated[c] * scale
+
+
+def mended(turned, mended_ref, at, lanes):
+    rows = turned.shape[0]
+    row = lax.broadcasted_iota(jnp.int32, turned.shape, 0)
+    turned = jnp.where(row == 0, mended_ref[0, at : at + 1, lanes], turned)
+    return jnp.where(row == rows - 1, mended_ref[1, at : at + 1, lanes], turned)
+
+
+def mend_and_send_kernel(
+    line,
+    units,
+    turned_ref,
+    edge_ref,
+    raw_ref,
+    beyond_ref,
+    axes_ref,
+    pins_ref,
+    out_ref,
+    sent_ref,
+    mended_ref,
 ):
-    rotate(field_ref, beyond_ref, axes_ref, out_ref)
-    for tile in range(field_ref.shape[3] // LANES):
-        send_tile(line, units, RHS, out_ref, axes_ref, pins_ref, sent_ref, tile)
-
-
-def last_kernel(field_ref, beyond_ref, axes_ref, out_hbm, out_ref, sems):
+    planes = line.planes
+    mend_edges(edge_ref, raw_ref, beyond_ref, mended_ref)
+    for tile in range(turned_ref.shape[3] // LANES):
+        lanes = slice(tile * LANES, (tile + 1) * LANES)
+        field = read_field(turned_ref, lanes)
+        for c in range(3):
+            for i in range(planes):
+                field[c][i] = mended(field[c][i], mended_ref, c * planes + i, lanes)
+                out_ref[c, i, :, lanes] = field[c][i]
+        send_tile(line, units, RHS, field, axes_ref, pins_ref, sent_ref, tile)
+
+
+def last_kernel(turned_ref, edge_ref, raw_ref, beyond_ref, out_hbm, out_ref, mended_ref, sems):
+    planes = turned_ref.shape[1]
+
     def copy(i):
         return pltpu.make_async_copy(out_ref.at[:, i], out_hbm.at[:, i], sems.at[i])
 
-    rotate(field_ref, beyond_ref, axes_ref, out_ref, lambda i: copy(i).start())
-    for i in range(field_ref.shape[1]):
+    mend_edges(edge_ref, raw_ref, beyond_ref, mended_ref)
+    for i in range(planes):
+        for c in range(3):
+            out_ref[c, i] = mended(turned_ref[c, i], mended_ref, c * planes + i, slice(None))
+        copy(i).start()
+    for i in range(planes):
         copy(i).wait()
 
 
@@ -367,6 +419,7 @@
     levels = make_levels(planes, groups)
     whole = magnetization.shape
     sent_shape = (groups * RHS * units, LANES)
+    edge_shape = (2, 3 * planes, width)
 
     field = magnetization
     (coupling,) = call(
@@ -396,31 +449,40 @@
         ghosts = exchange(ghosts, groups)
         solved, edges = call(
             functools.partial(finish_kernel, line, units),
-            [whole, (2, 3 * planes, width)],
+            [whole, edge_shape],
             field,
             easy_axes,
             pins,
             ghosts,
         )
         beyond = from_neighbours(edges)
+        turned, raw = call(turn_kernel, [whole, edge_shape], solved, easy_axes)
         if stepno < STEPS - 1:
             field, sent = call(
-                functools.partial(rotate_and_send_kernel, line, units),
+                functools.partial(mend_and_send_kernel, line, units),
                 [whole, sent_shape],
-                solved,
+                turned,
+                edges,
+                raw,
                 beyond,
                 easy_axes,
                 pins,
+                scratch=[pltpu.VMEM(edge_shape, jnp.float32)],
             )
         else:
             (field,) = call(
                 last_kernel,
                 [whole],
-                solved,
+                turned,
+                edges,
+                raw,
                 beyond,
-                easy_axes,
                 written=HBM,
-                scratch=[pltpu.VMEM(whole, jnp.float32), pltpu.SemaphoreType.DMA((planes,))],
+                scratch=[
+                    pltpu.VMEM(whole, jnp.float32),
+                    pltpu.VMEM(edge_shape, jnp.float32),
+                    pltpu.SemaphoreType.DMA((planes,)),
+                ],
             )
     return field
 

time: 72.3 us -> 71.5 us (0.989)
  waiting for transfers between devices: 2.14 us -> 0.01 us
  Pallas kernels: 8.67 us -> 9.88 us
    ppermute x2, waiting for transfers between devices: 2.14 us -> 0.01 us  [from_neighbours(): return lax.ppermute(edges, 'gy', forward)]
    pallas_call x8 -> x10, Pallas kernels: 8.67 us -> 9.88 us  [call(): pl.pallas_call(kernel, out_shape=tuple(shapes), in_specs=[VMEM] * len(ope...]
  transfers between devices with their start and end apart: 2 -> 2, of which waited for: 2 -> 0; matrix products, arithmetic and copies ran while one was open for 0% -> 0% of each run, Pallas kernels for 0% -> 4%
where the time goes in v6:
time: 71.5 us; the launch traced here: 71.2 us
  blocking collectives  53.7 us (75%)
  Pallas kernels  9.88 us (14%)
  starting transfers between devices  5.65 us (8%)
  local copies, waits for them, and re-layouts  1.89 us (3%)
    all_to_all x4, blocking collectives, exchange(): lax.all_to_all(parts, 'gx', split_axis=0, concat_axis=0, tiled=True)  53.7 us
    pallas_call x10, Pallas kernels, call(): pl.pallas_call(kernel, out_shape=tuple(shapes), in_specs=[VMEM] * len(ope...  9.88 us
    ppermute x2, starting transfers between devices, from_neighbours(): return lax.ppermute(edges, 'gy', forward)  5.65 us
    unnamed x8, local copies, waits for them, and re-layouts  1.89 us
  transfers between devices with their start and end apart: 2, of which 0 were waited for; matrix products, arithmetic and copies ran while one was open for 0% of the time, Pallas kernels for 4%

profile of v6, /device:TPU:1, one launch (start us, length us, event | category | flops | bytes accessed | tf_op | source)
XLA Modules:
  0.0 71.2 jit_solution(8579504175449931369)
XLA Ops:
  0.0 0.0 copy-start
  0.0 1.4 %copy-done = f32[3,16,16,512]{3,2,1,0:T(8,128)S(1)} copy-done((f32[3,16,16,512]{3,2,1,0:T(8,128)S(1)}, f32[3,16,16,512]{3,2,1,0:T(8,128)}, u32[]{:S(2)}) %copy-start) | copy-done | bytes 1572888
  1.4 0.9 %shard_map.37.coupling_ref = f32[640,128]{1,0:T(8,128)S(1)} custom-call(f32[3,16,16,512]{3,2,1,0:T(8,128)S(1)} %copy-done), custom_call_target="tpu_custom_call" | custom-call | tf_op jit(solution)/shard_map/pallas_call | solution.py:385
  2.3 0.5 copy-done.2
  2.8 0.0 copy-done.3
  2.8 1.0 %shard_map.38 = f32[1024,128]{1,0:T(8,128)S(1)} custom-call(f32[640,128]{1,0:T(8,128)S(1)} %shard_map.37.coupling_ref, f32[3,16,16,512]{3,2,1,0:T(8,128)S(1)} %copy-done.2, f32[3,16,16,512]{3,2,1,0:T(8,128)S(1)} %copy-done, f32[2,3,16,512]{3,2,1,0:T(8,128)S(1)} %copy-done.3), custom_call_target="tpu_custom_call" | custom-call | tf_op jit(solution)/shard_map/pallas_call | solution.py:385
  3.8 0.0 copy-start.1
  3.8 19.6 %all_to_all.20 = f32[16,64,128]{2,1,0:T(8,128)S(1)} all-to-all(f32[16,64,128]{2,1,0:T(8,128)S(1)} %bitcast.11), channel_id=1, replica_groups=mesh['gx'=16,'gy'=2] {'gx'}, dimensions={0} | all-to-all | bytes 1048576 | tf_op jit(solution)/shard_map/all_to_all | solution.py:397
  23.4 0.2 shard_map.39
  23.7 12.8 %all_to_all.21 = f32[16,24,128]{2,1,0:T(8,128)S(1)} all-to-all(f32[16,24,128]{2,1,0:T(8,128)S(1)} %bitcast.16), channel_id=1, replica_groups=mesh['gx'=16,'gy'=2] {'gx'}, dimensions={0} | all-to-all | bytes 393216 | tf_op jit(solution)/shard_map/all_to_all | solution.py:397
  36.5 0.0 copy-done.1
  36.5 1.0 %shard_map.40 = (f32[3,16,16,512]{3,2,1,0:T(8,128)S(1)}, f32[2,48,512]{2,1,0:T(8,128)S(1)}) custom-call(f32[3,16,16,512]{3,2,1,0:T(8,128)S(1)} %copy-done.2, f32[3,16,16,512]{3,2,1,0:T(8,128)S(1)} %copy-done.1, f32[2,3,16,512]{3,2,1,0:T(8,128)S(1)} %copy-done.3, f32[384,128]{1,0:T(8,128)S(1)} %bitcast.13), custom_call_target="tpu_custom_call" | custom-call | tf_op jit(solution)/shard_map/pallas_call | solution.py:385
  37.5 2.8 %collective-permute-start = (f32[2,48,512]{2,1,0:T(8,128)S(1)}, f32[2,48,512]{2,1,0:T(8,128)S(1)}, u32[]{:S(2)}, u32[]{:S(2)}) collective-permute-start(f32[2,48,512]{2,1,0:T(8,128)S(1)} %get-tuple-element.17.edge_ref), channel_id=1, source_target_pairs={{0,1},{1,0},{2,3},{3,2},{4,5},{5,4},{6,7},{7,6},{8,9},{9,8},{10,11... | collective-permute-start | bytes 589832 | tf_op jit(solution)/shard_map/ppermute | solution.py:406
  40.3 1.4 %shard_map.41 = (f32[3,16,16,512]{3,2,1,0:T(8,128)S(1)}, f32[2,48,512]{2,1,0:T(8,128)S(1)}) custom-call(f32[3,16,16,512]{3,2,1,0:T(8,128)S(1)} %get-tuple-element.15.field_ref, f32[3,16,16,512]{3,2,1,0:T(8,128)S(1)} %copy-done.1), custom_call_target="tpu_custom_call" | custom-call | tf_op jit(solution)/shard_map/pallas_call | solution.py:385
  41.8 0.0 collective-permute-done.beyond_ref
  41.8 1.3 %shard_map.42 = (f32[3,16,16,512]{3,2,1,0:T(8,128)S(1)}, f32[384,128]{1,0:T(8,128)S(1)}) custom-call(f32[3,16,16,512]{3,2,1,0:T(8,128)S(1)} %get-tuple-element.16.turned_ref, f32[2,48,512]{2,1,0:T(8,128)S(1)} %get-tuple-element.17.edge_ref, f32[2,48,512]{2,1,0:T(8,128)S(1)} %get-tuple-element.18.raw_ref, f32[2,48,512]{2,1,0:T(8,128)S(1)} %collective-permute-done.beyond_ref, ...), custom_call_target="tpu_custom_call" | custom-call | tf_op jit(solution)/shard_map/pallas_call | solution.py:385
  43.1 10.7 %all_to_all.22 = f32[16,24,128]{2,1,0:T(8,128)S(1)} all-to-all(f32[16,24,128]{2,1,0:T(8,128)S(1)} %bitcast.17), channel_id=1, replica_groups=mesh['gx'=16,'gy'=2] {'gx'}, dimensions={0} | all-to-all | bytes 393216 | tf_op jit(solution)/shard_map/all_to_all | solution.py:397
  53.8 0.2 shard_map.43
  54.0 10.5 %all_to_all.23 = f32[16,24,128]{2,1,0:T(8,128)S(1)} all-to-all(f32[16,24,128]{2,1,0:T(8,128)S(1)} %bitcast.15), channel_id=1, replica_groups=mesh['gx'=16,'gy'=2] {'gx'}, dimensions={0} | all-to-all | bytes 393216 | tf_op jit(solution)/shard_map/all_to_all | solution.py:397
  64.5 1.0 %shard_map.44 = (f32[3,16,16,512]{3,2,1,0:T(8,128)S(1)}, f32[2,48,512]{2,1,0:T(8,128)S(1)}) custom-call(f32[3,16,16,512]{3,2,1,0:T(8,128)S(1)} %get-tuple-element.19.field_ref, f32[3,16,16,512]{3,2,1,0:T(8,128)S(1)} %copy-done.1, f32[2,3,16,512]{3,2,1,0:T(8,128)S(1)} %copy-done.3, f32[384,128]{1,0:T(8,128)S(1)} %bitcast.12), custom_call_target="tpu_custom_call" | custom-call | tf_op jit(solution)/shard_map/pallas_call | solution.py:385
  65.5 2.8 %collective-permute-start.1 = (f32[2,48,512]{2,1,0:T(8,128)S(1)}, f32[2,48,512]{2,1,0:T(8,128)S(1)}, u32[]{:S(2)}, u32[]{:S(2)}) collective-permute-start(f32[2,48,512]{2,1,0:T(8,128)S(1)} %get-tuple-element.23.edge_ref), channel_id=1, source_target_pairs={{0,1},{1,0},{2,3},{3,2},{4,5},{5,4},{6,7},{7,6},{8,9},{9,8},{10,11... | collective-permute-start | bytes 589832 | tf_op jit(solution)/shard_map/ppermute | solution.py:406
  68.3 1.4 %shard_map.45 = (f32[3,16,16,512]{3,2,1,0:T(8,128)S(1)}, f32[2,48,512]{2,1,0:T(8,128)S(1)}) custom-call(f32[3,16,16,512]{3,2,1,0:T(8,128)S(1)} %get-tuple-element.21.field_ref, f32[3,16,16,512]{3,2,1,0:T(8,128)S(1)} %copy-done.1), custom_call_target="tpu_custom_call" | custom-call | tf_op jit(solution)/shard_map/pallas_call | solution.py:385
  69.8 0.0 collective-permute-done.1.beyond_ref
  69.8 1.3 %shard_map.46 = f32[3,16,16,512]{3,2,1,0:T(8,128)} custom-call(f32[3,16,16,512]{3,2,1,0:T(8,128)S(1)} %get-tuple-element.22.turned_ref, f32[2,48,512]{2,1,0:T(8,128)S(1)} %get-tuple-element.23.edge_ref, f32[2,48,512]{2,1,0:T(8,128)S(1)} %get-tuple-element.24.raw_ref, f32[2,48,512]{2,1,0:T(8,128)S(1)} %collective-permute-done.1.beyond_ref), custom_call_target="tpu_custom_call" | custom-call | tf_op jit(solution)/shard_map/pallas_call | solution.py:385
  (2 shorter events, 0.0 us)
Async XLA Ops:
  0.0 1.4 %copy-start = (f32[3,16,16,512]{3,2,1,0:T(8,128)S(1)}, f32[3,16,16,512]{3,2,1,0:T(8,128)}, u32[]{:S(2)}) copy-start(f32[3,16,16,512]{3,2,1,0:T(8,128)} %axes_ref.13) | copy-start | bytes 4718596
  1.4 1.4 %copy-start.2 = (f32[3,16,16,512]{3,2,1,0:T(8,128)S(1)}, f32[3,16,16,512]{3,2,1,0:T(8,128)}, u32[]{:S(2)}) copy-start(f32[3,16,16,512]{3,2,1,0:T(8,128)} %field_ref.3) | copy-start | bytes 4718596
  1.4 1.4 %copy-start.3 = (f32[2,3,16,512]{3,2,1,0:T(8,128)S(1)}, f32[2,3,16,512]{3,2,1,0:T(8,128)}, u32[]{:S(2)}) copy-start(f32[2,3,16,512]{3,2,1,0:T(8,128)} %pins_ref.7) | copy-start | bytes 589828
  3.8 32.7 %copy-start.1 = (f32[3,16,16,512]{3,2,1,0:T(8,128)S(1)}, f32[3,16,16,512]{3,2,1,0:T(8,128)}, u32[]{:S(2)}) copy-start(f32[3,16,16,512]{3,2,1,0:T(8,128)} %axes_ref.13) | copy-start | bytes 4718596
  37.5 4.3 %collective-permute-start = (f32[2,48,512]{2,1,0:T(8,128)S(1)}, f32[2,48,512]{2,1,0:T(8,128)S(1)}, u32[]{:S(2)}, u32[]{:S(2)}) collective-permute-start(f32[2,48,512]{2,1,0:T(8,128)S(1)} %get-tuple-element.17.edge_ref), channel_id=1, source_target_pairs={{0,1},{1,0},{2,3},{3,2},{4,5},{5,4},{6,7},{7,6},{8,9},{9,8},{10,11... | collective-permute-start | bytes 589832 | tf_op jit(solution)/shard_map/ppermute | solution.py:406
  65.5 4.3 %collective-permute-start.1 = (f32[2,48,512]{2,1,0:T(8,128)S(1)}, f32[2,48,512]{2,1,0:T(8,128)S(1)}, u32[]{:S(2)}, u32[]{:S(2)}) collective-permute-start(f32[2,48,512]{2,1,0:T(8,128)S(1)} %get-tuple-element.23.edge_ref), channel_id=1, source_target_pairs={{0,1},{1,0},{2,3},{3,2},{4,5},{5,4},{6,7},{7,6},{8,9},{9,8},{10,11... | collective-permute-start | bytes 589832 | tf_op jit(solution)/shard_map/ppermute | solution.py:406

commit v7 on v6

--- a/solution.py
+++ b/solution.py
@@ -120,9 +120,12 @@
     return total if term is None else total + weight * term
 
 
-def row_window(value, values, units, tile, tiles, rows):
-    start = (tile // units) * values * units + value * units + tile % units
-    return pl.ds(start, rows, stride=tiles * values)
+def pieces(value, values, units, tile, rows):
+    step = min(units, rows)
+    for start in range(0, rows, step):
+        at = tile * rows + start
+        to = (at // units * values + value) * units + at % units
+        yield slice(start, start + step), slice(to, to + step)
 
 
 def pinned(source, pins_ref, component, lanes):
@@ -189,14 +192,14 @@
 
 
 def send_tile(line, units, values, field, axes_ref, pins_ref, out_ref, tile):
-    rows, width = axes_ref.shape[2:]
-    tiles = width // LANES
+    rows = axes_ref.shape[2]
     lanes = slice(tile * LANES, (tile + 1) * LANES)
     solved = solve_components(line, field, axes_ref, pins_ref, lanes, None)
     for component in range(3):
         for side, end in enumerate((0, -1)):
-            at = row_window(2 * component + side, values, units, tile, tiles, rows)
-            out_ref[at, :] = solved[component][end]
+            value = 2 * component + side
+            for source, target in pieces(value, values, units, tile, rows):
+                out_ref[target, :] = solved[component][end][source]
 
 
 def coupling_kernel(line, units, axes_ref, out_ref):
@@ -205,7 +208,8 @@
     for tile in range(tiles):
         found = couplings(line, axes_ref, slice(tile * LANES, (tile + 1) * LANES))
         for value, one in enumerate(found):
-            out_ref[row_window(value, COUPLED - RHS, units, tile, tiles, rows), :] = one
+            for source, target in pieces(value, COUPLED - RHS, units, tile, rows):
+                out_ref[target, :] = one[source]
 
 
 def first_kernel(line, groups, units, coupling_ref, field_ref, axes_ref, pins_ref, out_ref):
@@ -218,40 +222,130 @@
         send_tile(line, units, COUPLED, field, axes_ref, pins_ref, out_ref, tile)
 
 
-def reduced_kernel(levels, groups, units, rhs_values, rhs_ref, coupling_ref, out_ref):
+def solve_children(level, levels, rhs, coupling, outer):
+    def ghosts(ends, component):
+        found = settle(levels, ends)
+        if outer is None:
+            return found
+        low, high = outer[component]
+        moved = []
+        for ghost, passed in zip(found, level.passed):
+            terms = combine(passed, [low, high])
+            moved.append(terms if ghost is None else ghost if terms is None else ghost + terms)
+        return moved
+
+    first = ghosts(rhs[0], 0)
+    middle = []
+    for d in range(level.radix):
+        c, low, high = coupling[d], first[2 * d], first[2 * d + 1]
+        middle.append(plus(plus(rhs[1][2 * d], c[0], low), c[1], high))
+        middle.append(plus(plus(rhs[1][2 * d + 1], c[1], low), c[2], high))
+    second = ghosts(middle, 1)
+    last = []
+    for d in range(level.radix):
+        c, low1, high1 = coupling[d], first[2 * d], first[2 * d + 1]
+        low2, high2 = second[2 * d], second[2 * d + 1]
+        total = plus(plus(rhs[2][2 * d], c[3], low2), c[4], high2)
+        last.append(plus(plus(total, c[6], low1), c[8], high1))
+        total = plus(plus(rhs[2][2 * d + 1], c[4], low2), c[5], high2)
+        last.append(plus(plus(total, c[7], low1), c[9], high1))
+    return (first, second, ghosts(last, 2)), (rhs[0], middle, last)
+
+
+def merged_coupling(level, levels, coupling):
+    radix = level.radix
+    from_first, from_second, across = [], [], []
+    for side in range(2):
+        passed = level.passed[:, side]
+        moved2, moved3 = [], []
+        for r in range(radix):
+            c, low, high = coupling[r], float(passed[2 * r]), float(passed[2 * r + 1])
+            moved2 += [c[0] * low + c[1] * high, c[1] * low + c[2] * high]
+            moved3 += [c[3] * low + c[4] * high, c[4] * low + c[5] * high]
+        inner = settle(levels, moved2)
+        through = []
+        for r in range(radix):
+            c, low, high = coupling[r], float(passed[2 * r]), float(passed[2 * r + 1])
+            k_low, k_high = inner[2 * r], inner[2 * r + 1]
+            total = plus(c[6] * low + c[8] * high, c[3], k_low)
+            through.append(plus(total, c[4], k_high))
+            total = plus(c[7] * low + c[9] * high, c[4], k_low)
+            through.append(plus(total, c[5], k_high))
+        for end in range(2):
+            if side <= end:
+                from_first.append(combine(level.ends[end], moved2))
+                from_second.append(combine(level.ends[end], moved3))
+            across.append(combine(level.ends[end], through))
+    return from_first + from_second + across
+
+
+def read_children(level, units, rhs_values, rhs_ref, coupling_ref):
     def read(ref, values, d, value):
         start = (d * values + value) * units
         return ref[start : start + units, :]
 
     rhs = [
-        [read(rhs_ref, rhs_values, k // 2, 2 * c + k % 2) for k in range(2 * groups)]
+        [read(rhs_ref, rhs_values, k // 2, 2 * c + k % 2) for k in range(2 * level.radix)]
         for c in range(3)
     ]
-
-    def coupling(d, value):
-        return read(coupling_ref, COUPLED, d, RHS + value)
-
-    first = settle(levels, rhs[0])
-    for d in range(groups):
-        low, high = first[2 * d], first[2 * d + 1]
-        mixed = coupling(d, 1)
-        rhs[1][2 * d] = plus(plus(rhs[1][2 * d], coupling(d, 0), low), mixed, high)
-        rhs[1][2 * d + 1] = plus(plus(rhs[1][2 * d + 1], mixed, low), coupling(d, 2), high)
-    second = settle(levels, rhs[1])
-    for d in range(groups):
-        low1, high1 = first[2 * d], first[2 * d + 1]
-        low2, high2 = second[2 * d], second[2 * d + 1]
-        mixed = coupling(d, 4)
-        total = plus(plus(rhs[2][2 * d], coupling(d, 3), low2), mixed, high2)
-        rhs[2][2 * d] = plus(plus(total, coupling(d, 6), low1), coupling(d, 8), high1)
-        total = plus(plus(rhs[2][2 * d + 1], mixed, low2), coupling(d, 5), high2)
-        rhs[2][2 * d + 1] = plus(plus(total, coupling(d, 7), low1), coupling(d, 9), high1)
-    third = settle(levels, rhs[2])
-    for c, ghosts in enumerate((first, second, third)):
+    coupling = [
+        [read(coupling_ref, COUPLED, d, v) for v in range(RHS, COUPLED)]
+        for d in range(level.radix)
+    ]
+    return rhs, coupling
+
+
+def join_kernel(level, levels, units, coupled, rhs_ref, coupling_ref, out_ref):
+    values = COUPLED if coupled else RHS
+    rhs, coupling = read_children(level, units, values, rhs_ref, coupling_ref)
+    _, seen = solve_children(level, levels, rhs, coupling, None)
+    joined = [combine(weights, seen[c]) for c in range(3) for weights in level.ends]
+    if coupled:
+        joined += merged_coupling(level, levels, coupling)
+    for value, one in enumerate(joined):
+        out_ref[value * units : (value + 1) * units, :] = one
+
+
+def part_kernel(
+    level,
+    levels,
+    pair,
+    units,
+    coupled,
+    own_ref,
+    other_ref,
+    own_coupling_ref,
+    other_coupling_ref,
+    rhs_ref,
+    coupling_ref,
+    out_ref,
+):
+    upper = lax.axis_index("gx") >= level.radix
+
+    def halves(own, other, value):
+        at = slice(value * units, (value + 1) * units)
+        mine, theirs = own[at, :], other[at, :]
+        return jnp.where(upper, theirs, mine), jnp.where(upper, mine, theirs)
+
+    both = [halves(own_ref, other_ref, v) for v in range(RHS)]
+    ends = [
+        [both[2 * c + side][half] for half in range(2) for side in range(2)] for c in range(3)
+    ]
+    across = [halves(own_coupling_ref, other_coupling_ref, v) for v in range(RHS, COUPLED)]
+    found, _ = solve_children(
+        pair, [pair], ends, [[one[half] for one in across] for half in range(2)], None
+    )
+    outer = []
+    zero = jnp.zeros((units, LANES), jnp.float32)
+    for ghosts in found:
+        ghosts = [zero if ghost is None else ghost for ghost in ghosts]
+        outer.append([jnp.where(upper, ghosts[2 + side], ghosts[side]) for side in range(2)])
+    values = COUPLED if coupled else RHS
+    rhs, coupling = read_children(level, units, values, rhs_ref, coupling_ref)
+    found, _ = solve_children(level, levels, rhs, coupling, outer)
+    for c, ghosts in enumerate(found):
         for k, ghost in enumerate(ghosts):
             start = (k // 2 * RHS + 2 * c + k % 2) * units
-            if ghost is None:
-                ghost = jnp.zeros((units, LANES), jnp.float32)
             out_ref[start : start + units, :] = ghost
 
 
@@ -263,7 +357,13 @@
         lanes = slice(tile * LANES, (tile + 1) * LANES)
         ghosts = [
             [
-                ghost_ref[row_window(2 * c + side, RHS, units, tile, tiles, rows), :]
+                jnp.concatenate(
+                    [
+                        ghost_ref[target, :]
+                        for _, target in pieces(2 * c + side, RHS, units, tile, rows)
+                    ],
+                    axis=0,
+                )
                 for side in range(2)
             ]
             for c in range(3)
@@ -394,9 +494,17 @@
 
 def exchange(block, groups):
     parts = block.reshape(groups, -1, LANES)
-    return lax.all_to_all(parts, "gx", split_axis=0, concat_axis=0, tiled=True).reshape(
-        block.shape
-    )
+    members = [
+        list(range(start, start + groups)) for start in range(0, lax.axis_size("gx"), groups)
+    ]
+    return lax.all_to_all(
+        parts, "gx", split_axis=0, concat_axis=0, axis_index_groups=members, tiled=True
+    ).reshape(block.shape)
+
+
+def swap_halves(block, groups):
+    pairs = [(i, (i + groups) % (2 * groups)) for i in range(2 * groups)]
+    return lax.ppermute(block, "gx", pairs)
 
 
 def from_neighbours(edges):
@@ -412,11 +520,11 @@
 
 def per_device(magnetization, easy_axes, pins):
     _, planes, rows, width = magnetization.shape
-    groups = lax.axis_size("gx")
-    tiles = width // LANES
-    units = rows * tiles // groups
+    groups = lax.axis_size("gx") // 2
+    units = rows * (width // LANES) // groups
     line = Line(planes)
     levels = make_levels(planes, groups)
+    level, pair = Level(planes, groups), Level(planes * groups, 2)
     whole = magnetization.shape
     sent_shape = (groups * RHS * units, LANES)
     edge_shape = (2, 3 * planes, width)
@@ -438,11 +546,24 @@
     coupling = None
     for stepno in range(STEPS):
         gathered = exchange(sent, groups)
-        if stepno == 0:
+        coupled = stepno == 0
+        if coupled:
             coupling = gathered
+        (joined,) = call(
+            functools.partial(join_kernel, level, levels, units, coupled),
+            [((COUPLED if coupled else RHS) * units, LANES)],
+            gathered,
+            coupling,
+        )
+        swapped = swap_halves(joined, groups)
+        if coupled:
+            across = (joined, swapped)
         (ghosts,) = call(
-            functools.partial(reduced_kernel, levels, groups, units, RHS if stepno else COUPLED),
+            functools.partial(part_kernel, level, levels, pair, units, coupled),
             [sent_shape],
+            joined,
+            swapped,
+            *across,
             gathered,
             coupling,
         )

time: 71.5 us -> 65.2 us (0.912)
  blocking collectives: 53.7 us -> 36.9 us
  starting transfers between devices: 5.65 us -> 12.9 us
  waiting for transfers between devices: 0.01 us -> 3.4 us
    all_to_all x4, blocking collectives: 53.7 us -> 36.9 us  [exchange(): lax.all_to_all(parts, 'gx', split_axis=0, concat_axis=0, axis_index_group...]
    ppermute x0 -> x2, starting transfers between devices: none -> 4.33 us  [swap_halves(): return lax.ppermute(block, 'gx', pairs)]
    ppermute x0 -> x2, waiting for transfers between devices: none -> 3.39 us  [swap_halves(): return lax.ppermute(block, 'gx', pairs)]
    ppermute x2, starting transfers between devices: 5.65 us -> 8.53 us  [from_neighbours(): return lax.ppermute(edges, 'gy', forward)]
    pallas_call x10 -> x12, Pallas kernels: 9.88 us -> 9.77 us  [call(): pl.pallas_call(kernel, out_shape=tuple(shapes), in_specs=[VMEM] * len(ope...]
  transfers between devices with their start and end apart: 2 -> 4, of which waited for: 0 -> 2; matrix products, arithmetic and copies ran while one was open for 0% -> 0% of each run, Pallas kernels for 4% -> 4%
where the time goes in v7:
time: 65.2 us; the launch traced here: 64.9 us
  blocking collectives  36.9 us (57%)
  starting transfers between devices  12.9 us (20%)
  Pallas kernels  9.77 us (15%)
  waiting for transfers between devices  3.4 us (5%)
  local copies, waits for them, and re-layouts  1.92 us (3%)
    all_to_all x4, blocking collectives, exchange(): lax.all_to_all(parts, 'gx', split_axis=0, concat_axis=0, axis_index_group...  36.9 us
    pallas_call x12, Pallas kernels, call(): pl.pallas_call(kernel, out_shape=tuple(shapes), in_specs=[VMEM] * len(ope...  9.77 us
    ppermute x2, starting transfers between devices, from_neighbours(): return lax.ppermute(edges, 'gy', forward)  8.53 us
    ppermute x2, starting transfers between devices, swap_halves(): return lax.ppermute(block, 'gx', pairs)  4.33 us
    ppermute x2, waiting for transfers between devices, swap_halves(): return lax.ppermute(block, 'gx', pairs)  3.39 us
    unnamed x8, local copies, waits for them, and re-layouts  1.92 us
  transfers between devices with their start and end apart: 4, of which 2 were waited for; matrix products, arithmetic and copies ran while one was open for 0% of the time, Pallas kernels for 4%

profile of v7, /device:TPU:1, one launch (start us, length us, event | category | flops | bytes accessed | tf_op | source)
XLA Modules:
  0.0 64.9 jit_solution(5726098630829269303)
XLA Ops:
  0.0 1.4 %copy-done = f32[3,16,16,512]{3,2,1,0:T(8,128)S(1)} copy-done((f32[3,16,16,512]{3,2,1,0:T(8,128)S(1)}, f32[3,16,16,512]{3,2,1,0:T(8,128)}, u32[]{:S(2)}) %copy-start) | copy-done | bytes 1572888
  1.4 0.9 %shard_map.37.coupling_ref = f32[640,128]{1,0:T(8,128)S(1)} custom-call(f32[3,16,16,512]{3,2,1,0:T(8,128)S(1)} %copy-done), custom_call_target="tpu_custom_call" | custom-call | tf_op jit(solution)/shard_map/pallas_call | solution.py:485
  2.3 0.5 copy-done.2
  2.8 0.9 %shard_map.38 = f32[1024,128]{1,0:T(8,128)S(1)} custom-call(f32[640,128]{1,0:T(8,128)S(1)} %shard_map.37.coupling_ref, f32[3,16,16,512]{3,2,1,0:T(8,128)S(1)} %copy-done.2, f32[3,16,16,512]{3,2,1,0:T(8,128)S(1)} %copy-done, f32[2,3,16,512]{3,2,1,0:T(8,128)S(1)} %copy-done.3), custom_call_target="tpu_custom_call" | custom-call | tf_op jit(solution)/shard_map/pallas_call | solution.py:485
  3.7 13.2 %all_to_all.20 = f32[8,128,128]{2,1,0:T(8,128)S(1)} all-to-all(f32[8,128,128]{2,1,0:T(8,128)S(1)} %bitcast.14), channel_id=1, replica_groups={{0,2,4,6,8,10,12,14},{16,18,20,22,24,26,28,30},{1,3,5,7,9,11,13,15},{17..., dimensions={0} | all-to-all | bytes 1048576 | tf_op jit(solution)/shard_map/all_to_all | solution.py:500
  17.0 0.2 shard_map.39.own_ref.own_coupling_ref
  17.2 2.4 %collective-permute-start = (f32[128,128]{1,0:T(8,128)S(1)}, f32[128,128]{1,0:T(8,128)S(1)}, u32[]{:S(2)}, u32[]{:S(2)}) collective-permute-start(f32[128,128]{1,0:T(8,128)S(1)} %shard_map.39.own_ref.own_coupling_ref), channel_id=1, source_target_pairs={{0,16},{2,18},{4,20},{6,22},{8,24},{10,26},{12,28},{14,30},{16,0},... | collective-permute-start | bytes 196616 | tf_op jit(solution)/shard_map/ppermute | solution.py:507
  19.6 1.7 %collective-permute-done.other_ref.other_coupling_ref = f32[128,128]{1,0:T(8,128)S(1)} collective-permute-done((f32[128,128]{1,0:T(8,128)S(1)}, f32[128,128]{1,0:T(8,128)S(1)}, u32[]{:S(2)}, u32[]{:S(2)}) %collective-permute-start) | collective-permute-done | bytes 65568 | tf_op jit(solution)/shard_map/ppermute | solution.py:507
  21.3 0.1 shard_map.40
  21.4 8.0 %all_to_all.21 = f32[8,48,128]{2,1,0:T(8,128)S(1)} all-to-all(f32[8,48,128]{2,1,0:T(8,128)S(1)} %bitcast.20), channel_id=1, replica_groups={{0,2,4,6,8,10,12,14},{16,18,20,22,24,26,28,30},{1,3,5,7,9,11,13,15},{17..., dimensions={0} | all-to-all | bytes 393216 | tf_op jit(solution)/shard_map/all_to_all | solution.py:500
  29.4 0.9 %shard_map.41 = (f32[3,16,16,512]{3,2,1,0:T(8,128)S(1)}, f32[2,48,512]{2,1,0:T(8,128)S(1)}) custom-call(f32[3,16,16,512]{3,2,1,0:T(8,128)S(1)} %copy-done.2, f32[3,16,16,512]{3,2,1,0:T(8,128)S(1)} %copy-done.1, f32[2,3,16,512]{3,2,1,0:T(8,128)S(1)} %copy-done.3, f32[384,128]{1,0:T(8,128)S(1)} %bitcast.18), custom_call_target="tpu_custom_call" | custom-call | tf_op jit(solution)/shard_map/pallas_call | solution.py:485
  30.3 4.9 %collective-permute-start.1 = (f32[2,48,512]{2,1,0:T(8,128)S(1)}, f32[2,48,512]{2,1,0:T(8,128)S(1)}, u32[]{:S(2)}, u32[]{:S(2)}) collective-permute-start(f32[2,48,512]{2,1,0:T(8,128)S(1)} %get-tuple-element.17.edge_ref), channel_id=1, source_target_pairs={{0,1},{1,0},{2,3},{3,2},{4,5},{5,4},{6,7},{7,6},{8,9},{9,8},{10,11... | collective-permute-start | bytes 589832 | tf_op jit(solution)/shard_map/ppermute | solution.py:514
  35.2 1.4 %shard_map.42 = (f32[3,16,16,512]{3,2,1,0:T(8,128)S(1)}, f32[2,48,512]{2,1,0:T(8,128)S(1)}) custom-call(f32[3,16,16,512]{3,2,1,0:T(8,128)S(1)} %get-tuple-element.15.field_ref, f32[3,16,16,512]{3,2,1,0:T(8,128)S(1)} %copy-done.1), custom_call_target="tpu_custom_call" | custom-call | tf_op jit(solution)/shard_map/pallas_call | solution.py:485
  36.7 1.3 %shard_map.43 = (f32[3,16,16,512]{3,2,1,0:T(8,128)S(1)}, f32[384,128]{1,0:T(8,128)S(1)}) custom-call(f32[3,16,16,512]{3,2,1,0:T(8,128)S(1)} %get-tuple-element.16.turned_ref, f32[2,48,512]{2,1,0:T(8,128)S(1)} %get-tuple-element.17.edge_ref, f32[2,48,512]{2,1,0:T(8,128)S(1)} %get-tuple-element.18.raw_ref, ...), custom_call_target="tpu_custom_call" | custom-call | tf_op jit(solution)/shard_map/pallas_call | solution.py:485
  38.0 8.0 %all_to_all.22 = f32[8,48,128]{2,1,0:T(8,128)S(1)} all-to-all(f32[8,48,128]{2,1,0:T(8,128)S(1)} %bitcast.21), channel_id=1, replica_groups={{0,2,4,6,8,10,12,14},{16,18,20,22,24,26,28,30},{1,3,5,7,9,11,13,15},{17..., dimensions={0} | all-to-all | bytes 393216 | tf_op jit(solution)/shard_map/all_to_all | solution.py:500
  46.0 0.1 shard_map.44.own_ref
  46.1 2.0 %collective-permute-start.2 = (f32[48,128]{1,0:T(8,128)S(1)}, f32[48,128]{1,0:T(8,128)S(1)}, u32[]{:S(2)}, u32[]{:S(2)}) collective-permute-start(f32[48,128]{1,0:T(8,128)S(1)} %shard_map.44.own_ref), channel_id=1, source_target_pairs={{0,16},{2,18},{4,20},{6,22},{8,24},{10,26},{12,28},{14,30},{16,0},... | collective-permute-start | bytes 73736 | tf_op jit(solution)/shard_map/ppermute | solution.py:507
  48.0 1.7 %collective-permute-done.2.other_ref = f32[48,128]{1,0:T(8,128)S(1)} collective-permute-done((f32[48,128]{1,0:T(8,128)S(1)}, f32[48,128]{1,0:T(8,128)S(1)}, u32[]{:S(2)}, u32[]{:S(2)}) %collective-permute-start.2) | collective-permute-done | bytes 24608 | tf_op jit(solution)/shard_map/ppermute | solution.py:507
  49.7 0.1 shard_map.45
  49.9 7.7 %all_to_all.23 = f32[8,48,128]{2,1,0:T(8,128)S(1)} all-to-all(f32[8,48,128]{2,1,0:T(8,128)S(1)} %bitcast.19), channel_id=1, replica_groups={{0,2,4,6,8,10,12,14},{16,18,20,22,24,26,28,30},{1,3,5,7,9,11,13,15},{17..., dimensions={0} | all-to-all | bytes 393216 | tf_op jit(solution)/shard_map/all_to_all | solution.py:500
  57.6 0.9 %shard_map.46 = (f32[3,16,16,512]{3,2,1,0:T(8,128)S(1)}, f32[2,48,512]{2,1,0:T(8,128)S(1)}) custom-call(f32[3,16,16,512]{3,2,1,0:T(8,128)S(1)} %get-tuple-element.19.field_ref, f32[3,16,16,512]{3,2,1,0:T(8,128)S(1)} %copy-done.1, f32[2,3,16,512]{3,2,1,0:T(8,128)S(1)} %copy-done.3, f32[384,128]{1,0:T(8,128)S(1)} %bitcast.17), custom_call_target="tpu_custom_call" | custom-call | tf_op jit(solution)/shard_map/pallas_call | solution.py:485
  58.5 3.6 %collective-permute-start.3 = (f32[2,48,512]{2,1,0:T(8,128)S(1)}, f32[2,48,512]{2,1,0:T(8,128)S(1)}, u32[]{:S(2)}, u32[]{:S(2)}) collective-permute-start(f32[2,48,512]{2,1,0:T(8,128)S(1)} %get-tuple-element.23.edge_ref), channel_id=1, source_target_pairs={{0,1},{1,0},{2,3},{3,2},{4,5},{5,4},{6,7},{7,6},{8,9},{9,8},{10,11... | collective-permute-start | bytes 589832 | tf_op jit(solution)/shard_map/ppermute | solution.py:514
  62.1 1.4 %shard_map.47 = (f32[3,16,16,512]{3,2,1,0:T(8,128)S(1)}, f32[2,48,512]{2,1,0:T(8,128)S(1)}) custom-call(f32[3,16,16,512]{3,2,1,0:T(8,128)S(1)} %get-tuple-element.21.field_ref, f32[3,16,16,512]{3,2,1,0:T(8,128)S(1)} %copy-done.1), custom_call_target="tpu_custom_call" | custom-call | tf_op jit(solution)/shard_map/pallas_call | solution.py:485
  63.6 1.3 %shard_map.48 = f32[3,16,16,512]{3,2,1,0:T(8,128)} custom-call(f32[3,16,16,512]{3,2,1,0:T(8,128)S(1)} %get-tuple-element.22.turned_ref, f32[2,48,512]{2,1,0:T(8,128)S(1)} %get-tuple-element.23.edge_ref, f32[2,48,512]{2,1,0:T(8,128)S(1)} %get-tuple-element.24.raw_ref, f32[2,48,512]{2,1,0:T(8,128)S(1)} %collective-permute-done.3.beyond_ref), custom_call_target="tpu_custom_call" | custom-call | tf_op jit(solution)/shard_map/pallas_call | solution.py:485
  (8 shorter events, 0.0 us)
Async XLA Ops:
  0.0 1.4 %copy-start = (f32[3,16,16,512]{3,2,1,0:T(8,128)S(1)}, f32[3,16,16,512]{3,2,1,0:T(8,128)}, u32[]{:S(2)}) copy-start(f32[3,16,16,512]{3,2,1,0:T(8,128)} %axes_ref.13) | copy-start | bytes 4718596
  1.4 1.4 %copy-start.2 = (f32[3,16,16,512]{3,2,1,0:T(8,128)S(1)}, f32[3,16,16,512]{3,2,1,0:T(8,128)}, u32[]{:S(2)}) copy-start(f32[3,16,16,512]{3,2,1,0:T(8,128)} %field_ref.3) | copy-start | bytes 4718596
  1.4 1.4 %copy-start.3 = (f32[2,3,16,512]{3,2,1,0:T(8,128)S(1)}, f32[2,3,16,512]{3,2,1,0:T(8,128)}, u32[]{:S(2)}) copy-start(f32[2,3,16,512]{3,2,1,0:T(8,128)} %pins_ref.7) | copy-start | bytes 589828
  17.0 12.4 %copy-start.1 = (f32[3,16,16,512]{3,2,1,0:T(8,128)S(1)}, f32[3,16,16,512]{3,2,1,0:T(8,128)}, u32[]{:S(2)}) copy-start(f32[3,16,16,512]{3,2,1,0:T(8,128)} %axes_ref.13) | copy-start | bytes 4718596
  17.2 4.1 %collective-permute-start = (f32[128,128]{1,0:T(8,128)S(1)}, f32[128,128]{1,0:T(8,128)S(1)}, u32[]{:S(2)}, u32[]{:S(2)}) collective-permute-start(f32[128,128]{1,0:T(8,128)S(1)} %shard_map.39.own_ref.own_coupling_ref), channel_id=1, source_target_pairs={{0,16},{2,18},{4,20},{6,22},{8,24},{10,26},{12,28},{14,30},{16,0},... | collective-permute-start | bytes 196616 | tf_op jit(solution)/shard_map/ppermute | solution.py:507
  30.3 6.4 %collective-permute-start.1 = (f32[2,48,512]{2,1,0:T(8,128)S(1)}, f32[2,48,512]{2,1,0:T(8,128)S(1)}, u32[]{:S(2)}, u32[]{:S(2)}) collective-permute-start(f32[2,48,512]{2,1,0:T(8,128)S(1)} %get-tuple-element.17.edge_ref), channel_id=1, source_target_pairs={{0,1},{1,0},{2,3},{3,2},{4,5},{5,4},{6,7},{7,6},{8,9},{9,8},{10,11... | collective-permute-start | bytes 589832 | tf_op jit(solution)/shard_map/ppermute | solution.py:514
  46.1 3.6 %collective-permute-start.2 = (f32[48,128]{1,0:T(8,128)S(1)}, f32[48,128]{1,0:T(8,128)S(1)}, u32[]{:S(2)}, u32[]{:S(2)}) collective-permute-start(f32[48,128]{1,0:T(8,128)S(1)} %shard_map.44.own_ref), channel_id=1, source_target_pairs={{0,16},{2,18},{4,20},{6,22},{8,24},{10,26},{12,28},{14,30},{16,0},... | collective-permute-start | bytes 73736 | tf_op jit(solution)/shard_map/ppermute | solution.py:507
  58.5 5.1 %collective-permute-start.3 = (f32[2,48,512]{2,1,0:T(8,128)S(1)}, f32[2,48,512]{2,1,0:T(8,128)S(1)}, u32[]{:S(2)}, u32[]{:S(2)}) collective-permute-start(f32[2,48,512]{2,1,0:T(8,128)S(1)} %get-tuple-element.23.edge_ref), channel_id=1, source_target_pairs={{0,1},{1,0},{2,3},{3,2},{4,5},{5,4},{6,7},{7,6},{8,9},{9,8},{10,11... | collective-permute-start | bytes 589832 | tf_op jit(solution)/shard_map/ppermute | solution.py:514

commit v8 on v7

--- a/solution.py
+++ b/solution.py
@@ -252,31 +252,23 @@
     return (first, second, ghosts(last, 2)), (rhs[0], middle, last)
 
 
-def merged_coupling(level, levels, coupling):
-    radix = level.radix
-    from_first, from_second, across = [], [], []
-    for side in range(2):
-        passed = level.passed[:, side]
-        moved2, moved3 = [], []
-        for r in range(radix):
-            c, low, high = coupling[r], float(passed[2 * r]), float(passed[2 * r + 1])
-            moved2 += [c[0] * low + c[1] * high, c[1] * low + c[2] * high]
-            moved3 += [c[3] * low + c[4] * high, c[4] * low + c[5] * high]
-        inner = settle(levels, moved2)
-        through = []
-        for r in range(radix):
-            c, low, high = coupling[r], float(passed[2 * r]), float(passed[2 * r + 1])
-            k_low, k_high = inner[2 * r], inner[2 * r + 1]
-            total = plus(c[6] * low + c[8] * high, c[3], k_low)
-            through.append(plus(total, c[4], k_high))
-            total = plus(c[7] * low + c[9] * high, c[4], k_low)
-            through.append(plus(total, c[5], k_high))
-        for end in range(2):
-            if side <= end:
-                from_first.append(combine(level.ends[end], moved2))
-                from_second.append(combine(level.ends[end], moved3))
-            across.append(combine(level.ends[end], through))
-    return from_first + from_second + across
+def facing_coupling(level, levels, coupling, side):
+    passed = level.passed[:, side]
+    moved2, moved3 = [], []
+    for r in range(level.radix):
+        c, low, high = coupling[r], float(passed[2 * r]), float(passed[2 * r + 1])
+        moved2 += [c[0] * low + c[1] * high, c[1] * low + c[2] * high]
+        moved3 += [c[3] * low + c[4] * high, c[4] * low + c[5] * high]
+    inner = settle(levels, moved2)
+    through = []
+    for r in range(level.radix):
+        c, low, high = coupling[r], float(passed[2 * r]), float(passed[2 * r + 1])
+        k_low, k_high = inner[2 * r], inner[2 * r + 1]
+        total = plus(c[6] * low + c[8] * high, c[3], k_low)
+        through.append(plus(total, c[4], k_high))
+        total = plus(c[7] * low + c[9] * high, c[4], k_low)
+        through.append(plus(total, c[5], k_high))
+    return [combine(level.ends[side], moved) for moved in (moved2, moved3, through)]
 
 
 def read_children(level, units, rhs_values, rhs_ref, coupling_ref):
@@ -296,20 +288,22 @@
 
 
 def join_kernel(level, levels, units, coupled, rhs_ref, coupling_ref, out_ref):
+    upper = lax.axis_index("gx") >= level.radix
     values = COUPLED if coupled else RHS
     rhs, coupling = read_children(level, units, values, rhs_ref, coupling_ref)
     _, seen = solve_children(level, levels, rhs, coupling, None)
-    joined = [combine(weights, seen[c]) for c in range(3) for weights in level.ends]
+    ends = [[combine(level.ends[side], seen[c]) for c in range(3)] for side in range(2)]
     if coupled:
-        joined += merged_coupling(level, levels, coupling)
-    for value, one in enumerate(joined):
-        out_ref[value * units : (value + 1) * units, :] = one
+        for side in range(2):
+            ends[side] += facing_coupling(level, levels, coupling, side)
+    for value, (first, last) in enumerate(zip(*ends)):
+        out_ref[value * units : (value + 1) * units, :] = jnp.where(upper, first, last)
 
 
 def part_kernel(
     level,
     levels,
-    pair,
+    near,
     units,
     coupled,
     own_ref,
@@ -322,24 +316,29 @@
 ):
     upper = lax.axis_index("gx") >= level.radix
 
-    def halves(own, other, value):
-        at = slice(value * units, (value + 1) * units)
-        mine, theirs = own[at, :], other[at, :]
-        return jnp.where(upper, theirs, mine), jnp.where(upper, mine, theirs)
-
-    both = [halves(own_ref, other_ref, v) for v in range(RHS)]
-    ends = [
-        [both[2 * c + side][half] for half in range(2) for side in range(2)] for c in range(3)
+    def read(ref, value):
+        return ref[value * units : (value + 1) * units, :]
+
+    settled = 1.0 / (1.0 - near * near)
+
+    def meet(own, other):
+        beyond = other * settled + own * (near * settled)
+        return beyond, own * settled + other * (near * settled)
+
+    own = [read(own_ref, c) for c in range(3)]
+    other = [read(other_ref, c) for c in range(3)]
+    own_c = [read(own_coupling_ref, 3 + v) for v in range(3)]
+    other_c = [read(other_coupling_ref, 3 + v) for v in range(3)]
+    beyond1, back1 = meet(own[0], other[0])
+    beyond2, back2 = meet(own[1] + own_c[0] * beyond1, other[1] + other_c[0] * back1)
+    beyond3, _ = meet(
+        own[2] + own_c[1] * beyond2 + own_c[2] * beyond1,
+        other[2] + other_c[1] * back2 + other_c[2] * back1,
+    )
+    outer = [
+        [jnp.where(upper, beyond, 0.0), jnp.where(upper, 0.0, beyond)]
+        for beyond in (beyond1, beyond2, beyond3)
     ]
-    across = [halves(own_coupling_ref, other_coupling_ref, v) for v in range(RHS, COUPLED)]
-    found, _ = solve_children(
-        pair, [pair], ends, [[one[half] for one in across] for half in range(2)], None
-    )
-    outer = []
-    zero = jnp.zeros((units, LANES), jnp.float32)
-    for ghosts in found:
-        ghosts = [zero if ghost is None else ghost for ghost in ghosts]
-        outer.append([jnp.where(upper, ghosts[2 + side], ghosts[side]) for side in range(2)])
     values = COUPLED if coupled else RHS
     rhs, coupling = read_children(level, units, values, rhs_ref, coupling_ref)
     found, _ = solve_children(level, levels, rhs, coupling, outer)
@@ -524,7 +523,8 @@
     units = rows * (width // LANES) // groups
     line = Line(planes)
     levels = make_levels(planes, groups)
-    level, pair = Level(planes, groups), Level(planes * groups, 2)
+    level = Level(planes, groups)
+    near = float(Line(planes * groups).from_low[0])
     whole = magnetization.shape
     sent_shape = (groups * RHS * units, LANES)
     edge_shape = (2, 3 * planes, width)
@@ -551,7 +551,7 @@
             coupling = gathered
         (joined,) = call(
             functools.partial(join_kernel, level, levels, units, coupled),
-            [((COUPLED if coupled else RHS) * units, LANES)],
+            [((6 if coupled else 3) * units, LANES)],
             gathered,
             coupling,
         )
@@ -559,7 +559,7 @@
         if coupled:
             across = (joined, swapped)
         (ghosts,) = call(
-            functools.partial(part_kernel, level, levels, pair, units, coupled),
+            functools.partial(part_kernel, level, levels, near, units, coupled),
             [sent_shape],
             joined,
             swapped,

time: 65.2 us -> 64 us (0.982)
  waiting for transfers between devices: 3.4 us -> 2.41 us
    ppermute x2, waiting for transfers between devices: 3.39 us -> 2.4 us  [swap_halves(): return lax.ppermute(block, 'gx', pairs)]
  transfers between devices with their start and end apart: 4 -> 4, of which waited for: 2 -> 2; matrix products, arithmetic and copies ran while one was open for 0% -> 0% of each run, Pallas kernels for 4% -> 5%
where the time goes in v8:
time: 64 us; the launch traced here: 63.7 us
  blocking collectives  36.6 us (57%)
  starting transfers between devices  12.9 us (20%)
  Pallas kernels  9.81 us (15%)
  waiting for transfers between devices  2.41 us (4%)
  local copies, waits for them, and re-layouts  1.92 us (3%)
    all_to_all x4, blocking collectives, exchange(): lax.all_to_all(parts, 'gx', split_axis=0, concat_axis=0, axis_index_group...  36.6 us
    pallas_call x12, Pallas kernels, call(): pl.pallas_call(kernel, out_shape=tuple(shapes), in_specs=[VMEM] * len(ope...  9.81 us
    ppermute x2, starting transfers between devices, from_neighbours(): return lax.ppermute(edges, 'gy', forward)  8.18 us
    ppermute x2, starting transfers between devices, swap_halves(): return lax.ppermute(block, 'gx', pairs)  4.75 us
    ppermute x2, waiting for transfers between devices, swap_halves(): return lax.ppermute(block, 'gx', pairs)  2.4 us
    unnamed x8, local copies, waits for them, and re-layouts  1.92 us
  transfers between devices with their start and end apart: 4, of which 2 were waited for; matrix products, arithmetic and copies ran while one was open for 0% of the time, Pallas kernels for 5%

profile of v8, /device:TPU:1, one launch (start us, length us, event | category | flops | bytes accessed | tf_op | source)
XLA Modules:
  0.0 63.7 jit_solution(792291186873997588)
XLA Ops:
  0.0 1.4 %copy-done = f32[3,16,16,512]{3,2,1,0:T(8,128)S(1)} copy-done((f32[3,16,16,512]{3,2,1,0:T(8,128)S(1)}, f32[3,16,16,512]{3,2,1,0:T(8,128)}, u32[]{:S(2)}) %copy-start) | copy-done | bytes 1572888
  1.4 0.9 %shard_map.37.coupling_ref = f32[640,128]{1,0:T(8,128)S(1)} custom-call(f32[3,16,16,512]{3,2,1,0:T(8,128)S(1)} %copy-done), custom_call_target="tpu_custom_call" | custom-call | tf_op jit(solution)/shard_map/pallas_call | solution.py:484
  2.3 0.5 copy-done.2
  2.8 0.9 %shard_map.38 = f32[1024,128]{1,0:T(8,128)S(1)} custom-call(f32[640,128]{1,0:T(8,128)S(1)} %shard_map.37.coupling_ref, f32[3,16,16,512]{3,2,1,0:T(8,128)S(1)} %copy-done.2, f32[3,16,16,512]{3,2,1,0:T(8,128)S(1)} %copy-done, f32[2,3,16,512]{3,2,1,0:T(8,128)S(1)} %copy-done.3), custom_call_target="tpu_custom_call" | custom-call | tf_op jit(solution)/shard_map/pallas_call | solution.py:484
  3.7 13.2 %all_to_all.20 = f32[8,128,128]{2,1,0:T(8,128)S(1)} all-to-all(f32[8,128,128]{2,1,0:T(8,128)S(1)} %bitcast.14), channel_id=1, replica_groups={{0,2,4,6,8,10,12,14},{16,18,20,22,24,26,28,30},{1,3,5,7,9,11,13,15},{17..., dimensions={0} | all-to-all | bytes 1048576 | tf_op jit(solution)/shard_map/all_to_all | solution.py:499
  17.0 0.2 shard_map.39.own_ref.own_coupling_ref
  17.2 2.4 %collective-permute-start = (f32[48,128]{1,0:T(8,128)S(1)}, f32[48,128]{1,0:T(8,128)S(1)}, u32[]{:S(2)}, u32[]{:S(2)}) collective-permute-start(f32[48,128]{1,0:T(8,128)S(1)} %shard_map.39.own_ref.own_coupling_ref), channel_id=1, source_target_pairs={{0,16},{2,18},{4,20},{6,22},{8,24},{10,26},{12,28},{14,30},{16,0},... | collective-permute-start | bytes 73736 | tf_op jit(solution)/shard_map/ppermute | solution.py:506
  19.6 1.3 %collective-permute-done.other_ref.other_coupling_ref = f32[48,128]{1,0:T(8,128)S(1)} collective-permute-done((f32[48,128]{1,0:T(8,128)S(1)}, f32[48,128]{1,0:T(8,128)S(1)}, u32[]{:S(2)}, u32[]{:S(2)}) %collective-permute-start) | collective-permute-done | bytes 24608 | tf_op jit(solution)/shard_map/ppermute | solution.py:506
  20.8 0.1 shard_map.40
  21.0 7.6 %all_to_all.21 = f32[8,48,128]{2,1,0:T(8,128)S(1)} all-to-all(f32[8,48,128]{2,1,0:T(8,128)S(1)} %bitcast.20), channel_id=1, replica_groups={{0,2,4,6,8,10,12,14},{16,18,20,22,24,26,28,30},{1,3,5,7,9,11,13,15},{17..., dimensions={0} | all-to-all | bytes 393216 | tf_op jit(solution)/shard_map/all_to_all | solution.py:499
  28.6 0.9 %shard_map.41 = (f32[3,16,16,512]{3,2,1,0:T(8,128)S(1)}, f32[2,48,512]{2,1,0:T(8,128)S(1)}) custom-call(f32[3,16,16,512]{3,2,1,0:T(8,128)S(1)} %copy-done.2, f32[3,16,16,512]{3,2,1,0:T(8,128)S(1)} %copy-done.1, f32[2,3,16,512]{3,2,1,0:T(8,128)S(1)} %copy-done.3, f32[384,128]{1,0:T(8,128)S(1)} %bitcast.18), custom_call_target="tpu_custom_call" | custom-call | tf_op jit(solution)/shard_map/pallas_call | solution.py:484
  29.5 4.6 %collective-permute-start.1 = (f32[2,48,512]{2,1,0:T(8,128)S(1)}, f32[2,48,512]{2,1,0:T(8,128)S(1)}, u32[]{:S(2)}, u32[]{:S(2)}) collective-permute-start(f32[2,48,512]{2,1,0:T(8,128)S(1)} %get-tuple-element.17.edge_ref), channel_id=1, source_target_pairs={{0,1},{1,0},{2,3},{3,2},{4,5},{5,4},{6,7},{7,6},{8,9},{9,8},{10,11... | collective-permute-start | bytes 589832 | tf_op jit(solution)/shard_map/ppermute | solution.py:513
  34.1 1.5 %shard_map.42 = (f32[3,16,16,512]{3,2,1,0:T(8,128)S(1)}, f32[2,48,512]{2,1,0:T(8,128)S(1)}) custom-call(f32[3,16,16,512]{3,2,1,0:T(8,128)S(1)} %get-tuple-element.15.field_ref, f32[3,16,16,512]{3,2,1,0:T(8,128)S(1)} %copy-done.1), custom_call_target="tpu_custom_call" | custom-call | tf_op jit(solution)/shard_map/pallas_call | solution.py:484
  35.6 1.3 %shard_map.43 = (f32[3,16,16,512]{3,2,1,0:T(8,128)S(1)}, f32[384,128]{1,0:T(8,128)S(1)}) custom-call(f32[3,16,16,512]{3,2,1,0:T(8,128)S(1)} %get-tuple-element.16.turned_ref, f32[2,48,512]{2,1,0:T(8,128)S(1)} %get-tuple-element.17.edge_ref, f32[2,48,512]{2,1,0:T(8,128)S(1)} %get-tuple-element.18.raw_ref, ...), custom_call_target="tpu_custom_call" | custom-call | tf_op jit(solution)/shard_map/pallas_call | solution.py:484
  36.9 8.0 %all_to_all.22 = f32[8,48,128]{2,1,0:T(8,128)S(1)} all-to-all(f32[8,48,128]{2,1,0:T(8,128)S(1)} %bitcast.21), channel_id=1, replica_groups={{0,2,4,6,8,10,12,14},{16,18,20,22,24,26,28,30},{1,3,5,7,9,11,13,15},{17..., dimensions={0} | all-to-all | bytes 393216 | tf_op jit(solution)/shard_map/all_to_all | solution.py:499
  44.9 0.1 shard_map.44.own_ref
  45.0 2.4 %collective-permute-start.2 = (f32[24,128]{1,0:T(8,128)S(1)}, f32[24,128]{1,0:T(8,128)S(1)}, u32[]{:S(2)}, u32[]{:S(2)}) collective-permute-start(f32[24,128]{1,0:T(8,128)S(1)} %shard_map.44.own_ref), channel_id=1, source_target_pairs={{0,16},{2,18},{4,20},{6,22},{8,24},{10,26},{12,28},{14,30},{16,0},... | collective-permute-start | bytes 36872 | tf_op jit(solution)/shard_map/ppermute | solution.py:506
  47.4 1.1 %collective-permute-done.2.other_ref = f32[24,128]{1,0:T(8,128)S(1)} collective-permute-done((f32[24,128]{1,0:T(8,128)S(1)}, f32[24,128]{1,0:T(8,128)S(1)}, u32[]{:S(2)}, u32[]{:S(2)}) %collective-permute-start.2) | collective-permute-done | bytes 12320 | tf_op jit(solution)/shard_map/ppermute | solution.py:506
  48.5 0.1 shard_map.45
  48.6 7.7 %all_to_all.23 = f32[8,48,128]{2,1,0:T(8,128)S(1)} all-to-all(f32[8,48,128]{2,1,0:T(8,128)S(1)} %bitcast.19), channel_id=1, replica_groups={{0,2,4,6,8,10,12,14},{16,18,20,22,24,26,28,30},{1,3,5,7,9,11,13,15},{17..., dimensions={0} | all-to-all | bytes 393216 | tf_op jit(solution)/shard_map/all_to_all | solution.py:499
  56.3 0.9 %shard_map.46 = (f32[3,16,16,512]{3,2,1,0:T(8,128)S(1)}, f32[2,48,512]{2,1,0:T(8,128)S(1)}) custom-call(f32[3,16,16,512]{3,2,1,0:T(8,128)S(1)} %get-tuple-element.19.field_ref, f32[3,16,16,512]{3,2,1,0:T(8,128)S(1)} %copy-done.1, f32[2,3,16,512]{3,2,1,0:T(8,128)S(1)} %copy-done.3, f32[384,128]{1,0:T(8,128)S(1)} %bitcast.17), custom_call_target="tpu_custom_call" | custom-call | tf_op jit(solution)/shard_map/pallas_call | solution.py:484
  57.3 3.6 %collective-permute-start.3 = (f32[2,48,512]{2,1,0:T(8,128)S(1)}, f32[2,48,512]{2,1,0:T(8,128)S(1)}, u32[]{:S(2)}, u32[]{:S(2)}) collective-permute-start(f32[2,48,512]{2,1,0:T(8,128)S(1)} %get-tuple-element.23.edge_ref), channel_id=1, source_target_pairs={{0,1},{1,0},{2,3},{3,2},{4,5},{5,4},{6,7},{7,6},{8,9},{9,8},{10,11... | collective-permute-start | bytes 589832 | tf_op jit(solution)/shard_map/ppermute | solution.py:513
  60.9 1.4 %shard_map.47 = (f32[3,16,16,512]{3,2,1,0:T(8,128)S(1)}, f32[2,48,512]{2,1,0:T(8,128)S(1)}) custom-call(f32[3,16,16,512]{3,2,1,0:T(8,128)S(1)} %get-tuple-element.21.field_ref, f32[3,16,16,512]{3,2,1,0:T(8,128)S(1)} %copy-done.1), custom_call_target="tpu_custom_call" | custom-call | tf_op jit(solution)/shard_map/pallas_call | solution.py:484
  62.3 1.3 %shard_map.48 = f32[3,16,16,512]{3,2,1,0:T(8,128)} custom-call(f32[3,16,16,512]{3,2,1,0:T(8,128)S(1)} %get-tuple-element.22.turned_ref, f32[2,48,512]{2,1,0:T(8,128)S(1)} %get-tuple-element.23.edge_ref, f32[2,48,512]{2,1,0:T(8,128)S(1)} %get-tuple-element.24.raw_ref, f32[2,48,512]{2,1,0:T(8,128)S(1)} %collective-permute-done.3.beyond_ref), custom_call_target="tpu_custom_call" | custom-call | tf_op jit(solution)/shard_map/pallas_call | solution.py:484
  (8 shorter events, 0.0 us)
Async XLA Ops:
  0.0 1.4 %copy-start = (f32[3,16,16,512]{3,2,1,0:T(8,128)S(1)}, f32[3,16,16,512]{3,2,1,0:T(8,128)}, u32[]{:S(2)}) copy-start(f32[3,16,16,512]{3,2,1,0:T(8,128)} %axes_ref.13) | copy-start | bytes 4718596
  1.4 1.4 %copy-start.2 = (f32[3,16,16,512]{3,2,1,0:T(8,128)S(1)}, f32[3,16,16,512]{3,2,1,0:T(8,128)}, u32[]{:S(2)}) copy-start(f32[3,16,16,512]{3,2,1,0:T(8,128)} %field_ref.3) | copy-start | bytes 4718596
  1.4 1.4 %copy-start.3 = (f32[2,3,16,512]{3,2,1,0:T(8,128)S(1)}, f32[2,3,16,512]{3,2,1,0:T(8,128)}, u32[]{:S(2)}) copy-start(f32[2,3,16,512]{3,2,1,0:T(8,128)} %pins_ref.7) | copy-start | bytes 589828
  17.0 11.6 %copy-start.1 = (f32[3,16,16,512]{3,2,1,0:T(8,128)S(1)}, f32[3,16,16,512]{3,2,1,0:T(8,128)}, u32[]{:S(2)}) copy-start(f32[3,16,16,512]{3,2,1,0:T(8,128)} %axes_ref.13) | copy-start | bytes 4718596
  17.2 3.6 %collective-permute-start = (f32[48,128]{1,0:T(8,128)S(1)}, f32[48,128]{1,0:T(8,128)S(1)}, u32[]{:S(2)}, u32[]{:S(2)}) collective-permute-start(f32[48,128]{1,0:T(8,128)S(1)} %shard_map.39.own_ref.own_coupling_ref), channel_id=1, source_target_pairs={{0,16},{2,18},{4,20},{6,22},{8,24},{10,26},{12,28},{14,30},{16,0},... | collective-permute-start | bytes 73736 | tf_op jit(solution)/shard_map/ppermute | solution.py:506
  29.5 6.1 %collective-permute-start.1 = (f32[2,48,512]{2,1,0:T(8,128)S(1)}, f32[2,48,512]{2,1,0:T(8,128)S(1)}, u32[]{:S(2)}, u32[]{:S(2)}) collective-permute-start(f32[2,48,512]{2,1,0:T(8,128)S(1)} %get-tuple-element.17.edge_ref), channel_id=1, source_target_pairs={{0,1},{1,0},{2,3},{3,2},{4,5},{5,4},{6,7},{7,6},{8,9},{9,8},{10,11... | collective-permute-start | bytes 589832 | tf_op jit(solution)/shard_map/ppermute | solution.py:513
  45.0 3.5 %collective-permute-start.2 = (f32[24,128]{1,0:T(8,128)S(1)}, f32[24,128]{1,0:T(8,128)S(1)}, u32[]{:S(2)}, u32[]{:S(2)}) collective-permute-start(f32[24,128]{1,0:T(8,128)S(1)} %shard_map.44.own_ref), channel_id=1, source_target_pairs={{0,16},{2,18},{4,20},{6,22},{8,24},{10,26},{12,28},{14,30},{16,0},... | collective-permute-start | bytes 36872 | tf_op jit(solution)/shard_map/ppermute | solution.py:506
  57.3 5.1 %collective-permute-start.3 = (f32[2,48,512]{2,1,0:T(8,128)S(1)}, f32[2,48,512]{2,1,0:T(8,128)S(1)}, u32[]{:S(2)}, u32[]{:S(2)}) collective-permute-start(f32[2,48,512]{2,1,0:T(8,128)S(1)} %get-tuple-element.23.edge_ref), channel_id=1, source_target_pairs={{0,1},{1,0},{2,3},{3,2},{4,5},{5,4},{6,7},{7,6},{8,9},{9,8},{10,11... | collective-permute-start | bytes 589832 | tf_op jit(solution)/shard_map/ppermute | solution.py:513

commit v9 on v8

--- a/solution.py
+++ b/solution.py
@@ -142,34 +142,37 @@
     return [[field_ref[c, i, :, lanes] for i in range(planes)] for c in range(3)]
 
 
-def solve_components(line, field, axes_ref, pins_ref, lanes, ghosts):
+def solve_components(line, field, scaled_ref, pins_ref, lanes, ghosts):
     planes = line.planes
-    axes = [[axes_ref[c, i, :, lanes] for i in range(planes)] for c in range(3)]
+    scaled = [[scaled_ref[c, i, :, lanes] for i in range(planes)] for c in range(3)]
+    projection = [
+        field[0][i] * scaled[0][i] + field[1][i] * scaled[1][i] + field[2][i] * scaled[2][i]
+        for i in range(planes)
+    ]
     for component in range(3):
-        source = []
-        for i in range(planes):
-            projection = (
-                field[0][i] * axes[0][i] + field[1][i] * axes[1][i] + field[2][i] * axes[2][i]
-            )
-            source.append(
-                field[component][i] + (anisotropy_rate * projection) * axes[component][i]
-            )
+        source = [
+            field[component][i] + projection[i] * scaled[component][i] for i in range(planes)
+        ]
         source = pinned(source, pins_ref, component, lanes)
         if ghosts is not None:
             source[0] = source[0] + diffusion * ghosts[component][0]
             source[-1] = source[-1] + diffusion * ghosts[component][1]
-        field[component] = line.solve(source)
+        solved = line.solve(source)
+        if component < 2:
+            projection = [
+                projection[i] + (solved[i] - field[component][i]) * scaled[component][i]
+                for i in range(planes)
+            ]
+        field[component] = solved
     return field
 
 
-def couplings(line, axes_ref, lanes):
+def couplings(line, scaled):
     planes = line.planes
     low, high = line.from_low, line.from_high
-    axes = [[axes_ref[c, i, :, lanes] for i in range(planes)] for c in range(3)]
-    scaled = [anisotropy_rate * a for a in axes[1]]
-    first_second = [axes[0][i] * scaled[i] for i in range(planes)]
-    second_third = [axes[2][i] * scaled[i] for i in range(planes)]
-    first_third = [(anisotropy_rate * axes[0][i]) * axes[2][i] for i in range(planes)]
+    first_second = [scaled[0][i] * scaled[1][i] for i in range(planes)]
+    second_third = [scaled[1][i] * scaled[2][i] for i in range(planes)]
+    first_third = [scaled[0][i] * scaled[2][i] for i in range(planes)]
 
     def weighted(terms, weights):
         total = terms[0] * float(weights[0] / diffusion)
@@ -191,10 +194,10 @@
     return found
 
 
-def send_tile(line, units, values, field, axes_ref, pins_ref, out_ref, tile):
-    rows = axes_ref.shape[2]
+def send_tile(line, units, values, field, scaled_ref, pins_ref, out_ref, tile):
+    rows = scaled_ref.shape[2]
     lanes = slice(tile * LANES, (tile + 1) * LANES)
-    solved = solve_components(line, field, axes_ref, pins_ref, lanes, None)
+    solved = solve_components(line, field, scaled_ref, pins_ref, lanes, None)
     for component in range(3):
         for side, end in enumerate((0, -1)):
             value = 2 * component + side
@@ -202,24 +205,35 @@
                 out_ref[target, :] = solved[component][end][source]
 
 
+def scaled_tile(axes_ref, lanes):
+    root = float(np.sqrt(anisotropy_rate))
+    planes = axes_ref.shape[1]
+    return [[root * axes_ref[c, i, :, lanes] for i in range(planes)] for c in range(3)]
+
+
 def coupling_kernel(line, units, axes_ref, out_ref):
     rows, width = axes_ref.shape[2:]
-    tiles = width // LANES
-    for tile in range(tiles):
-        found = couplings(line, axes_ref, slice(tile * LANES, (tile + 1) * LANES))
-        for value, one in enumerate(found):
+    for tile in range(width // LANES):
+        lanes = slice(tile * LANES, (tile + 1) * LANES)
+        for value, one in enumerate(couplings(line, scaled_tile(axes_ref, lanes))):
             for source, target in pieces(value, COUPLED - RHS, units, tile, rows):
                 out_ref[target, :] = one[source]
 
 
-def first_kernel(line, groups, units, coupling_ref, field_ref, axes_ref, pins_ref, out_ref):
+def first_kernel(
+    line, groups, units, coupling_ref, field_ref, axes_ref, pins_ref, out_ref, scaled_ref
+):
     extra = (COUPLED - RHS) * units
     for d in range(groups):
         start = (d * COUPLED + RHS) * units
         out_ref[start : start + extra, :] = coupling_ref[d * extra : (d + 1) * extra, :]
     for tile in range(field_ref.shape[3] // LANES):
-        field = read_field(field_ref, slice(tile * LANES, (tile + 1) * LANES))
-        send_tile(line, units, COUPLED, field, axes_ref, pins_ref, out_ref, tile)
+        lanes = slice(tile * LANES, (tile + 1) * LANES)
+        for c, parts in enumerate(scaled_tile(axes_ref, lanes)):
+            for i, part in enumerate(parts):
+                scaled_ref[c, i, :, lanes] = part
+        field = read_field(field_ref, lanes)
+        send_tile(line, units, COUPLED, field, scaled_ref, pins_ref, out_ref, tile)
 
 
 def solve_children(level, levels, rhs, coupling, outer):
@@ -348,7 +362,7 @@
             out_ref[start : start + units, :] = ghost
 
 
-def finish_kernel(line, units, field_ref, axes_ref, pins_ref, ghost_ref, out_ref, edge_ref):
+def finish_kernel(line, units, field_ref, scaled_ref, pins_ref, ghost_ref, out_ref, edge_ref):
     planes = line.planes
     rows, width = field_ref.shape[2], field_ref.shape[3]
     tiles = width // LANES
@@ -368,7 +382,7 @@
             for c in range(3)
         ]
         field = read_field(field_ref, lanes)
-        solved = solve_components(line, field, axes_ref, pins_ref, lanes, ghosts)
+        solved = solve_components(line, field, scaled_ref, pins_ref, lanes, ghosts)
         for c in range(3):
             for i in range(planes):
                 out_ref[c, i, :, lanes] = solved[c][i]
@@ -382,13 +396,14 @@
     return jnp.minimum(lax.rsqrt(square), 1.0 / norm_floor)
 
 
-def turn_kernel(field_ref, axes_ref, out_ref, raw_ref):
+def turn_kernel(field_ref, scaled_ref, out_ref, raw_ref):
     planes, rows, width = field_ref.shape[1:]
     row = lax.broadcasted_iota(jnp.int32, (rows, width), 0)
     for i in range(planes):
         field = [field_ref[c, i] for c in range(3)]
-        axes = [axes_ref[c, i] for c in range(3)]
-        projection = field[0] * axes[0] + field[1] * axes[1] + field[2] * axes[2]
+        scaled = [scaled_ref[c, i] for c in range(3)]
+        projection = field[0] * scaled[0] + field[1] * scaled[1] + field[2] * scaled[2]
+        projection = projection * (1.0 / anisotropy_rate)
         effective = []
         for c in range(3):
             below = jnp.where(row == 0, 0.0, pltpu.roll(field[c], 1, 0))
@@ -396,7 +411,7 @@
             beside = pltpu.roll(field[c], 1, 1) + pltpu.roll(field[c], width - 1, 1)
             effective.append(
                 exchange_rate * (((above + below) + beside) - 4.0 * field[c])
-                + projection * axes[c]
+                + projection * scaled[c]
             )
         rotated = []
         for c in range(3):
@@ -441,7 +456,7 @@
     edge_ref,
     raw_ref,
     beyond_ref,
-    axes_ref,
+    scaled_ref,
     pins_ref,
     out_ref,
     sent_ref,
@@ -456,7 +471,7 @@
             for i in range(planes):
                 field[c][i] = mended(field[c][i], mended_ref, c * planes + i, lanes)
                 out_ref[c, i, :, lanes] = field[c][i]
-        send_tile(line, units, RHS, field, axes_ref, pins_ref, sent_ref, tile)
+        send_tile(line, units, RHS, field, scaled_ref, pins_ref, sent_ref, tile)
 
 
 def last_kernel(turned_ref, edge_ref, raw_ref, beyond_ref, out_hbm, out_ref, mended_ref, sems):
@@ -535,9 +550,9 @@
         [(groups * (COUPLED - RHS) * units, LANES)],
         easy_axes,
     )
-    (sent,) = call(
+    sent, scaled = call(
         functools.partial(first_kernel, line, groups, units),
-        [(groups * COUPLED * units, LANES)],
+        [(groups * COUPLED * units, LANES), whole],
         coupling,
         field,
         easy_axes,
@@ -572,12 +587,12 @@
             functools.partial(finish_kernel, line, units),
             [whole, edge_shape],
             field,
-            easy_axes,
+            scaled,
             pins,
             ghosts,
         )
         beyond = from_neighbours(edges)
-        turned, raw = call(turn_kernel, [whole, edge_shape], solved, easy_axes)
+        turned, raw = call(turn_kernel, [whole, edge_shape], solved, scaled)
         if stepno < STEPS - 1:
             field, sent = call(
                 functools.partial(mend_and_send_kernel, line, units),
@@ -586,7 +601,7 @@
                 edges,
                 raw,
                 beyond,
-                easy_axes,
+                scaled,
                 pins,
                 scratch=[pltpu.VMEM(edge_shape, jnp.float32)],
             )

time: 64 us -> 64.6 us (level)
  Pallas kernels: 9.81 us -> 10.5 us
    pallas_call x12, Pallas kernels: 9.81 us -> 10.5 us  [call(): pl.pallas_call(kernel, out_shape=tuple(shapes), in_specs=[VMEM] * len(ope...]
    unnamed x8 -> x6, local copies, waits for them, and re-layouts: 1.92 us -> 1.87 us
where the time goes in v9:
time: 64.6 us; the launch traced here: 64.3 us
  blocking collectives  36.6 us (57%)
  starting transfers between devices  12.9 us (20%)
  Pallas kernels  10.5 us (16%)
  waiting for transfers between devices  2.41 us (4%)
  local copies, waits for them, and re-layouts  1.87 us (3%)
    all_to_all x4, blocking collectives, exchange(): lax.all_to_all(parts, 'gx', split_axis=0, concat_axis=0, axis_index_group...  36.6 us
    pallas_call x12, Pallas kernels, call(): pl.pallas_call(kernel, out_shape=tuple(shapes), in_specs=[VMEM] * len(ope...  10.5 us
    ppermute x2, starting transfers between devices, from_neighbours(): return lax.ppermute(edges, 'gy', forward)  8.18 us
    ppermute x2, starting transfers between devices, swap_halves(): return lax.ppermute(block, 'gx', pairs)  4.75 us
    ppermute x2, waiting for transfers between devices, swap_halves(): return lax.ppermute(block, 'gx', pairs)  2.4 us
    unnamed x6, local copies, waits for them, and re-layouts  1.87 us
  transfers between devices with their start and end apart: 4, of which 2 were waited for; matrix products, arithmetic and copies ran while one was open for 0% of the time, Pallas kernels for 5%

profile of v9, /device:TPU:1, one launch (start us, length us, event | category | flops | bytes accessed | tf_op | source)
XLA Modules:
  0.0 64.3 jit_solution(9579931207093589032)
XLA Ops:
  0.0 1.4 %copy-done.1 = f32[3,16,16,512]{3,2,1,0:T(8,128)S(1)} copy-done((f32[3,16,16,512]{3,2,1,0:T(8,128)S(1)}, f32[3,16,16,512]{3,2,1,0:T(8,128)}, u32[]{:S(2)}) %copy-start.1) | copy-done | bytes 1572888
  1.4 0.9 %shard_map.37.coupling_ref = f32[640,128]{1,0:T(8,128)S(1)} custom-call(f32[3,16,16,512]{3,2,1,0:T(8,128)S(1)} %copy-done.1), custom_call_target="tpu_custom_call" | custom-call | tf_op jit(solution)/shard_map/pallas_call | solution.py:499
  2.4 0.5 copy-done
  2.8 1.3 %shard_map.38 = (f32[1024,128]{1,0:T(8,128)S(1)}, f32[3,16,16,512]{3,2,1,0:T(8,128)S(1)}) custom-call(f32[640,128]{1,0:T(8,128)S(1)} %shard_map.37.coupling_ref, f32[3,16,16,512]{3,2,1,0:T(8,128)S(1)} %copy-done, f32[3,16,16,512]{3,2,1,0:T(8,128)S(1)} %copy-done.1, f32[2,3,16,512]{3,2,1,0:T(8,128)S(1)} %copy-done.2), custom_call_target="tpu_custom_call" | custom-call | tf_op jit(solution)/shard_map/pallas_call | solution.py:499
  4.1 13.2 %all_to_all.20 = f32[8,128,128]{2,1,0:T(8,128)S(1)} all-to-all(f32[8,128,128]{2,1,0:T(8,128)S(1)} %bitcast.20), channel_id=1, replica_groups={{0,2,4,6,8,10,12,14},{16,18,20,22,24,26,28,30},{1,3,5,7,9,11,13,15},{17..., dimensions={0} | all-to-all | bytes 1048576 | tf_op jit(solution)/shard_map/all_to_all | solution.py:514
  17.3 0.2 shard_map.39.own_ref.own_coupling_ref
  17.5 2.4 %collective-permute-start = (f32[48,128]{1,0:T(8,128)S(1)}, f32[48,128]{1,0:T(8,128)S(1)}, u32[]{:S(2)}, u32[]{:S(2)}) collective-permute-start(f32[48,128]{1,0:T(8,128)S(1)} %shard_map.39.own_ref.own_coupling_ref), channel_id=1, source_target_pairs={{0,16},{2,18},{4,20},{6,22},{8,24},{10,26},{12,28},{14,30},{16,0},... | collective-permute-start | bytes 73736 | tf_op jit(solution)/shard_map/ppermute | solution.py:521
  19.9 1.3 %collective-permute-done.other_ref.other_coupling_ref = f32[48,128]{1,0:T(8,128)S(1)} collective-permute-done((f32[48,128]{1,0:T(8,128)S(1)}, f32[48,128]{1,0:T(8,128)S(1)}, u32[]{:S(2)}, u32[]{:S(2)}) %collective-permute-start) | collective-permute-done | bytes 24608 | tf_op jit(solution)/shard_map/ppermute | solution.py:521
  21.2 0.1 shard_map.40
  21.3 7.6 %all_to_all.21 = f32[8,48,128]{2,1,0:T(8,128)S(1)} all-to-all(f32[8,48,128]{2,1,0:T(8,128)S(1)} %bitcast.19), channel_id=1, replica_groups={{0,2,4,6,8,10,12,14},{16,18,20,22,24,26,28,30},{1,3,5,7,9,11,13,15},{17..., dimensions={0} | all-to-all | bytes 393216 | tf_op jit(solution)/shard_map/all_to_all | solution.py:514
  28.9 1.0 %shard_map.41 = (f32[3,16,16,512]{3,2,1,0:T(8,128)S(1)}, f32[2,48,512]{2,1,0:T(8,128)S(1)}) custom-call(f32[3,16,16,512]{3,2,1,0:T(8,128)S(1)} %copy-done, f32[3,16,16,512]{3,2,1,0:T(8,128)S(1)} %get-tuple-element.17.scaled_ref, f32[2,3,16,512]{3,2,1,0:T(8,128)S(1)} %copy-done.2, f32[384,128]{1,0:T(8,128)S(1)} %bitcast.17), custom_call_target="tpu_custom_call" | custom-call | tf_op jit(solution)/shard_map/pallas_call | solution.py:499
  29.9 4.6 %collective-permute-start.1 = (f32[2,48,512]{2,1,0:T(8,128)S(1)}, f32[2,48,512]{2,1,0:T(8,128)S(1)}, u32[]{:S(2)}, u32[]{:S(2)}) collective-permute-start(f32[2,48,512]{2,1,0:T(8,128)S(1)} %get-tuple-element.21.edge_ref), channel_id=1, source_target_pairs={{0,1},{1,0},{2,3},{3,2},{4,5},{5,4},{6,7},{7,6},{8,9},{9,8},{10,11... | collective-permute-start | bytes 589832 | tf_op jit(solution)/shard_map/ppermute | solution.py:528
  34.5 1.5 %shard_map.42 = (f32[3,16,16,512]{3,2,1,0:T(8,128)S(1)}, f32[2,48,512]{2,1,0:T(8,128)S(1)}) custom-call(f32[3,16,16,512]{3,2,1,0:T(8,128)S(1)} %get-tuple-element.19.field_ref, f32[3,16,16,512]{3,2,1,0:T(8,128)S(1)} %get-tuple-element.17.scaled_ref), custom_call_target="tpu_custom_call" | custom-call | tf_op jit(solution)/shard_map/pallas_call | solution.py:499
  36.0 1.4 %shard_map.43 = (f32[3,16,16,512]{3,2,1,0:T(8,128)S(1)}, f32[384,128]{1,0:T(8,128)S(1)}) custom-call(f32[3,16,16,512]{3,2,1,0:T(8,128)S(1)} %get-tuple-element.20.turned_ref, f32[2,48,512]{2,1,0:T(8,128)S(1)} %get-tuple-element.21.edge_ref, f32[2,48,512]{2,1,0:T(8,128)S(1)} %get-tuple-element.22.raw_ref, ...), custom_call_target="tpu_custom_call" | custom-call | tf_op jit(solution)/shard_map/pallas_call | solution.py:499
  37.4 8.0 %all_to_all.22 = f32[8,48,128]{2,1,0:T(8,128)S(1)} all-to-all(f32[8,48,128]{2,1,0:T(8,128)S(1)} %bitcast.21), channel_id=1, replica_groups={{0,2,4,6,8,10,12,14},{16,18,20,22,24,26,28,30},{1,3,5,7,9,11,13,15},{17..., dimensions={0} | all-to-all | bytes 393216 | tf_op jit(solution)/shard_map/all_to_all | solution.py:514
  45.4 0.1 shard_map.44.own_ref
  45.5 2.4 %collective-permute-start.2 = (f32[24,128]{1,0:T(8,128)S(1)}, f32[24,128]{1,0:T(8,128)S(1)}, u32[]{:S(2)}, u32[]{:S(2)}) collective-permute-start(f32[24,128]{1,0:T(8,128)S(1)} %shard_map.44.own_ref), channel_id=1, source_target_pairs={{0,16},{2,18},{4,20},{6,22},{8,24},{10,26},{12,28},{14,30},{16,0},... | collective-permute-start | bytes 36872 | tf_op jit(solution)/shard_map/ppermute | solution.py:521
  47.9 1.1 %collective-permute-done.2.other_ref = f32[24,128]{1,0:T(8,128)S(1)} collective-permute-done((f32[24,128]{1,0:T(8,128)S(1)}, f32[24,128]{1,0:T(8,128)S(1)}, u32[]{:S(2)}, u32[]{:S(2)}) %collective-permute-start.2) | collective-permute-done | bytes 12320 | tf_op jit(solution)/shard_map/ppermute | solution.py:521
  49.0 0.1 shard_map.45
  49.1 7.7 %all_to_all.23 = f32[8,48,128]{2,1,0:T(8,128)S(1)} all-to-all(f32[8,48,128]{2,1,0:T(8,128)S(1)} %bitcast.18), channel_id=1, replica_groups={{0,2,4,6,8,10,12,14},{16,18,20,22,24,26,28,30},{1,3,5,7,9,11,13,15},{17..., dimensions={0} | all-to-all | bytes 393216 | tf_op jit(solution)/shard_map/all_to_all | solution.py:514
  56.9 1.0 %shard_map.46 = (f32[3,16,16,512]{3,2,1,0:T(8,128)S(1)}, f32[2,48,512]{2,1,0:T(8,128)S(1)}) custom-call(f32[3,16,16,512]{3,2,1,0:T(8,128)S(1)} %get-tuple-element.23.field_ref, f32[3,16,16,512]{3,2,1,0:T(8,128)S(1)} %get-tuple-element.17.scaled_ref, f32[2,3,16,512]{3,2,1,0:T(8,128)S(1)} %copy-done.2, f32[384,128]{1,0:T(8,128)S(1)} %bitcast.16), custom_call_target="tpu_custom_call" | custom-call | tf_op jit(solution)/shard_map/pallas_call | solution.py:499
  57.9 3.6 %collective-permute-start.3 = (f32[2,48,512]{2,1,0:T(8,128)S(1)}, f32[2,48,512]{2,1,0:T(8,128)S(1)}, u32[]{:S(2)}, u32[]{:S(2)}) collective-permute-start(f32[2,48,512]{2,1,0:T(8,128)S(1)} %get-tuple-element.27.edge_ref), channel_id=1, source_target_pairs={{0,1},{1,0},{2,3},{3,2},{4,5},{5,4},{6,7},{7,6},{8,9},{9,8},{10,11... | collective-permute-start | bytes 589832 | tf_op jit(solution)/shard_map/ppermute | solution.py:528
  61.5 1.5 %shard_map.47 = (f32[3,16,16,512]{3,2,1,0:T(8,128)S(1)}, f32[2,48,512]{2,1,0:T(8,128)S(1)}) custom-call(f32[3,16,16,512]{3,2,1,0:T(8,128)S(1)} %get-tuple-element.25.field_ref, f32[3,16,16,512]{3,2,1,0:T(8,128)S(1)} %get-tuple-element.17.scaled_ref), custom_call_target="tpu_custom_call" | custom-call | tf_op jit(solution)/shard_map/pallas_call | solution.py:499
  63.0 1.3 %shard_map.48 = f32[3,16,16,512]{3,2,1,0:T(8,128)} custom-call(f32[3,16,16,512]{3,2,1,0:T(8,128)S(1)} %get-tuple-element.26.turned_ref, f32[2,48,512]{2,1,0:T(8,128)S(1)} %get-tuple-element.27.edge_ref, f32[2,48,512]{2,1,0:T(8,128)S(1)} %get-tuple-element.28.raw_ref, f32[2,48,512]{2,1,0:T(8,128)S(1)} %collective-permute-done.3.beyond_ref), custom_call_target="tpu_custom_call" | custom-call | tf_op jit(solution)/shard_map/pallas_call | solution.py:499
  (6 shorter events, 0.0 us)
Async XLA Ops:
  0.0 1.4 %copy-start.1 = (f32[3,16,16,512]{3,2,1,0:T(8,128)S(1)}, f32[3,16,16,512]{3,2,1,0:T(8,128)}, u32[]{:S(2)}) copy-start(f32[3,16,16,512]{3,2,1,0:T(8,128)} %axes_ref.3) | copy-start | bytes 4718596
  1.4 1.4 %copy-start = (f32[3,16,16,512]{3,2,1,0:T(8,128)S(1)}, f32[3,16,16,512]{3,2,1,0:T(8,128)}, u32[]{:S(2)}) copy-start(f32[3,16,16,512]{3,2,1,0:T(8,128)} %field_ref.3) | copy-start | bytes 4718596
  1.4 1.4 %copy-start.2 = (f32[2,3,16,512]{3,2,1,0:T(8,128)S(1)}, f32[2,3,16,512]{3,2,1,0:T(8,128)}, u32[]{:S(2)}) copy-start(f32[2,3,16,512]{3,2,1,0:T(8,128)} %pins_ref.7) | copy-start | bytes 589828
  17.5 3.6 %collective-permute-start = (f32[48,128]{1,0:T(8,128)S(1)}, f32[48,128]{1,0:T(8,128)S(1)}, u32[]{:S(2)}, u32[]{:S(2)}) collective-permute-start(f32[48,128]{1,0:T(8,128)S(1)} %shard_map.39.own_ref.own_coupling_ref), channel_id=1, source_target_pairs={{0,16},{2,18},{4,20},{6,22},{8,24},{10,26},{12,28},{14,30},{16,0},... | collective-permute-start | bytes 73736 | tf_op jit(solution)/shard_map/ppermute | solution.py:521
  29.9 6.1 %collective-permute-start.1 = (f32[2,48,512]{2,1,0:T(8,128)S(1)}, f32[2,48,512]{2,1,0:T(8,128)S(1)}, u32[]{:S(2)}, u32[]{:S(2)}) collective-permute-start(f32[2,48,512]{2,1,0:T(8,128)S(1)} %get-tuple-element.21.edge_ref), channel_id=1, source_target_pairs={{0,1},{1,0},{2,3},{3,2},{4,5},{5,4},{6,7},{7,6},{8,9},{9,8},{10,11... | collective-permute-start | bytes 589832 | tf_op jit(solution)/shard_map/ppermute | solution.py:528
  45.5 3.5 %collective-permute-start.2 = (f32[24,128]{1,0:T(8,128)S(1)}, f32[24,128]{1,0:T(8,128)S(1)}, u32[]{:S(2)}, u32[]{:S(2)}) collective-permute-start(f32[24,128]{1,0:T(8,128)S(1)} %shard_map.44.own_ref), channel_id=1, source_target_pairs={{0,16},{2,18},{4,20},{6,22},{8,24},{10,26},{12,28},{14,30},{16,0},... | collective-permute-start | bytes 36872 | tf_op jit(solution)/shard_map/ppermute | solution.py:521
  57.9 5.1 %collective-permute-start.3 = (f32[2,48,512]{2,1,0:T(8,128)S(1)}, f32[2,48,512]{2,1,0:T(8,128)S(1)}, u32[]{:S(2)}, u32[]{:S(2)}) collective-permute-start(f32[2,48,512]{2,1,0:T(8,128)S(1)} %get-tuple-element.27.edge_ref), channel_id=1, source_target_pairs={{0,1},{1,0},{2,3},{3,2},{4,5},{5,4},{6,7},{7,6},{8,9},{9,8},{10,11... | collective-permute-start | bytes 589832 | tf_op jit(solution)/shard_map/ppermute | solution.py:528

commit v10 on v8

--- a/solution.py
+++ b/solution.py
@@ -37,16 +37,38 @@
         self.from_low = diffusion * np.linalg.inv(block)[:, 0]
         self.from_high = self.from_low[::-1]
 
-    def solve(self, source):
-        planes = self.planes
+    def sweep(self, source):
         carried = [source[0]]
-        for i in range(1, planes):
+        for i in range(1, len(source)):
             carried.append(source[i] + self.factor[i] * carried[-1])
-        solved = [None] * planes
-        solved[-1] = carried[-1] * self.inverse_pivot[-1]
-        for i in range(planes - 2, -1, -1):
+        return carried
+
+    def unwind(self, carried, meeting):
+        solved = [None] * len(carried)
+        solved[-1] = meeting
+        for i in range(len(carried) - 2, -1, -1):
             solved[i] = carried[i] * self.inverse_pivot[i] + self.factor[i + 1] * solved[i + 1]
         return solved
+
+    def solve(self, source):
+        half = self.planes // 2
+        low, high = self.sweep(source[:half]), self.sweep(source[half:][::-1])
+        pivot_low = 1.0 / self.inverse_pivot[len(low) - 1]
+        pivot_high = 1.0 / self.inverse_pivot[len(high) - 1]
+        scale = 1.0 / (pivot_low * pivot_high - diffusion * diffusion)
+        cross = diffusion * scale
+        meeting_low = low[-1] * (pivot_high * scale) + high[-1] * cross
+        meeting_high = high[-1] * (pivot_low * scale) + low[-1] * cross
+        return self.unwind(low, meeting_low) + self.unwind(high, meeting_high)[::-1]
+
+    def ends(self, source):
+        found = []
+        for weights in (self.from_low, self.from_high):
+            total = source[0] * float(weights[0] / diffusion)
+            for weight, value in zip(weights[1:], source[1:]):
+                total = total + value * float(weight / diffusion)
+            found.append(total)
+        return found
 
 
 class Level:
@@ -144,6 +166,7 @@
 
 def solve_components(line, field, axes_ref, pins_ref, lanes, ghosts):
     planes = line.planes
+    field = list(field)
     axes = [[axes_ref[c, i, :, lanes] for i in range(planes)] for c in range(3)]
     for component in range(3):
         source = []
@@ -158,6 +181,8 @@
         if ghosts is not None:
             source[0] = source[0] + diffusion * ghosts[component][0]
             source[-1] = source[-1] + diffusion * ghosts[component][1]
+        if ghosts is None and component == 2:
+            return field[:2] + [line.ends(source)]
         field[component] = line.solve(source)
     return field
 

time: 64 us -> 64.1 us (level)
  no operation moved by 1% of the time
where the time goes in v10:
time: 64.1 us; the launch traced here: 63.8 us
  blocking collectives  36.6 us (57%)
  starting transfers between devices  12.9 us (20%)
  Pallas kernels  9.88 us (15%)
  waiting for transfers between devices  2.41 us (4%)
  local copies, waits for them, and re-layouts  1.95 us (3%)
    all_to_all x4, blocking collectives, exchange(): lax.all_to_all(parts, 'gx', split_axis=0, concat_axis=0, axis_index_group...  36.6 us
    pallas_call x12, Pallas kernels, call(): pl.pallas_call(kernel, out_shape=tuple(shapes), in_specs=[VMEM] * len(ope...  9.88 us
    ppermute x2, starting transfers between devices, from_neighbours(): return lax.ppermute(edges, 'gy', forward)  8.18 us
    ppermute x2, starting transfers between devices, swap_halves(): return lax.ppermute(block, 'gx', pairs)  4.75 us
    ppermute x2, waiting for transfers between devices, swap_halves(): return lax.ppermute(block, 'gx', pairs)  2.4 us
    unnamed x8, local copies, waits for them, and re-layouts  1.95 us
  transfers between devices with their start and end apart: 4, of which 2 were waited for; matrix products, arithmetic and copies ran while one was open for 0% of the time, Pallas kernels for 5%

profile of v10, /device:TPU:1, one launch (start us, length us, event | category | flops | bytes accessed | tf_op | source)
XLA Modules:
  0.0 63.8 jit_solution(7293680191321605712)
XLA Ops:
  0.0 1.4 %copy-done = f32[3,16,16,512]{3,2,1,0:T(8,128)S(1)} copy-done((f32[3,16,16,512]{3,2,1,0:T(8,128)S(1)}, f32[3,16,16,512]{3,2,1,0:T(8,128)}, u32[]{:S(2)}) %copy-start) | copy-done | bytes 1572888
  1.4 0.9 %shard_map.37.coupling_ref = f32[640,128]{1,0:T(8,128)S(1)} custom-call(f32[3,16,16,512]{3,2,1,0:T(8,128)S(1)} %copy-done), custom_call_target="tpu_custom_call" | custom-call | tf_op jit(solution)/shard_map/pallas_call | solution.py:509
  2.3 0.5 copy-done.2
  2.8 0.9 %shard_map.38 = f32[1024,128]{1,0:T(8,128)S(1)} custom-call(f32[640,128]{1,0:T(8,128)S(1)} %shard_map.37.coupling_ref, f32[3,16,16,512]{3,2,1,0:T(8,128)S(1)} %copy-done.2, f32[3,16,16,512]{3,2,1,0:T(8,128)S(1)} %copy-done, f32[2,3,16,512]{3,2,1,0:T(8,128)S(1)} %copy-done.3), custom_call_target="tpu_custom_call" | custom-call | tf_op jit(solution)/shard_map/pallas_call | solution.py:509
  3.7 13.2 %all_to_all.20 = f32[8,128,128]{2,1,0:T(8,128)S(1)} all-to-all(f32[8,128,128]{2,1,0:T(8,128)S(1)} %bitcast.14), channel_id=1, replica_groups={{0,2,4,6,8,10,12,14},{16,18,20,22,24,26,28,30},{1,3,5,7,9,11,13,15},{17..., dimensions={0} | all-to-all | bytes 1048576 | tf_op jit(solution)/shard_map/all_to_all | solution.py:524
  17.0 0.2 shard_map.39.own_ref.own_coupling_ref
  17.2 2.4 %collective-permute-start = (f32[48,128]{1,0:T(8,128)S(1)}, f32[48,128]{1,0:T(8,128)S(1)}, u32[]{:S(2)}, u32[]{:S(2)}) collective-permute-start(f32[48,128]{1,0:T(8,128)S(1)} %shard_map.39.own_ref.own_coupling_ref), channel_id=1, source_target_pairs={{0,16},{2,18},{4,20},{6,22},{8,24},{10,26},{12,28},{14,30},{16,0},... | collective-permute-start | bytes 73736 | tf_op jit(solution)/shard_map/ppermute | solution.py:531
  19.6 1.3 %collective-permute-done.other_ref.other_coupling_ref = f32[48,128]{1,0:T(8,128)S(1)} collective-permute-done((f32[48,128]{1,0:T(8,128)S(1)}, f32[48,128]{1,0:T(8,128)S(1)}, u32[]{:S(2)}, u32[]{:S(2)}) %collective-permute-start) | collective-permute-done | bytes 24608 | tf_op jit(solution)/shard_map/ppermute | solution.py:531
  20.8 0.1 shard_map.40
  21.0 7.6 %all_to_all.21 = f32[8,48,128]{2,1,0:T(8,128)S(1)} all-to-all(f32[8,48,128]{2,1,0:T(8,128)S(1)} %bitcast.20), channel_id=1, replica_groups={{0,2,4,6,8,10,12,14},{16,18,20,22,24,26,28,30},{1,3,5,7,9,11,13,15},{17..., dimensions={0} | all-to-all | bytes 393216 | tf_op jit(solution)/shard_map/all_to_all | solution.py:524
  28.6 1.0 %shard_map.41 = (f32[3,16,16,512]{3,2,1,0:T(8,128)S(1)}, f32[2,48,512]{2,1,0:T(8,128)S(1)}) custom-call(f32[3,16,16,512]{3,2,1,0:T(8,128)S(1)} %copy-done.2, f32[3,16,16,512]{3,2,1,0:T(8,128)S(1)} %copy-done.1, f32[2,3,16,512]{3,2,1,0:T(8,128)S(1)} %copy-done.3, f32[384,128]{1,0:T(8,128)S(1)} %bitcast.18), custom_call_target="tpu_custom_call" | custom-call | tf_op jit(solution)/shard_map/pallas_call | solution.py:509
  29.6 4.6 %collective-permute-start.1 = (f32[2,48,512]{2,1,0:T(8,128)S(1)}, f32[2,48,512]{2,1,0:T(8,128)S(1)}, u32[]{:S(2)}, u32[]{:S(2)}) collective-permute-start(f32[2,48,512]{2,1,0:T(8,128)S(1)} %get-tuple-element.17.edge_ref), channel_id=1, source_target_pairs={{0,1},{1,0},{2,3},{3,2},{4,5},{5,4},{6,7},{7,6},{8,9},{9,8},{10,11... | collective-permute-start | bytes 589832 | tf_op jit(solution)/shard_map/ppermute | solution.py:538
  34.1 1.5 %shard_map.42 = (f32[3,16,16,512]{3,2,1,0:T(8,128)S(1)}, f32[2,48,512]{2,1,0:T(8,128)S(1)}) custom-call(f32[3,16,16,512]{3,2,1,0:T(8,128)S(1)} %get-tuple-element.15.field_ref, f32[3,16,16,512]{3,2,1,0:T(8,128)S(1)} %copy-done.1), custom_call_target="tpu_custom_call" | custom-call | tf_op jit(solution)/shard_map/pallas_call | solution.py:509
  35.6 1.3 %shard_map.43 = (f32[3,16,16,512]{3,2,1,0:T(8,128)S(1)}, f32[384,128]{1,0:T(8,128)S(1)}) custom-call(f32[3,16,16,512]{3,2,1,0:T(8,128)S(1)} %get-tuple-element.16.turned_ref, f32[2,48,512]{2,1,0:T(8,128)S(1)} %get-tuple-element.17.edge_ref, f32[2,48,512]{2,1,0:T(8,128)S(1)} %get-tuple-element.18.raw_ref, ...), custom_call_target="tpu_custom_call" | custom-call | tf_op jit(solution)/shard_map/pallas_call | solution.py:509
  36.9 8.0 %all_to_all.22 = f32[8,48,128]{2,1,0:T(8,128)S(1)} all-to-all(f32[8,48,128]{2,1,0:T(8,128)S(1)} %bitcast.21), channel_id=1, replica_groups={{0,2,4,6,8,10,12,14},{16,18,20,22,24,26,28,30},{1,3,5,7,9,11,13,15},{17..., dimensions={0} | all-to-all | bytes 393216 | tf_op jit(solution)/shard_map/all_to_all | solution.py:524
  44.9 0.1 shard_map.44.own_ref
  45.0 2.4 %collective-permute-start.2 = (f32[24,128]{1,0:T(8,128)S(1)}, f32[24,128]{1,0:T(8,128)S(1)}, u32[]{:S(2)}, u32[]{:S(2)}) collective-permute-start(f32[24,128]{1,0:T(8,128)S(1)} %shard_map.44.own_ref), channel_id=1, source_target_pairs={{0,16},{2,18},{4,20},{6,22},{8,24},{10,26},{12,28},{14,30},{16,0},... | collective-permute-start | bytes 36872 | tf_op jit(solution)/shard_map/ppermute | solution.py:531
  47.4 1.1 %collective-permute-done.2.other_ref = f32[24,128]{1,0:T(8,128)S(1)} collective-permute-done((f32[24,128]{1,0:T(8,128)S(1)}, f32[24,128]{1,0:T(8,128)S(1)}, u32[]{:S(2)}, u32[]{:S(2)}) %collective-permute-start.2) | collective-permute-done | bytes 12320 | tf_op jit(solution)/shard_map/ppermute | solution.py:531
  48.6 0.1 shard_map.45
  48.7 7.7 %all_to_all.23 = f32[8,48,128]{2,1,0:T(8,128)S(1)} all-to-all(f32[8,48,128]{2,1,0:T(8,128)S(1)} %bitcast.19), channel_id=1, replica_groups={{0,2,4,6,8,10,12,14},{16,18,20,22,24,26,28,30},{1,3,5,7,9,11,13,15},{17..., dimensions={0} | all-to-all | bytes 393216 | tf_op jit(solution)/shard_map/all_to_all | solution.py:524
  56.4 1.0 %shard_map.46 = (f32[3,16,16,512]{3,2,1,0:T(8,128)S(1)}, f32[2,48,512]{2,1,0:T(8,128)S(1)}) custom-call(f32[3,16,16,512]{3,2,1,0:T(8,128)S(1)} %get-tuple-element.19.field_ref, f32[3,16,16,512]{3,2,1,0:T(8,128)S(1)} %copy-done.1, f32[2,3,16,512]{3,2,1,0:T(8,128)S(1)} %copy-done.3, f32[384,128]{1,0:T(8,128)S(1)} %bitcast.17), custom_call_target="tpu_custom_call" | custom-call | tf_op jit(solution)/shard_map/pallas_call | solution.py:509
  57.4 3.6 %collective-permute-start.3 = (f32[2,48,512]{2,1,0:T(8,128)S(1)}, f32[2,48,512]{2,1,0:T(8,128)S(1)}, u32[]{:S(2)}, u32[]{:S(2)}) collective-permute-start(f32[2,48,512]{2,1,0:T(8,128)S(1)} %get-tuple-element.23.edge_ref), channel_id=1, source_target_pairs={{0,1},{1,0},{2,3},{3,2},{4,5},{5,4},{6,7},{7,6},{8,9},{9,8},{10,11... | collective-permute-start | bytes 589832 | tf_op jit(solution)/shard_map/ppermute | solution.py:538
  61.0 1.4 %shard_map.47 = (f32[3,16,16,512]{3,2,1,0:T(8,128)S(1)}, f32[2,48,512]{2,1,0:T(8,128)S(1)}) custom-call(f32[3,16,16,512]{3,2,1,0:T(8,128)S(1)} %get-tuple-element.21.field_ref, f32[3,16,16,512]{3,2,1,0:T(8,128)S(1)} %copy-done.1), custom_call_target="tpu_custom_call" | custom-call | tf_op jit(solution)/shard_map/pallas_call | solution.py:509
  62.5 1.3 %shard_map.48 = f32[3,16,16,512]{3,2,1,0:T(8,128)} custom-call(f32[3,16,16,512]{3,2,1,0:T(8,128)S(1)} %get-tuple-element.22.turned_ref, f32[2,48,512]{2,1,0:T(8,128)S(1)} %get-tuple-element.23.edge_ref, f32[2,48,512]{2,1,0:T(8,128)S(1)} %get-tuple-element.24.raw_ref, f32[2,48,512]{2,1,0:T(8,128)S(1)} %collective-permute-done.3.beyond_ref), custom_call_target="tpu_custom_call" | custom-call | tf_op jit(solution)/shard_map/pallas_call | solution.py:509
  (8 shorter events, 0.0 us)
Async XLA Ops:
  0.0 1.4 %copy-start = (f32[3,16,16,512]{3,2,1,0:T(8,128)S(1)}, f32[3,16,16,512]{3,2,1,0:T(8,128)}, u32[]{:S(2)}) copy-start(f32[3,16,16,512]{3,2,1,0:T(8,128)} %axes_ref.13) | copy-start | bytes 4718596
  1.4 1.4 %copy-start.2 = (f32[3,16,16,512]{3,2,1,0:T(8,128)S(1)}, f32[3,16,16,512]{3,2,1,0:T(8,128)}, u32[]{:S(2)}) copy-start(f32[3,16,16,512]{3,2,1,0:T(8,128)} %field_ref.3) | copy-start | bytes 4718596
  1.4 1.4 %copy-start.3 = (f32[2,3,16,512]{3,2,1,0:T(8,128)S(1)}, f32[2,3,16,512]{3,2,1,0:T(8,128)}, u32[]{:S(2)}) copy-start(f32[2,3,16,512]{3,2,1,0:T(8,128)} %pins_ref.7) | copy-start | bytes 589828
  17.0 11.6 %copy-start.1 = (f32[3,16,16,512]{3,2,1,0:T(8,128)S(1)}, f32[3,16,16,512]{3,2,1,0:T(8,128)}, u32[]{:S(2)}) copy-start(f32[3,16,16,512]{3,2,1,0:T(8,128)} %axes_ref.13) | copy-start | bytes 4718596
  17.2 3.6 %collective-permute-start = (f32[48,128]{1,0:T(8,128)S(1)}, f32[48,128]{1,0:T(8,128)S(1)}, u32[]{:S(2)}, u32[]{:S(2)}) collective-permute-start(f32[48,128]{1,0:T(8,128)S(1)} %shard_map.39.own_ref.own_coupling_ref), channel_id=1, source_target_pairs={{0,16},{2,18},{4,20},{6,22},{8,24},{10,26},{12,28},{14,30},{16,0},... | collective-permute-start | bytes 73736 | tf_op jit(solution)/shard_map/ppermute | solution.py:531
  29.6 6.1 %collective-permute-start.1 = (f32[2,48,512]{2,1,0:T(8,128)S(1)}, f32[2,48,512]{2,1,0:T(8,128)S(1)}, u32[]{:S(2)}, u32[]{:S(2)}) collective-permute-start(f32[2,48,512]{2,1,0:T(8,128)S(1)} %get-tuple-element.17.edge_ref), channel_id=1, source_target_pairs={{0,1},{1,0},{2,3},{3,2},{4,5},{5,4},{6,7},{7,6},{8,9},{9,8},{10,11... | collective-permute-start | bytes 589832 | tf_op jit(solution)/shard_map/ppermute | solution.py:538
  45.0 3.5 %collective-permute-start.2 = (f32[24,128]{1,0:T(8,128)S(1)}, f32[24,128]{1,0:T(8,128)S(1)}, u32[]{:S(2)}, u32[]{:S(2)}) collective-permute-start(f32[24,128]{1,0:T(8,128)S(1)} %shard_map.44.own_ref), channel_id=1, source_target_pairs={{0,16},{2,18},{4,20},{6,22},{8,24},{10,26},{12,28},{14,30},{16,0},... | collective-permute-start | bytes 36872 | tf_op jit(solution)/shard_map/ppermute | solution.py:531
  57.4 5.1 %collective-permute-start.3 = (f32[2,48,512]{2,1,0:T(8,128)S(1)}, f32[2,48,512]{2,1,0:T(8,128)S(1)}, u32[]{:S(2)}, u32[]{:S(2)}) collective-permute-start(f32[2,48,512]{2,1,0:T(8,128)S(1)} %get-tuple-element.23.edge_ref), channel_id=1, source_target_pairs={{0,1},{1,0},{2,3},{3,2},{4,5},{5,4},{6,7},{7,6},{8,9},{9,8},{10,11... | collective-permute-start | bytes 589832 | tf_op jit(solution)/shard_map/ppermute | solution.py:538

commit v11 on v10

--- a/solution.py
+++ b/solution.py
@@ -10,6 +10,7 @@
 
 STEPS = 2
 LANES = 128
+SUBLANES = 8
 RHS = 6
 COUPLED = 16
 
@@ -142,32 +143,41 @@
     return total if term is None else total + weight * term
 
 
-def pieces(value, values, units, tile, rows):
-    step = min(units, rows)
-    for start in range(0, rows, step):
-        at = tile * rows + start
+def tiles_of(shape):
+    rows, width = shape[-2:]
+    band = SUBLANES if rows % SUBLANES == 0 else rows
+    for tile in range(width // LANES):
+        for row in range(0, rows, band):
+            yield tile, slice(row, row + band), slice(tile * LANES, (tile + 1) * LANES)
+
+
+def pieces(value, values, units, tile, band, rows):
+    count = band.stop - band.start
+    step = min(units, count)
+    for start in range(0, count, step):
+        at = tile * rows + band.start + start
         to = (at // units * values + value) * units + at % units
         yield slice(start, start + step), slice(to, to + step)
 
 
-def pinned(source, pins_ref, component, lanes):
+def pinned(source, pins_ref, component, band, lanes):
     position = lax.axis_index("gx")
     first = jnp.where(position == 0, diffusion, 0.0).astype(jnp.float32)
     last = jnp.where(position == lax.axis_size("gx") - 1, diffusion, 0.0).astype(jnp.float32)
-    source[0] = source[0] + first * pins_ref[0, component, :, lanes]
-    source[-1] = source[-1] + last * pins_ref[1, component, :, lanes]
+    source[0] = source[0] + first * pins_ref[0, component, band, lanes]
+    source[-1] = source[-1] + last * pins_ref[1, component, band, lanes]
     return source
 
 
-def read_field(field_ref, lanes):
+def read_field(field_ref, band, lanes):
     planes = field_ref.shape[1]
-    return [[field_ref[c, i, :, lanes] for i in range(planes)] for c in range(3)]
-
-
-def solve_components(line, field, axes_ref, pins_ref, lanes, ghosts):
+    return [[field_ref[c, i, band, lanes] for i in range(planes)] for c in range(3)]
+
+
+def solve_components(line, field, axes_ref, pins_ref, band, lanes, ghosts):
     planes = line.planes
     field = list(field)
-    axes = [[axes_ref[c, i, :, lanes] for i in range(planes)] for c in range(3)]
+    axes = [[axes_ref[c, i, band, lanes] for i in range(planes)] for c in range(3)]
     for component in range(3):
         source = []
         for i in range(planes):
@@ -177,7 +187,7 @@
             source.append(
                 field[component][i] + (anisotropy_rate * projection) * axes[component][i]
             )
-        source = pinned(source, pins_ref, component, lanes)
+        source = pinned(source, pins_ref, component, band, lanes)
         if ghosts is not None:
             source[0] = source[0] + diffusion * ghosts[component][0]
             source[-1] = source[-1] + diffusion * ghosts[component][1]
@@ -187,10 +197,10 @@
     return field
 
 
-def couplings(line, axes_ref, lanes):
+def couplings(line, axes_ref, band, lanes):
     planes = line.planes
     low, high = line.from_low, line.from_high
-    axes = [[axes_ref[c, i, :, lanes] for i in range(planes)] for c in range(3)]
+    axes = [[axes_ref[c, i, band, lanes] for i in range(planes)] for c in range(3)]
     scaled = [anisotropy_rate * a for a in axes[1]]
     first_second = [axes[0][i] * scaled[i] for i in range(planes)]
     second_third = [axes[2][i] * scaled[i] for i in range(planes)]
@@ -216,24 +226,21 @@
     return found
 
 
-def send_tile(line, units, values, field, axes_ref, pins_ref, out_ref, tile):
+def send_tile(line, units, values, field, axes_ref, pins_ref, out_ref, tile, band, lanes):
     rows = axes_ref.shape[2]
-    lanes = slice(tile * LANES, (tile + 1) * LANES)
-    solved = solve_components(line, field, axes_ref, pins_ref, lanes, None)
+    solved = solve_components(line, field, axes_ref, pins_ref, band, lanes, None)
     for component in range(3):
         for side, end in enumerate((0, -1)):
             value = 2 * component + side
-            for source, target in pieces(value, values, units, tile, rows):
+            for source, target in pieces(value, values, units, tile, band, rows):
                 out_ref[target, :] = solved[component][end][source]
 
 
 def coupling_kernel(line, units, axes_ref, out_ref):
-    rows, width = axes_ref.shape[2:]
-    tiles = width // LANES
-    for tile in range(tiles):
-        found = couplings(line, axes_ref, slice(tile * LANES, (tile + 1) * LANES))
-        for value, one in enumerate(found):
-            for source, target in pieces(value, COUPLED - RHS, units, tile, rows):
+    rows = axes_ref.shape[2]
+    for tile, band, lanes in tiles_of(axes_ref.shape):
+        for value, one in enumerate(couplings(line, axes_ref, band, lanes)):
+            for source, target in pieces(value, COUPLED - RHS, units, tile, band, rows):
                 out_ref[target, :] = one[source]
 
 
@@ -242,9 +249,9 @@
     for d in range(groups):
         start = (d * COUPLED + RHS) * units
         out_ref[start : start + extra, :] = coupling_ref[d * extra : (d + 1) * extra, :]
-    for tile in range(field_ref.shape[3] // LANES):
-        field = read_field(field_ref, slice(tile * LANES, (tile + 1) * LANES))
-        send_tile(line, units, COUPLED, field, axes_ref, pins_ref, out_ref, tile)
+    for tile, band, lanes in tiles_of(field_ref.shape):
+        field = read_field(field_ref, band, lanes)
+        send_tile(line, units, COUPLED, field, axes_ref, pins_ref, out_ref, tile, band, lanes)
 
 
 def solve_children(level, levels, rhs, coupling, outer):
@@ -374,32 +381,24 @@
 
 
 def finish_kernel(line, units, field_ref, axes_ref, pins_ref, ghost_ref, out_ref, edge_ref):
-    planes = line.planes
-    rows, width = field_ref.shape[2], field_ref.shape[3]
-    tiles = width // LANES
-    for tile in range(tiles):
-        lanes = slice(tile * LANES, (tile + 1) * LANES)
-        ghosts = [
-            [
-                jnp.concatenate(
-                    [
-                        ghost_ref[target, :]
-                        for _, target in pieces(2 * c + side, RHS, units, tile, rows)
-                    ],
-                    axis=0,
-                )
-                for side in range(2)
-            ]
-            for c in range(3)
-        ]
-        field = read_field(field_ref, lanes)
-        solved = solve_components(line, field, axes_ref, pins_ref, lanes, ghosts)
+    planes, rows = line.planes, field_ref.shape[2]
+
+    def ghost(value, tile, band):
+        parts = [ghost_ref[at, :] for _, at in pieces(value, RHS, units, tile, band, rows)]
+        return jnp.concatenate(parts, axis=0) if len(parts) > 1 else parts[0]
+
+    for tile, band, lanes in tiles_of(field_ref.shape):
+        ghosts = [[ghost(2 * c + side, tile, band) for side in range(2)] for c in range(3)]
+        field = read_field(field_ref, band, lanes)
+        solved = solve_components(line, field, axes_ref, pins_ref, band, lanes, ghosts)
         for c in range(3):
             for i in range(planes):
-                out_ref[c, i, :, lanes] = solved[c][i]
                 at = c * planes + i
-                edge_ref[0, at : at + 1, lanes] = solved[c][i][:1]
-                edge_ref[1, at : at + 1, lanes] = solved[c][i][rows - 1 :]
+                out_ref[c, i, band, lanes] = solved[c][i]
+                if band.start == 0:
+                    edge_ref[0, at : at + 1, lanes] = solved[c][i][:1]
+                if band.stop == rows:
+                    edge_ref[1, at : at + 1, lanes] = solved[c][i][-1:]
 
 
 def unit_scale(parts):
@@ -452,11 +451,14 @@
             mended_ref[side, parts[c], :] = rotated[c] * scale
 
 
-def mended(turned, mended_ref, at, lanes):
-    rows = turned.shape[0]
+def mended(turned, mended_ref, at, band, rows, lanes):
     row = lax.broadcasted_iota(jnp.int32, turned.shape, 0)
-    turned = jnp.where(row == 0, mended_ref[0, at : at + 1, lanes], turned)
-    return jnp.where(row == rows - 1, mended_ref[1, at : at + 1, lanes], turned)
+    if band.start == 0:
+        turned = jnp.where(row == 0, mended_ref[0, at : at + 1, lanes], turned)
+    if band.stop == rows:
+        last = row == turned.shape[0] - 1
+        turned = jnp.where(last, mended_ref[1, at : at + 1, lanes], turned)
+    return turned
 
 
 def mend_and_send_kernel(
@@ -474,18 +476,20 @@
 ):
     planes = line.planes
     mend_edges(edge_ref, raw_ref, beyond_ref, mended_ref)
-    for tile in range(turned_ref.shape[3] // LANES):
-        lanes = slice(tile * LANES, (tile + 1) * LANES)
-        field = read_field(turned_ref, lanes)
+    rows = turned_ref.shape[2]
+    for tile, band, lanes in tiles_of(turned_ref.shape):
+        field = read_field(turned_ref, band, lanes)
         for c in range(3):
             for i in range(planes):
-                field[c][i] = mended(field[c][i], mended_ref, c * planes + i, lanes)
-                out_ref[c, i, :, lanes] = field[c][i]
-        send_tile(line, units, RHS, field, axes_ref, pins_ref, sent_ref, tile)
+                at = c * planes + i
+                field[c][i] = mended(field[c][i], mended_ref, at, band, rows, lanes)
+                out_ref[c, i, band, lanes] = field[c][i]
+        send_tile(line, units, RHS, field, axes_ref, pins_ref, sent_ref, tile, band, lanes)
 
 
 def last_kernel(turned_ref, edge_ref, raw_ref, beyond_ref, out_hbm, out_ref, mended_ref, sems):
-    planes = turned_ref.shape[1]
+    planes, rows = turned_ref.shape[1:3]
+    whole = slice(0, rows)
 
     def copy(i):
         return pltpu.make_async_copy(out_ref.at[:, i], out_hbm.at[:, i], sems.at[i])
@@ -493,7 +497,8 @@
     mend_edges(edge_ref, raw_ref, beyond_ref, mended_ref)
     for i in range(planes):
         for c in range(3):
-            out_ref[c, i] = mended(turned_ref[c, i], mended_ref, c * planes + i, slice(None))
+            at = c * planes + i
+            out_ref[c, i] = mended(turned_ref[c, i], mended_ref, at, whole, rows, slice(None))
         copy(i).start()
     for i in range(planes):
         copy(i).wait()

time: 64.1 us -> 64 us (level)
  no operation moved by 1% of the time
where the time goes in v11:
time: 64 us; the launch traced here: 63.7 us
  blocking collectives  36.6 us (57%)
  starting transfers between devices  12.9 us (20%)
  Pallas kernels  9.71 us (15%)
  waiting for transfers between devices  2.41 us (4%)
  local copies, waits for them, and re-layouts  1.98 us (3%)
    all_to_all x4, blocking collectives, exchange(): lax.all_to_all(parts, 'gx', split_axis=0, concat_axis=0, axis_index_group...  36.6 us
    pallas_call x12, Pallas kernels, call(): pl.pallas_call(kernel, out_shape=tuple(shapes), in_specs=[VMEM] * len(ope...  9.71 us
    ppermute x2, starting transfers between devices, from_neighbours(): return lax.ppermute(edges, 'gy', forward)  8.18 us
    ppermute x2, starting transfers between devices, swap_halves(): return lax.ppermute(block, 'gx', pairs)  4.75 us
    ppermute x2, waiting for transfers between devices, swap_halves(): return lax.ppermute(block, 'gx', pairs)  2.4 us
    unnamed x8, local copies, waits for them, and re-layouts  1.98 us
  transfers between devices with their start and end apart: 4, of which 2 were waited for; matrix products, arithmetic and copies ran while one was open for 0% of the time, Pallas kernels for 5%

profile of v11, /device:TPU:1, one launch (start us, length us, event | category | flops | bytes accessed | tf_op | source)
XLA Modules:
  0.0 63.7 jit_solution(3819116177797564607)
XLA Ops:
  0.0 1.4 %copy-done = f32[3,16,16,512]{3,2,1,0:T(8,128)S(1)} copy-done((f32[3,16,16,512]{3,2,1,0:T(8,128)S(1)}, f32[3,16,16,512]{3,2,1,0:T(8,128)}, u32[]{:S(2)}) %copy-start) | copy-done | bytes 1572888
  1.4 0.8 %shard_map.37.coupling_ref = f32[640,128]{1,0:T(8,128)S(1)} custom-call(f32[3,16,16,512]{3,2,1,0:T(8,128)S(1)} %copy-done), custom_call_target="tpu_custom_call" | custom-call | tf_op jit(solution)/shard_map/pallas_call | solution.py:514
  2.3 0.6 copy-done.2
  2.8 0.9 %shard_map.38 = f32[1024,128]{1,0:T(8,128)S(1)} custom-call(f32[640,128]{1,0:T(8,128)S(1)} %shard_map.37.coupling_ref, f32[3,16,16,512]{3,2,1,0:T(8,128)S(1)} %copy-done.2, f32[3,16,16,512]{3,2,1,0:T(8,128)S(1)} %copy-done, f32[2,3,16,512]{3,2,1,0:T(8,128)S(1)} %copy-done.3), custom_call_target="tpu_custom_call" | custom-call | tf_op jit(solution)/shard_map/pallas_call | solution.py:514
  3.7 13.2 %all_to_all.20 = f32[8,128,128]{2,1,0:T(8,128)S(1)} all-to-all(f32[8,128,128]{2,1,0:T(8,128)S(1)} %bitcast.14), channel_id=1, replica_groups={{0,2,4,6,8,10,12,14},{16,18,20,22,24,26,28,30},{1,3,5,7,9,11,13,15},{17..., dimensions={0} | all-to-all | bytes 1048576 | tf_op jit(solution)/shard_map/all_to_all | solution.py:529
  16.9 0.2 shard_map.39.own_ref.own_coupling_ref
  17.2 2.4 %collective-permute-start = (f32[48,128]{1,0:T(8,128)S(1)}, f32[48,128]{1,0:T(8,128)S(1)}, u32[]{:S(2)}, u32[]{:S(2)}) collective-permute-start(f32[48,128]{1,0:T(8,128)S(1)} %shard_map.39.own_ref.own_coupling_ref), channel_id=1, source_target_pairs={{0,16},{2,18},{4,20},{6,22},{8,24},{10,26},{12,28},{14,30},{16,0},... | collective-permute-start | bytes 73736 | tf_op jit(solution)/shard_map/ppermute | solution.py:536
  19.6 1.3 %collective-permute-done.other_ref.other_coupling_ref = f32[48,128]{1,0:T(8,128)S(1)} collective-permute-done((f32[48,128]{1,0:T(8,128)S(1)}, f32[48,128]{1,0:T(8,128)S(1)}, u32[]{:S(2)}, u32[]{:S(2)}) %collective-permute-start) | collective-permute-done | bytes 24608 | tf_op jit(solution)/shard_map/ppermute | solution.py:536
  20.8 0.1 shard_map.40
  21.0 7.6 %all_to_all.21 = f32[8,48,128]{2,1,0:T(8,128)S(1)} all-to-all(f32[8,48,128]{2,1,0:T(8,128)S(1)} %bitcast.20), channel_id=1, replica_groups={{0,2,4,6,8,10,12,14},{16,18,20,22,24,26,28,30},{1,3,5,7,9,11,13,15},{17..., dimensions={0} | all-to-all | bytes 393216 | tf_op jit(solution)/shard_map/all_to_all | solution.py:529
  28.6 1.0 %shard_map.41 = (f32[3,16,16,512]{3,2,1,0:T(8,128)S(1)}, f32[2,48,512]{2,1,0:T(8,128)S(1)}) custom-call(f32[3,16,16,512]{3,2,1,0:T(8,128)S(1)} %copy-done.2, f32[3,16,16,512]{3,2,1,0:T(8,128)S(1)} %copy-done.1, f32[2,3,16,512]{3,2,1,0:T(8,128)S(1)} %copy-done.3, f32[384,128]{1,0:T(8,128)S(1)} %bitcast.18), custom_call_target="tpu_custom_call" | custom-call | tf_op jit(solution)/shard_map/pallas_call | solution.py:514
  29.5 4.6 %collective-permute-start.1 = (f32[2,48,512]{2,1,0:T(8,128)S(1)}, f32[2,48,512]{2,1,0:T(8,128)S(1)}, u32[]{:S(2)}, u32[]{:S(2)}) collective-permute-start(f32[2,48,512]{2,1,0:T(8,128)S(1)} %get-tuple-element.17.edge_ref), channel_id=1, source_target_pairs={{0,1},{1,0},{2,3},{3,2},{4,5},{5,4},{6,7},{7,6},{8,9},{9,8},{10,11... | collective-permute-start | bytes 589832 | tf_op jit(solution)/shard_map/ppermute | solution.py:543
  34.1 1.5 %shard_map.42 = (f32[3,16,16,512]{3,2,1,0:T(8,128)S(1)}, f32[2,48,512]{2,1,0:T(8,128)S(1)}) custom-call(f32[3,16,16,512]{3,2,1,0:T(8,128)S(1)} %get-tuple-element.15.field_ref, f32[3,16,16,512]{3,2,1,0:T(8,128)S(1)} %copy-done.1), custom_call_target="tpu_custom_call" | custom-call | tf_op jit(solution)/shard_map/pallas_call | solution.py:514
  35.6 1.1 %shard_map.43 = (f32[3,16,16,512]{3,2,1,0:T(8,128)S(1)}, f32[384,128]{1,0:T(8,128)S(1)}) custom-call(f32[3,16,16,512]{3,2,1,0:T(8,128)S(1)} %get-tuple-element.16.turned_ref, f32[2,48,512]{2,1,0:T(8,128)S(1)} %get-tuple-element.17.edge_ref, f32[2,48,512]{2,1,0:T(8,128)S(1)} %get-tuple-element.18.raw_ref, ...), custom_call_target="tpu_custom_call" | custom-call | tf_op jit(solution)/shard_map/pallas_call | solution.py:514
  36.8 8.0 %all_to_all.22 = f32[8,48,128]{2,1,0:T(8,128)S(1)} all-to-all(f32[8,48,128]{2,1,0:T(8,128)S(1)} %bitcast.21), channel_id=1, replica_groups={{0,2,4,6,8,10,12,14},{16,18,20,22,24,26,28,30},{1,3,5,7,9,11,13,15},{17..., dimensions={0} | all-to-all | bytes 393216 | tf_op jit(solution)/shard_map/all_to_all | solution.py:529
  44.8 0.1 shard_map.44.own_ref
  44.9 2.4 %collective-permute-start.2 = (f32[24,128]{1,0:T(8,128)S(1)}, f32[24,128]{1,0:T(8,128)S(1)}, u32[]{:S(2)}, u32[]{:S(2)}) collective-permute-start(f32[24,128]{1,0:T(8,128)S(1)} %shard_map.44.own_ref), channel_id=1, source_target_pairs={{0,16},{2,18},{4,20},{6,22},{8,24},{10,26},{12,28},{14,30},{16,0},... | collective-permute-start | bytes 36872 | tf_op jit(solution)/shard_map/ppermute | solution.py:536
  47.3 1.1 %collective-permute-done.2.other_ref = f32[24,128]{1,0:T(8,128)S(1)} collective-permute-done((f32[24,128]{1,0:T(8,128)S(1)}, f32[24,128]{1,0:T(8,128)S(1)}, u32[]{:S(2)}, u32[]{:S(2)}) %collective-permute-start.2) | collective-permute-done | bytes 12320 | tf_op jit(solution)/shard_map/ppermute | solution.py:536
  48.4 0.1 shard_map.45
  48.5 7.7 %all_to_all.23 = f32[8,48,128]{2,1,0:T(8,128)S(1)} all-to-all(f32[8,48,128]{2,1,0:T(8,128)S(1)} %bitcast.19), channel_id=1, replica_groups={{0,2,4,6,8,10,12,14},{16,18,20,22,24,26,28,30},{1,3,5,7,9,11,13,15},{17..., dimensions={0} | all-to-all | bytes 393216 | tf_op jit(solution)/shard_map/all_to_all | solution.py:529
  56.3 1.0 %shard_map.46 = (f32[3,16,16,512]{3,2,1,0:T(8,128)S(1)}, f32[2,48,512]{2,1,0:T(8,128)S(1)}) custom-call(f32[3,16,16,512]{3,2,1,0:T(8,128)S(1)} %get-tuple-element.19.field_ref, f32[3,16,16,512]{3,2,1,0:T(8,128)S(1)} %copy-done.1, f32[2,3,16,512]{3,2,1,0:T(8,128)S(1)} %copy-done.3, f32[384,128]{1,0:T(8,128)S(1)} %bitcast.17), custom_call_target="tpu_custom_call" | custom-call | tf_op jit(solution)/shard_map/pallas_call | solution.py:514
  57.3 3.6 %collective-permute-start.3 = (f32[2,48,512]{2,1,0:T(8,128)S(1)}, f32[2,48,512]{2,1,0:T(8,128)S(1)}, u32[]{:S(2)}, u32[]{:S(2)}) collective-permute-start(f32[2,48,512]{2,1,0:T(8,128)S(1)} %get-tuple-element.23.edge_ref), channel_id=1, source_target_pairs={{0,1},{1,0},{2,3},{3,2},{4,5},{5,4},{6,7},{7,6},{8,9},{9,8},{10,11... | collective-permute-start | bytes 589832 | tf_op jit(solution)/shard_map/ppermute | solution.py:543
  60.9 1.4 %shard_map.47 = (f32[3,16,16,512]{3,2,1,0:T(8,128)S(1)}, f32[2,48,512]{2,1,0:T(8,128)S(1)}) custom-call(f32[3,16,16,512]{3,2,1,0:T(8,128)S(1)} %get-tuple-element.21.field_ref, f32[3,16,16,512]{3,2,1,0:T(8,128)S(1)} %copy-done.1), custom_call_target="tpu_custom_call" | custom-call | tf_op jit(solution)/shard_map/pallas_call | solution.py:514
  62.3 1.3 %shard_map.48 = f32[3,16,16,512]{3,2,1,0:T(8,128)} custom-call(f32[3,16,16,512]{3,2,1,0:T(8,128)S(1)} %get-tuple-element.22.turned_ref, f32[2,48,512]{2,1,0:T(8,128)S(1)} %get-tuple-element.23.edge_ref, f32[2,48,512]{2,1,0:T(8,128)S(1)} %get-tuple-element.24.raw_ref, f32[2,48,512]{2,1,0:T(8,128)S(1)} %collective-permute-done.3.beyond_ref), custom_call_target="tpu_custom_call" | custom-call | tf_op jit(solution)/shard_map/pallas_call | solution.py:514
  (8 shorter events, 0.0 us)
Async XLA Ops:
  0.0 1.4 %copy-start = (f32[3,16,16,512]{3,2,1,0:T(8,128)S(1)}, f32[3,16,16,512]{3,2,1,0:T(8,128)}, u32[]{:S(2)}) copy-start(f32[3,16,16,512]{3,2,1,0:T(8,128)} %axes_ref.13) | copy-start | bytes 4718596
  1.4 1.4 %copy-start.2 = (f32[3,16,16,512]{3,2,1,0:T(8,128)S(1)}, f32[3,16,16,512]{3,2,1,0:T(8,128)}, u32[]{:S(2)}) copy-start(f32[3,16,16,512]{3,2,1,0:T(8,128)} %field_ref.3) | copy-start | bytes 4718596
  1.4 1.4 %copy-start.3 = (f32[2,3,16,512]{3,2,1,0:T(8,128)S(1)}, f32[2,3,16,512]{3,2,1,0:T(8,128)}, u32[]{:S(2)}) copy-start(f32[2,3,16,512]{3,2,1,0:T(8,128)} %pins_ref.7) | copy-start | bytes 589828
  16.9 11.6 %copy-start.1 = (f32[3,16,16,512]{3,2,1,0:T(8,128)S(1)}, f32[3,16,16,512]{3,2,1,0:T(8,128)}, u32[]{:S(2)}) copy-start(f32[3,16,16,512]{3,2,1,0:T(8,128)} %axes_ref.13) | copy-start | bytes 4718596
  17.2 3.6 %collective-permute-start = (f32[48,128]{1,0:T(8,128)S(1)}, f32[48,128]{1,0:T(8,128)S(1)}, u32[]{:S(2)}, u32[]{:S(2)}) collective-permute-start(f32[48,128]{1,0:T(8,128)S(1)} %shard_map.39.own_ref.own_coupling_ref), channel_id=1, source_target_pairs={{0,16},{2,18},{4,20},{6,22},{8,24},{10,26},{12,28},{14,30},{16,0},... | collective-permute-start | bytes 73736 | tf_op jit(solution)/shard_map/ppermute | solution.py:536
  29.5 6.1 %collective-permute-start.1 = (f32[2,48,512]{2,1,0:T(8,128)S(1)}, f32[2,48,512]{2,1,0:T(8,128)S(1)}, u32[]{:S(2)}, u32[]{:S(2)}) collective-permute-start(f32[2,48,512]{2,1,0:T(8,128)S(1)} %get-tuple-element.17.edge_ref), channel_id=1, source_target_pairs={{0,1},{1,0},{2,3},{3,2},{4,5},{5,4},{6,7},{7,6},{8,9},{9,8},{10,11... | collective-permute-start | bytes 589832 | tf_op jit(solution)/shard_map/ppermute | solution.py:543
  44.9 3.5 %collective-permute-start.2 = (f32[24,128]{1,0:T(8,128)S(1)}, f32[24,128]{1,0:T(8,128)S(1)}, u32[]{:S(2)}, u32[]{:S(2)}) collective-permute-start(f32[24,128]{1,0:T(8,128)S(1)} %shard_map.44.own_ref), channel_id=1, source_target_pairs={{0,16},{2,18},{4,20},{6,22},{8,24},{10,26},{12,28},{14,30},{16,0},... | collective-permute-start | bytes 36872 | tf_op jit(solution)/shard_map/ppermute | solution.py:536
  57.3 5.1 %collective-permute-start.3 = (f32[2,48,512]{2,1,0:T(8,128)S(1)}, f32[2,48,512]{2,1,0:T(8,128)S(1)}, u32[]{:S(2)}, u32[]{:S(2)}) collective-permute-start(f32[2,48,512]{2,1,0:T(8,128)S(1)} %get-tuple-element.23.edge_ref), channel_id=1, source_target_pairs={{0,1},{1,0},{2,3},{3,2},{4,5},{5,4},{6,7},{7,6},{8,9},{9,8},{10,11... | collective-permute-start | bytes 589832 | tf_op jit(solution)/shard_map/ppermute | solution.py:543

commit v12 on v11

--- a/solution.py
+++ b/solution.py
@@ -408,25 +408,24 @@
 
 def turn_kernel(field_ref, axes_ref, out_ref, raw_ref):
     planes, rows, width = field_ref.shape[1:]
-    row = lax.broadcasted_iota(jnp.int32, (rows, width), 0)
     for i in range(planes):
         field = [field_ref[c, i] for c in range(3)]
         axes = [axes_ref[c, i] for c in range(3)]
         projection = field[0] * axes[0] + field[1] * axes[1] + field[2] * axes[2]
+        projection = torque_rate * projection
         effective = []
         for c in range(3):
-            below = jnp.where(row == 0, 0.0, pltpu.roll(field[c], 1, 0))
-            above = jnp.where(row == rows - 1, 0.0, pltpu.roll(field[c], rows - 1, 0))
+            below = pltpu.roll(field[c], 1, 0)
+            above = pltpu.roll(field[c], rows - 1, 0)
             beside = pltpu.roll(field[c], 1, 1) + pltpu.roll(field[c], width - 1, 1)
             effective.append(
-                exchange_rate * (((above + below) + beside) - 4.0 * field[c])
+                (torque_rate * exchange_rate) * (((above + below) + beside) - 4.0 * field[c])
                 + projection * axes[c]
             )
         rotated = []
         for c in range(3):
             d, e = (c + 1) % 3, (c + 2) % 3
-            twisted = field[d] * effective[e] - field[e] * effective[d]
-            rotated.append(field[c] - torque_rate * twisted)
+            rotated.append(field[c] - field[d] * effective[e] + field[e] * effective[d])
         scale = unit_scale(rotated)
         for c in range(3):
             at = c * planes + i
@@ -440,7 +439,7 @@
     for side in range(2):
         parts = [slice(c * planes, (c + 1) * planes) for c in range(3)]
         field = [edge_ref[side, part, :] for part in parts]
-        beyond = [beyond_ref[1 - side, part, :] for part in parts]
+        beyond = [beyond_ref[1 - side, part, :] - edge_ref[1 - side, part, :] for part in parts]
         rotated = []
         for c in range(3):
             d, e = (c + 1) % 3, (c + 2) % 3

time: 64 us -> 64 us (level)
  no operation moved by 1% of the time
where the time goes in v12:
time: 64 us; the launch traced here: 63.7 us
  blocking collectives  36.6 us (57%)
  starting transfers between devices  12.9 us (20%)
  Pallas kernels  9.68 us (15%)
  waiting for transfers between devices  2.41 us (4%)
  local copies, waits for them, and re-layouts  1.98 us (3%)
    all_to_all x4, blocking collectives, exchange(): lax.all_to_all(parts, 'gx', split_axis=0, concat_axis=0, axis_index_group...  36.6 us
    pallas_call x12, Pallas kernels, call(): pl.pallas_call(kernel, out_shape=tuple(shapes), in_specs=[VMEM] * len(ope...  9.68 us
    ppermute x2, starting transfers between devices, from_neighbours(): return lax.ppermute(edges, 'gy', forward)  8.18 us
    ppermute x2, starting transfers between devices, swap_halves(): return lax.ppermute(block, 'gx', pairs)  4.75 us
    ppermute x2, waiting for transfers between devices, swap_halves(): return lax.ppermute(block, 'gx', pairs)  2.4 us
    unnamed x8, local copies, waits for them, and re-layouts  1.98 us
  transfers between devices with their start and end apart: 4, of which 2 were waited for; matrix products, arithmetic and copies ran while one was open for 0% of the time, Pallas kernels for 5%

profile of v12, /device:TPU:1, one launch (start us, length us, event | category | flops | bytes accessed | tf_op | source)
XLA Modules:
  0.0 63.7 jit_solution(5253636341122260440)
XLA Ops:
  0.0 1.4 %copy-done = f32[3,16,16,512]{3,2,1,0:T(8,128)S(1)} copy-done((f32[3,16,16,512]{3,2,1,0:T(8,128)S(1)}, f32[3,16,16,512]{3,2,1,0:T(8,128)}, u32[]{:S(2)}) %copy-start) | copy-done | bytes 1572888
  1.4 0.8 %shard_map.37.coupling_ref = f32[640,128]{1,0:T(8,128)S(1)} custom-call(f32[3,16,16,512]{3,2,1,0:T(8,128)S(1)} %copy-done), custom_call_target="tpu_custom_call" | custom-call | tf_op jit(solution)/shard_map/pallas_call | solution.py:513
  2.3 0.6 copy-done.2
  2.8 0.9 %shard_map.38 = f32[1024,128]{1,0:T(8,128)S(1)} custom-call(f32[640,128]{1,0:T(8,128)S(1)} %shard_map.37.coupling_ref, f32[3,16,16,512]{3,2,1,0:T(8,128)S(1)} %copy-done.2, f32[3,16,16,512]{3,2,1,0:T(8,128)S(1)} %copy-done, f32[2,3,16,512]{3,2,1,0:T(8,128)S(1)} %copy-done.3), custom_call_target="tpu_custom_call" | custom-call | tf_op jit(solution)/shard_map/pallas_call | solution.py:513
  3.7 13.2 %all_to_all.20 = f32[8,128,128]{2,1,0:T(8,128)S(1)} all-to-all(f32[8,128,128]{2,1,0:T(8,128)S(1)} %bitcast.14), channel_id=1, replica_groups={{0,2,4,6,8,10,12,14},{16,18,20,22,24,26,28,30},{1,3,5,7,9,11,13,15},{17..., dimensions={0} | all-to-all | bytes 1048576 | tf_op jit(solution)/shard_map/all_to_all | solution.py:528
  16.9 0.2 shard_map.39.own_ref.own_coupling_ref
  17.2 2.4 %collective-permute-start = (f32[48,128]{1,0:T(8,128)S(1)}, f32[48,128]{1,0:T(8,128)S(1)}, u32[]{:S(2)}, u32[]{:S(2)}) collective-permute-start(f32[48,128]{1,0:T(8,128)S(1)} %shard_map.39.own_ref.own_coupling_ref), channel_id=1, source_target_pairs={{0,16},{2,18},{4,20},{6,22},{8,24},{10,26},{12,28},{14,30},{16,0},... | collective-permute-start | bytes 73736 | tf_op jit(solution)/shard_map/ppermute | solution.py:535
  19.6 1.3 %collective-permute-done.other_ref.other_coupling_ref = f32[48,128]{1,0:T(8,128)S(1)} collective-permute-done((f32[48,128]{1,0:T(8,128)S(1)}, f32[48,128]{1,0:T(8,128)S(1)}, u32[]{:S(2)}, u32[]{:S(2)}) %collective-permute-start) | collective-permute-done | bytes 24608 | tf_op jit(solution)/shard_map/ppermute | solution.py:535
  20.8 0.1 shard_map.40
  21.0 7.6 %all_to_all.21 = f32[8,48,128]{2,1,0:T(8,128)S(1)} all-to-all(f32[8,48,128]{2,1,0:T(8,128)S(1)} %bitcast.20), channel_id=1, replica_groups={{0,2,4,6,8,10,12,14},{16,18,20,22,24,26,28,30},{1,3,5,7,9,11,13,15},{17..., dimensions={0} | all-to-all | bytes 393216 | tf_op jit(solution)/shard_map/all_to_all | solution.py:528
  28.6 1.0 %shard_map.41 = (f32[3,16,16,512]{3,2,1,0:T(8,128)S(1)}, f32[2,48,512]{2,1,0:T(8,128)S(1)}) custom-call(f32[3,16,16,512]{3,2,1,0:T(8,128)S(1)} %copy-done.2, f32[3,16,16,512]{3,2,1,0:T(8,128)S(1)} %copy-done.1, f32[2,3,16,512]{3,2,1,0:T(8,128)S(1)} %copy-done.3, f32[384,128]{1,0:T(8,128)S(1)} %bitcast.18), custom_call_target="tpu_custom_call" | custom-call | tf_op jit(solution)/shard_map/pallas_call | solution.py:513
  29.5 4.6 %collective-permute-start.1 = (f32[2,48,512]{2,1,0:T(8,128)S(1)}, f32[2,48,512]{2,1,0:T(8,128)S(1)}, u32[]{:S(2)}, u32[]{:S(2)}) collective-permute-start(f32[2,48,512]{2,1,0:T(8,128)S(1)} %get-tuple-element.17.edge_ref), channel_id=1, source_target_pairs={{0,1},{1,0},{2,3},{3,2},{4,5},{5,4},{6,7},{7,6},{8,9},{9,8},{10,11... | collective-permute-start | bytes 589832 | tf_op jit(solution)/shard_map/ppermute | solution.py:542
  34.1 1.5 %shard_map.42 = (f32[3,16,16,512]{3,2,1,0:T(8,128)S(1)}, f32[2,48,512]{2,1,0:T(8,128)S(1)}) custom-call(f32[3,16,16,512]{3,2,1,0:T(8,128)S(1)} %get-tuple-element.15.field_ref, f32[3,16,16,512]{3,2,1,0:T(8,128)S(1)} %copy-done.1), custom_call_target="tpu_custom_call" | custom-call | tf_op jit(solution)/shard_map/pallas_call | solution.py:513
  35.6 1.2 %shard_map.43 = (f32[3,16,16,512]{3,2,1,0:T(8,128)S(1)}, f32[384,128]{1,0:T(8,128)S(1)}) custom-call(f32[3,16,16,512]{3,2,1,0:T(8,128)S(1)} %get-tuple-element.16.turned_ref, f32[2,48,512]{2,1,0:T(8,128)S(1)} %get-tuple-element.17.edge_ref, f32[2,48,512]{2,1,0:T(8,128)S(1)} %get-tuple-element.18.raw_ref, ...), custom_call_target="tpu_custom_call" | custom-call | tf_op jit(solution)/shard_map/pallas_call | solution.py:513
  36.8 8.0 %all_to_all.22 = f32[8,48,128]{2,1,0:T(8,128)S(1)} all-to-all(f32[8,48,128]{2,1,0:T(8,128)S(1)} %bitcast.21), channel_id=1, replica_groups={{0,2,4,6,8,10,12,14},{16,18,20,22,24,26,28,30},{1,3,5,7,9,11,13,15},{17..., dimensions={0} | all-to-all | bytes 393216 | tf_op jit(solution)/shard_map/all_to_all | solution.py:528
  44.8 0.1 shard_map.44.own_ref
  44.9 2.4 %collective-permute-start.2 = (f32[24,128]{1,0:T(8,128)S(1)}, f32[24,128]{1,0:T(8,128)S(1)}, u32[]{:S(2)}, u32[]{:S(2)}) collective-permute-start(f32[24,128]{1,0:T(8,128)S(1)} %shard_map.44.own_ref), channel_id=1, source_target_pairs={{0,16},{2,18},{4,20},{6,22},{8,24},{10,26},{12,28},{14,30},{16,0},... | collective-permute-start | bytes 36872 | tf_op jit(solution)/shard_map/ppermute | solution.py:535
  47.3 1.1 %collective-permute-done.2.other_ref = f32[24,128]{1,0:T(8,128)S(1)} collective-permute-done((f32[24,128]{1,0:T(8,128)S(1)}, f32[24,128]{1,0:T(8,128)S(1)}, u32[]{:S(2)}, u32[]{:S(2)}) %collective-permute-start.2) | collective-permute-done | bytes 12320 | tf_op jit(solution)/shard_map/ppermute | solution.py:535
  48.4 0.1 shard_map.45
  48.5 7.7 %all_to_all.23 = f32[8,48,128]{2,1,0:T(8,128)S(1)} all-to-all(f32[8,48,128]{2,1,0:T(8,128)S(1)} %bitcast.19), channel_id=1, replica_groups={{0,2,4,6,8,10,12,14},{16,18,20,22,24,26,28,30},{1,3,5,7,9,11,13,15},{17..., dimensions={0} | all-to-all | bytes 393216 | tf_op jit(solution)/shard_map/all_to_all | solution.py:528
  56.3 1.0 %shard_map.46 = (f32[3,16,16,512]{3,2,1,0:T(8,128)S(1)}, f32[2,48,512]{2,1,0:T(8,128)S(1)}) custom-call(f32[3,16,16,512]{3,2,1,0:T(8,128)S(1)} %get-tuple-element.19.field_ref, f32[3,16,16,512]{3,2,1,0:T(8,128)S(1)} %copy-done.1, f32[2,3,16,512]{3,2,1,0:T(8,128)S(1)} %copy-done.3, f32[384,128]{1,0:T(8,128)S(1)} %bitcast.17), custom_call_target="tpu_custom_call" | custom-call | tf_op jit(solution)/shard_map/pallas_call | solution.py:513
  57.3 3.6 %collective-permute-start.3 = (f32[2,48,512]{2,1,0:T(8,128)S(1)}, f32[2,48,512]{2,1,0:T(8,128)S(1)}, u32[]{:S(2)}, u32[]{:S(2)}) collective-permute-start(f32[2,48,512]{2,1,0:T(8,128)S(1)} %get-tuple-element.23.edge_ref), channel_id=1, source_target_pairs={{0,1},{1,0},{2,3},{3,2},{4,5},{5,4},{6,7},{7,6},{8,9},{9,8},{10,11... | collective-permute-start | bytes 589832 | tf_op jit(solution)/shard_map/ppermute | solution.py:542
  60.9 1.4 %shard_map.47 = (f32[3,16,16,512]{3,2,1,0:T(8,128)S(1)}, f32[2,48,512]{2,1,0:T(8,128)S(1)}) custom-call(f32[3,16,16,512]{3,2,1,0:T(8,128)S(1)} %get-tuple-element.21.field_ref, f32[3,16,16,512]{3,2,1,0:T(8,128)S(1)} %copy-done.1), custom_call_target="tpu_custom_call" | custom-call | tf_op jit(solution)/shard_map/pallas_call | solution.py:513
  62.3 1.4 %shard_map.48 = f32[3,16,16,512]{3,2,1,0:T(8,128)} custom-call(f32[3,16,16,512]{3,2,1,0:T(8,128)S(1)} %get-tuple-element.22.turned_ref, f32[2,48,512]{2,1,0:T(8,128)S(1)} %get-tuple-element.23.edge_ref, f32[2,48,512]{2,1,0:T(8,128)S(1)} %get-tuple-element.24.raw_ref, f32[2,48,512]{2,1,0:T(8,128)S(1)} %collective-permute-done.3.beyond_ref), custom_call_target="tpu_custom_call" | custom-call | tf_op jit(solution)/shard_map/pallas_call | solution.py:513
  (8 shorter events, 0.0 us)
Async XLA Ops:
  0.0 1.4 %copy-start = (f32[3,16,16,512]{3,2,1,0:T(8,128)S(1)}, f32[3,16,16,512]{3,2,1,0:T(8,128)}, u32[]{:S(2)}) copy-start(f32[3,16,16,512]{3,2,1,0:T(8,128)} %axes_ref.13) | copy-start | bytes 4718596
  1.4 1.4 %copy-start.2 = (f32[3,16,16,512]{3,2,1,0:T(8,128)S(1)}, f32[3,16,16,512]{3,2,1,0:T(8,128)}, u32[]{:S(2)}) copy-start(f32[3,16,16,512]{3,2,1,0:T(8,128)} %field_ref.3) | copy-start | bytes 4718596
  1.4 1.4 %copy-start.3 = (f32[2,3,16,512]{3,2,1,0:T(8,128)S(1)}, f32[2,3,16,512]{3,2,1,0:T(8,128)}, u32[]{:S(2)}) copy-start(f32[2,3,16,512]{3,2,1,0:T(8,128)} %pins_ref.7) | copy-start | bytes 589828
  16.9 11.6 %copy-start.1 = (f32[3,16,16,512]{3,2,1,0:T(8,128)S(1)}, f32[3,16,16,512]{3,2,1,0:T(8,128)}, u32[]{:S(2)}) copy-start(f32[3,16,16,512]{3,2,1,0:T(8,128)} %axes_ref.13) | copy-start | bytes 4718596
  17.2 3.6 %collective-permute-start = (f32[48,128]{1,0:T(8,128)S(1)}, f32[48,128]{1,0:T(8,128)S(1)}, u32[]{:S(2)}, u32[]{:S(2)}) collective-permute-start(f32[48,128]{1,0:T(8,128)S(1)} %shard_map.39.own_ref.own_coupling_ref), channel_id=1, source_target_pairs={{0,16},{2,18},{4,20},{6,22},{8,24},{10,26},{12,28},{14,30},{16,0},... | collective-permute-start | bytes 73736 | tf_op jit(solution)/shard_map/ppermute | solution.py:535
  29.5 6.1 %collective-permute-start.1 = (f32[2,48,512]{2,1,0:T(8,128)S(1)}, f32[2,48,512]{2,1,0:T(8,128)S(1)}, u32[]{:S(2)}, u32[]{:S(2)}) collective-permute-start(f32[2,48,512]{2,1,0:T(8,128)S(1)} %get-tuple-element.17.edge_ref), channel_id=1, source_target_pairs={{0,1},{1,0},{2,3},{3,2},{4,5},{5,4},{6,7},{7,6},{8,9},{9,8},{10,11... | collective-permute-start | bytes 589832 | tf_op jit(solution)/shard_map/ppermute | solution.py:542
  44.9 3.5 %collective-permute-start.2 = (f32[24,128]{1,0:T(8,128)S(1)}, f32[24,128]{1,0:T(8,128)S(1)}, u32[]{:S(2)}, u32[]{:S(2)}) collective-permute-start(f32[24,128]{1,0:T(8,128)S(1)} %shard_map.44.own_ref), channel_id=1, source_target_pairs={{0,16},{2,18},{4,20},{6,22},{8,24},{10,26},{12,28},{14,30},{16,0},... | collective-permute-start | bytes 36872 | tf_op jit(solution)/shard_map/ppermute | solution.py:535
  57.3 5.0 %collective-permute-start.3 = (f32[2,48,512]{2,1,0:T(8,128)S(1)}, f32[2,48,512]{2,1,0:T(8,128)S(1)}, u32[]{:S(2)}, u32[]{:S(2)}) collective-permute-start(f32[2,48,512]{2,1,0:T(8,128)S(1)} %get-tuple-element.23.edge_ref), channel_id=1, source_target_pairs={{0,1},{1,0},{2,3},{3,2},{4,5},{5,4},{6,7},{7,6},{8,9},{9,8},{10,11... | collective-permute-start | bytes 589832 | tf_op jit(solution)/shard_map/ppermute | solution.py:542

commit v13 on v12

--- a/solution.py
+++ b/solution.py
@@ -50,6 +50,10 @@
         for i in range(len(carried) - 2, -1, -1):
             solved[i] = carried[i] * self.inverse_pivot[i] + self.factor[i + 1] * solved[i + 1]
         return solved
+
+    def solve_one_way(self, source):
+        carried = self.sweep(source)
+        return self.unwind(carried, carried[-1] * self.inverse_pivot[-1])
 
     def solve(self, source):
         half = self.planes // 2
@@ -143,9 +147,9 @@
     return total if term is None else total + weight * term
 
 
-def tiles_of(shape):
+def tiles_of(shape, banded=True):
     rows, width = shape[-2:]
-    band = SUBLANES if rows % SUBLANES == 0 else rows
+    band = SUBLANES if banded and rows % SUBLANES == 0 else rows
     for tile in range(width // LANES):
         for row in range(0, rows, band):
             yield tile, slice(row, row + band), slice(tile * LANES, (tile + 1) * LANES)
@@ -193,7 +197,7 @@
             source[-1] = source[-1] + diffusion * ghosts[component][1]
         if ghosts is None and component == 2:
             return field[:2] + [line.ends(source)]
-        field[component] = line.solve(source)
+        field[component] = line.solve(source) if ghosts is None else line.solve_one_way(source)
     return field
 
 
@@ -387,7 +391,7 @@
         parts = [ghost_ref[at, :] for _, at in pieces(value, RHS, units, tile, band, rows)]
         return jnp.concatenate(parts, axis=0) if len(parts) > 1 else parts[0]
 
-    for tile, band, lanes in tiles_of(field_ref.shape):
+    for tile, band, lanes in tiles_of(field_ref.shape, banded=False):
         ghosts = [[ghost(2 * c + side, tile, band) for side in range(2)] for c in range(3)]
         field = read_field(field_ref, band, lanes)
         solved = solve_components(line, field, axes_ref, pins_ref, band, lanes, ghosts)

time: 64 us -> 63.8 us (level)
  no operation moved by 1% of the time
where the time goes in v13:
time: 63.8 us; the launch traced here: 63.5 us
  blocking collectives  36.6 us (57%)
  starting transfers between devices  12.9 us (20%)
  Pallas kernels  9.57 us (15%)
  waiting for transfers between devices  2.41 us (4%)
  local copies, waits for them, and re-layouts  1.98 us (3%)
    all_to_all x4, blocking collectives, exchange(): lax.all_to_all(parts, 'gx', split_axis=0, concat_axis=0, axis_index_group...  36.6 us
    pallas_call x12, Pallas kernels, call(): pl.pallas_call(kernel, out_shape=tuple(shapes), in_specs=[VMEM] * len(ope...  9.57 us
    ppermute x2, starting transfers between devices, from_neighbours(): return lax.ppermute(edges, 'gy', forward)  8.18 us
    ppermute x2, starting transfers between devices, swap_halves(): return lax.ppermute(block, 'gx', pairs)  4.75 us
    ppermute x2, waiting for transfers between devices, swap_halves(): return lax.ppermute(block, 'gx', pairs)  2.4 us
    unnamed x8, local copies, waits for them, and re-layouts  1.98 us
  transfers between devices with their start and end apart: 4, of which 2 were waited for; matrix products, arithmetic and copies ran while one was open for 0% of the time, Pallas kernels for 5%

profile of v13, /device:TPU:1, one launch (start us, length us, event | category | flops | bytes accessed | tf_op | source)
XLA Modules:
  0.0 63.5 jit_solution(8047012523323987604)
XLA Ops:
  0.0 1.4 %copy-done = f32[3,16,16,512]{3,2,1,0:T(8,128)S(1)} copy-done((f32[3,16,16,512]{3,2,1,0:T(8,128)S(1)}, f32[3,16,16,512]{3,2,1,0:T(8,128)}, u32[]{:S(2)}) %copy-start) | copy-done | bytes 1572888
  1.4 0.8 %shard_map.37.coupling_ref = f32[640,128]{1,0:T(8,128)S(1)} custom-call(f32[3,16,16,512]{3,2,1,0:T(8,128)S(1)} %copy-done), custom_call_target="tpu_custom_call" | custom-call | tf_op jit(solution)/shard_map/pallas_call | solution.py:517
  2.3 0.6 copy-done.2
  2.8 0.9 %shard_map.38 = f32[1024,128]{1,0:T(8,128)S(1)} custom-call(f32[640,128]{1,0:T(8,128)S(1)} %shard_map.37.coupling_ref, f32[3,16,16,512]{3,2,1,0:T(8,128)S(1)} %copy-done.2, f32[3,16,16,512]{3,2,1,0:T(8,128)S(1)} %copy-done, f32[2,3,16,512]{3,2,1,0:T(8,128)S(1)} %copy-done.3), custom_call_target="tpu_custom_call" | custom-call | tf_op jit(solution)/shard_map/pallas_call | solution.py:517
  3.7 13.2 %all_to_all.20 = f32[8,128,128]{2,1,0:T(8,128)S(1)} all-to-all(f32[8,128,128]{2,1,0:T(8,128)S(1)} %bitcast.14), channel_id=1, replica_groups={{0,2,4,6,8,10,12,14},{16,18,20,22,24,26,28,30},{1,3,5,7,9,11,13,15},{17..., dimensions={0} | all-to-all | bytes 1048576 | tf_op jit(solution)/shard_map/all_to_all | solution.py:532
  16.9 0.2 shard_map.39.own_ref.own_coupling_ref
  17.2 2.4 %collective-permute-start = (f32[48,128]{1,0:T(8,128)S(1)}, f32[48,128]{1,0:T(8,128)S(1)}, u32[]{:S(2)}, u32[]{:S(2)}) collective-permute-start(f32[48,128]{1,0:T(8,128)S(1)} %shard_map.39.own_ref.own_coupling_ref), channel_id=1, source_target_pairs={{0,16},{2,18},{4,20},{6,22},{8,24},{10,26},{12,28},{14,30},{16,0},... | collective-permute-start | bytes 73736 | tf_op jit(solution)/shard_map/ppermute | solution.py:539
  19.6 1.3 %collective-permute-done.other_ref.other_coupling_ref = f32[48,128]{1,0:T(8,128)S(1)} collective-permute-done((f32[48,128]{1,0:T(8,128)S(1)}, f32[48,128]{1,0:T(8,128)S(1)}, u32[]{:S(2)}, u32[]{:S(2)}) %collective-permute-start) | collective-permute-done | bytes 24608 | tf_op jit(solution)/shard_map/ppermute | solution.py:539
  20.8 0.1 shard_map.40
  21.0 7.6 %all_to_all.21 = f32[8,48,128]{2,1,0:T(8,128)S(1)} all-to-all(f32[8,48,128]{2,1,0:T(8,128)S(1)} %bitcast.20), channel_id=1, replica_groups={{0,2,4,6,8,10,12,14},{16,18,20,22,24,26,28,30},{1,3,5,7,9,11,13,15},{17..., dimensions={0} | all-to-all | bytes 393216 | tf_op jit(solution)/shard_map/all_to_all | solution.py:532
  28.6 0.9 %shard_map.41 = (f32[3,16,16,512]{3,2,1,0:T(8,128)S(1)}, f32[2,48,512]{2,1,0:T(8,128)S(1)}) custom-call(f32[3,16,16,512]{3,2,1,0:T(8,128)S(1)} %copy-done.2, f32[3,16,16,512]{3,2,1,0:T(8,128)S(1)} %copy-done.1, f32[2,3,16,512]{3,2,1,0:T(8,128)S(1)} %copy-done.3, f32[384,128]{1,0:T(8,128)S(1)} %bitcast.18), custom_call_target="tpu_custom_call" | custom-call | tf_op jit(solution)/shard_map/pallas_call | solution.py:517
  29.5 4.6 %collective-permute-start.1 = (f32[2,48,512]{2,1,0:T(8,128)S(1)}, f32[2,48,512]{2,1,0:T(8,128)S(1)}, u32[]{:S(2)}, u32[]{:S(2)}) collective-permute-start(f32[2,48,512]{2,1,0:T(8,128)S(1)} %get-tuple-element.17.edge_ref), channel_id=1, source_target_pairs={{0,1},{1,0},{2,3},{3,2},{4,5},{5,4},{6,7},{7,6},{8,9},{9,8},{10,11... | collective-permute-start | bytes 589832 | tf_op jit(solution)/shard_map/ppermute | solution.py:546
  34.1 1.5 %shard_map.42 = (f32[3,16,16,512]{3,2,1,0:T(8,128)S(1)}, f32[2,48,512]{2,1,0:T(8,128)S(1)}) custom-call(f32[3,16,16,512]{3,2,1,0:T(8,128)S(1)} %get-tuple-element.15.field_ref, f32[3,16,16,512]{3,2,1,0:T(8,128)S(1)} %copy-done.1), custom_call_target="tpu_custom_call" | custom-call | tf_op jit(solution)/shard_map/pallas_call | solution.py:517
  35.6 1.2 %shard_map.43 = (f32[3,16,16,512]{3,2,1,0:T(8,128)S(1)}, f32[384,128]{1,0:T(8,128)S(1)}) custom-call(f32[3,16,16,512]{3,2,1,0:T(8,128)S(1)} %get-tuple-element.16.turned_ref, f32[2,48,512]{2,1,0:T(8,128)S(1)} %get-tuple-element.17.edge_ref, f32[2,48,512]{2,1,0:T(8,128)S(1)} %get-tuple-element.18.raw_ref, ...), custom_call_target="tpu_custom_call" | custom-call | tf_op jit(solution)/shard_map/pallas_call | solution.py:517
  36.7 8.0 %all_to_all.22 = f32[8,48,128]{2,1,0:T(8,128)S(1)} all-to-all(f32[8,48,128]{2,1,0:T(8,128)S(1)} %bitcast.21), channel_id=1, replica_groups={{0,2,4,6,8,10,12,14},{16,18,20,22,24,26,28,30},{1,3,5,7,9,11,13,15},{17..., dimensions={0} | all-to-all | bytes 393216 | tf_op jit(solution)/shard_map/all_to_all | solution.py:532
  44.7 0.1 shard_map.44.own_ref
  44.8 2.4 %collective-permute-start.2 = (f32[24,128]{1,0:T(8,128)S(1)}, f32[24,128]{1,0:T(8,128)S(1)}, u32[]{:S(2)}, u32[]{:S(2)}) collective-permute-start(f32[24,128]{1,0:T(8,128)S(1)} %shard_map.44.own_ref), channel_id=1, source_target_pairs={{0,16},{2,18},{4,20},{6,22},{8,24},{10,26},{12,28},{14,30},{16,0},... | collective-permute-start | bytes 36872 | tf_op jit(solution)/shard_map/ppermute | solution.py:539
  47.2 1.1 %collective-permute-done.2.other_ref = f32[24,128]{1,0:T(8,128)S(1)} collective-permute-done((f32[24,128]{1,0:T(8,128)S(1)}, f32[24,128]{1,0:T(8,128)S(1)}, u32[]{:S(2)}, u32[]{:S(2)}) %collective-permute-start.2) | collective-permute-done | bytes 12320 | tf_op jit(solution)/shard_map/ppermute | solution.py:539
  48.3 0.1 shard_map.45
  48.5 7.7 %all_to_all.23 = f32[8,48,128]{2,1,0:T(8,128)S(1)} all-to-all(f32[8,48,128]{2,1,0:T(8,128)S(1)} %bitcast.19), channel_id=1, replica_groups={{0,2,4,6,8,10,12,14},{16,18,20,22,24,26,28,30},{1,3,5,7,9,11,13,15},{17..., dimensions={0} | all-to-all | bytes 393216 | tf_op jit(solution)/shard_map/all_to_all | solution.py:532
  56.2 0.9 %shard_map.46 = (f32[3,16,16,512]{3,2,1,0:T(8,128)S(1)}, f32[2,48,512]{2,1,0:T(8,128)S(1)}) custom-call(f32[3,16,16,512]{3,2,1,0:T(8,128)S(1)} %get-tuple-element.19.field_ref, f32[3,16,16,512]{3,2,1,0:T(8,128)S(1)} %copy-done.1, f32[2,3,16,512]{3,2,1,0:T(8,128)S(1)} %copy-done.3, f32[384,128]{1,0:T(8,128)S(1)} %bitcast.17), custom_call_target="tpu_custom_call" | custom-call | tf_op jit(solution)/shard_map/pallas_call | solution.py:517
  57.1 3.6 %collective-permute-start.3 = (f32[2,48,512]{2,1,0:T(8,128)S(1)}, f32[2,48,512]{2,1,0:T(8,128)S(1)}, u32[]{:S(2)}, u32[]{:S(2)}) collective-permute-start(f32[2,48,512]{2,1,0:T(8,128)S(1)} %get-tuple-element.23.edge_ref), channel_id=1, source_target_pairs={{0,1},{1,0},{2,3},{3,2},{4,5},{5,4},{6,7},{7,6},{8,9},{9,8},{10,11... | collective-permute-start | bytes 589832 | tf_op jit(solution)/shard_map/ppermute | solution.py:546
  60.7 1.4 %shard_map.47 = (f32[3,16,16,512]{3,2,1,0:T(8,128)S(1)}, f32[2,48,512]{2,1,0:T(8,128)S(1)}) custom-call(f32[3,16,16,512]{3,2,1,0:T(8,128)S(1)} %get-tuple-element.21.field_ref, f32[3,16,16,512]{3,2,1,0:T(8,128)S(1)} %copy-done.1), custom_call_target="tpu_custom_call" | custom-call | tf_op jit(solution)/shard_map/pallas_call | solution.py:517
  62.2 1.4 %shard_map.48 = f32[3,16,16,512]{3,2,1,0:T(8,128)} custom-call(f32[3,16,16,512]{3,2,1,0:T(8,128)S(1)} %get-tuple-element.22.turned_ref, f32[2,48,512]{2,1,0:T(8,128)S(1)} %get-tuple-element.23.edge_ref, f32[2,48,512]{2,1,0:T(8,128)S(1)} %get-tuple-element.24.raw_ref, f32[2,48,512]{2,1,0:T(8,128)S(1)} %collective-permute-done.3.beyond_ref), custom_call_target="tpu_custom_call" | custom-call | tf_op jit(solution)/shard_map/pallas_call | solution.py:517
  (8 shorter events, 0.0 us)
Async XLA Ops:
  0.0 1.4 %copy-start = (f32[3,16,16,512]{3,2,1,0:T(8,128)S(1)}, f32[3,16,16,512]{3,2,1,0:T(8,128)}, u32[]{:S(2)}) copy-start(f32[3,16,16,512]{3,2,1,0:T(8,128)} %axes_ref.13) | copy-start | bytes 4718596
  1.4 1.4 %copy-start.2 = (f32[3,16,16,512]{3,2,1,0:T(8,128)S(1)}, f32[3,16,16,512]{3,2,1,0:T(8,128)}, u32[]{:S(2)}) copy-start(f32[3,16,16,512]{3,2,1,0:T(8,128)} %field_ref.3) | copy-start | bytes 4718596
  1.4 1.4 %copy-start.3 = (f32[2,3,16,512]{3,2,1,0:T(8,128)S(1)}, f32[2,3,16,512]{3,2,1,0:T(8,128)}, u32[]{:S(2)}) copy-start(f32[2,3,16,512]{3,2,1,0:T(8,128)} %pins_ref.7) | copy-start | bytes 589828
  16.9 11.6 %copy-start.1 = (f32[3,16,16,512]{3,2,1,0:T(8,128)S(1)}, f32[3,16,16,512]{3,2,1,0:T(8,128)}, u32[]{:S(2)}) copy-start(f32[3,16,16,512]{3,2,1,0:T(8,128)} %axes_ref.13) | copy-start | bytes 4718596
  17.2 3.6 %collective-permute-start = (f32[48,128]{1,0:T(8,128)S(1)}, f32[48,128]{1,0:T(8,128)S(1)}, u32[]{:S(2)}, u32[]{:S(2)}) collective-permute-start(f32[48,128]{1,0:T(8,128)S(1)} %shard_map.39.own_ref.own_coupling_ref), channel_id=1, source_target_pairs={{0,16},{2,18},{4,20},{6,22},{8,24},{10,26},{12,28},{14,30},{16,0},... | collective-permute-start | bytes 73736 | tf_op jit(solution)/shard_map/ppermute | solution.py:539
  29.5 6.1 %collective-permute-start.1 = (f32[2,48,512]{2,1,0:T(8,128)S(1)}, f32[2,48,512]{2,1,0:T(8,128)S(1)}, u32[]{:S(2)}, u32[]{:S(2)}) collective-permute-start(f32[2,48,512]{2,1,0:T(8,128)S(1)} %get-tuple-element.17.edge_ref), channel_id=1, source_target_pairs={{0,1},{1,0},{2,3},{3,2},{4,5},{5,4},{6,7},{7,6},{8,9},{9,8},{10,11... | collective-permute-start | bytes 589832 | tf_op jit(solution)/shard_map/ppermute | solution.py:546
  44.8 3.5 %collective-permute-start.2 = (f32[24,128]{1,0:T(8,128)S(1)}, f32[24,128]{1,0:T(8,128)S(1)}, u32[]{:S(2)}, u32[]{:S(2)}) collective-permute-start(f32[24,128]{1,0:T(8,128)S(1)} %shard_map.44.own_ref), channel_id=1, source_target_pairs={{0,16},{2,18},{4,20},{6,22},{8,24},{10,26},{12,28},{14,30},{16,0},... | collective-permute-start | bytes 36872 | tf_op jit(solution)/shard_map/ppermute | solution.py:539
  57.1 5.0 %collective-permute-start.3 = (f32[2,48,512]{2,1,0:T(8,128)S(1)}, f32[2,48,512]{2,1,0:T(8,128)S(1)}, u32[]{:S(2)}, u32[]{:S(2)}) collective-permute-start(f32[2,48,512]{2,1,0:T(8,128)S(1)} %get-tuple-element.23.edge_ref), channel_id=1, source_target_pairs={{0,1},{1,0},{2,3},{3,2},{4,5},{5,4},{6,7},{7,6},{8,9},{9,8},{10,11... | collective-permute-start | bytes 589832 | tf_op jit(solution)/shard_map/ppermute | solution.py:546

commit v14 on v13

--- a/solution.py
+++ b/solution.py
@@ -494,16 +494,20 @@
     planes, rows = turned_ref.shape[1:3]
     whole = slice(0, rows)
 
+    group = 4 if planes % 4 == 0 else 1
+
     def copy(i):
-        return pltpu.make_async_copy(out_ref.at[:, i], out_hbm.at[:, i], sems.at[i])
+        part = pl.ds(i, group)
+        return pltpu.make_async_copy(out_ref.at[:, part], out_hbm.at[:, part], sems.at[i])
 
     mend_edges(edge_ref, raw_ref, beyond_ref, mended_ref)
     for i in range(planes):
         for c in range(3):
             at = c * planes + i
             out_ref[c, i] = mended(turned_ref[c, i], mended_ref, at, whole, rows, slice(None))
-        copy(i).start()
-    for i in range(planes):
+        if i % group == group - 1:
+            copy(i + 1 - group).start()
+    for i in range(0, planes, group):
         copy(i).wait()
 
 

time: 63.8 us -> 63.9 us (level)
  no operation moved by 1% of the time
where the time goes in v14:
time: 63.9 us; the launch traced here: 63.6 us
  blocking collectives  36.6 us (57%)
  starting transfers between devices  12.9 us (20%)
  Pallas kernels  9.61 us (15%)
  waiting for transfers between devices  2.41 us (4%)
  local copies, waits for them, and re-layouts  1.98 us (3%)
    all_to_all x4, blocking collectives, exchange(): lax.all_to_all(parts, 'gx', split_axis=0, concat_axis=0, axis_index_group...  36.6 us
    pallas_call x12, Pallas kernels, call(): pl.pallas_call(kernel, out_shape=tuple(shapes), in_specs=[VMEM] * len(ope...  9.61 us
    ppermute x2, starting transfers between devices, from_neighbours(): return lax.ppermute(edges, 'gy', forward)  8.18 us
    ppermute x2, starting transfers between devices, swap_halves(): return lax.ppermute(block, 'gx', pairs)  4.75 us
    ppermute x2, waiting for transfers between devices, swap_halves(): return lax.ppermute(block, 'gx', pairs)  2.4 us
    unnamed x8, local copies, waits for them, and re-layouts  1.98 us
  transfers between devices with their start and end apart: 4, of which 2 were waited for; matrix products, arithmetic and copies ran while one was open for 0% of the time, Pallas kernels for 5%

profile of v14, /device:TPU:1, one launch (start us, length us, event | category | flops | bytes accessed | tf_op | source)
XLA Modules:
  0.0 63.6 jit_solution(15622518686285544299)
XLA Ops:
  0.0 1.4 %copy-done = f32[3,16,16,512]{3,2,1,0:T(8,128)S(1)} copy-done((f32[3,16,16,512]{3,2,1,0:T(8,128)S(1)}, f32[3,16,16,512]{3,2,1,0:T(8,128)}, u32[]{:S(2)}) %copy-start) | copy-done | bytes 1572888
  1.4 0.8 %shard_map.37.coupling_ref = f32[640,128]{1,0:T(8,128)S(1)} custom-call(f32[3,16,16,512]{3,2,1,0:T(8,128)S(1)} %copy-done), custom_call_target="tpu_custom_call" | custom-call | tf_op jit(solution)/shard_map/pallas_call | solution.py:521
  2.3 0.6 copy-done.2
  2.8 0.9 %shard_map.38 = f32[1024,128]{1,0:T(8,128)S(1)} custom-call(f32[640,128]{1,0:T(8,128)S(1)} %shard_map.37.coupling_ref, f32[3,16,16,512]{3,2,1,0:T(8,128)S(1)} %copy-done.2, f32[3,16,16,512]{3,2,1,0:T(8,128)S(1)} %copy-done, f32[2,3,16,512]{3,2,1,0:T(8,128)S(1)} %copy-done.3), custom_call_target="tpu_custom_call" | custom-call | tf_op jit(solution)/shard_map/pallas_call | solution.py:521
  3.7 13.2 %all_to_all.20 = f32[8,128,128]{2,1,0:T(8,128)S(1)} all-to-all(f32[8,128,128]{2,1,0:T(8,128)S(1)} %bitcast.14), channel_id=1, replica_groups={{0,2,4,6,8,10,12,14},{16,18,20,22,24,26,28,30},{1,3,5,7,9,11,13,15},{17..., dimensions={0} | all-to-all | bytes 1048576 | tf_op jit(solution)/shard_map/all_to_all | solution.py:536
  16.9 0.2 shard_map.39.own_ref.own_coupling_ref
  17.2 2.4 %collective-permute-start = (f32[48,128]{1,0:T(8,128)S(1)}, f32[48,128]{1,0:T(8,128)S(1)}, u32[]{:S(2)}, u32[]{:S(2)}) collective-permute-start(f32[48,128]{1,0:T(8,128)S(1)} %shard_map.39.own_ref.own_coupling_ref), channel_id=1, source_target_pairs={{0,16},{2,18},{4,20},{6,22},{8,24},{10,26},{12,28},{14,30},{16,0},... | collective-permute-start | bytes 73736 | tf_op jit(solution)/shard_map/ppermute | solution.py:543
  19.6 1.3 %collective-permute-done.other_ref.other_coupling_ref = f32[48,128]{1,0:T(8,128)S(1)} collective-permute-done((f32[48,128]{1,0:T(8,128)S(1)}, f32[48,128]{1,0:T(8,128)S(1)}, u32[]{:S(2)}, u32[]{:S(2)}) %collective-permute-start) | collective-permute-done | bytes 24608 | tf_op jit(solution)/shard_map/ppermute | solution.py:543
  20.8 0.1 shard_map.40
  21.0 7.6 %all_to_all.21 = f32[8,48,128]{2,1,0:T(8,128)S(1)} all-to-all(f32[8,48,128]{2,1,0:T(8,128)S(1)} %bitcast.20), channel_id=1, replica_groups={{0,2,4,6,8,10,12,14},{16,18,20,22,24,26,28,30},{1,3,5,7,9,11,13,15},{17..., dimensions={0} | all-to-all | bytes 393216 | tf_op jit(solution)/shard_map/all_to_all | solution.py:536
  28.6 0.9 %shard_map.41 = (f32[3,16,16,512]{3,2,1,0:T(8,128)S(1)}, f32[2,48,512]{2,1,0:T(8,128)S(1)}) custom-call(f32[3,16,16,512]{3,2,1,0:T(8,128)S(1)} %copy-done.2, f32[3,16,16,512]{3,2,1,0:T(8,128)S(1)} %copy-done.1, f32[2,3,16,512]{3,2,1,0:T(8,128)S(1)} %copy-done.3, f32[384,128]{1,0:T(8,128)S(1)} %bitcast.18), custom_call_target="tpu_custom_call" | custom-call | tf_op jit(solution)/shard_map/pallas_call | solution.py:521
  29.5 4.6 %collective-permute-start.1 = (f32[2,48,512]{2,1,0:T(8,128)S(1)}, f32[2,48,512]{2,1,0:T(8,128)S(1)}, u32[]{:S(2)}, u32[]{:S(2)}) collective-permute-start(f32[2,48,512]{2,1,0:T(8,128)S(1)} %get-tuple-element.17.edge_ref), channel_id=1, source_target_pairs={{0,1},{1,0},{2,3},{3,2},{4,5},{5,4},{6,7},{7,6},{8,9},{9,8},{10,11... | collective-permute-start | bytes 589832 | tf_op jit(solution)/shard_map/ppermute | solution.py:550
  34.1 1.5 %shard_map.42 = (f32[3,16,16,512]{3,2,1,0:T(8,128)S(1)}, f32[2,48,512]{2,1,0:T(8,128)S(1)}) custom-call(f32[3,16,16,512]{3,2,1,0:T(8,128)S(1)} %get-tuple-element.15.field_ref, f32[3,16,16,512]{3,2,1,0:T(8,128)S(1)} %copy-done.1), custom_call_target="tpu_custom_call" | custom-call | tf_op jit(solution)/shard_map/pallas_call | solution.py:521
  35.6 1.2 %shard_map.43 = (f32[3,16,16,512]{3,2,1,0:T(8,128)S(1)}, f32[384,128]{1,0:T(8,128)S(1)}) custom-call(f32[3,16,16,512]{3,2,1,0:T(8,128)S(1)} %get-tuple-element.16.turned_ref, f32[2,48,512]{2,1,0:T(8,128)S(1)} %get-tuple-element.17.edge_ref, f32[2,48,512]{2,1,0:T(8,128)S(1)} %get-tuple-element.18.raw_ref, ...), custom_call_target="tpu_custom_call" | custom-call | tf_op jit(solution)/shard_map/pallas_call | solution.py:521
  36.7 8.0 %all_to_all.22 = f32[8,48,128]{2,1,0:T(8,128)S(1)} all-to-all(f32[8,48,128]{2,1,0:T(8,128)S(1)} %bitcast.21), channel_id=1, replica_groups={{0,2,4,6,8,10,12,14},{16,18,20,22,24,26,28,30},{1,3,5,7,9,11,13,15},{17..., dimensions={0} | all-to-all | bytes 393216 | tf_op jit(solution)/shard_map/all_to_all | solution.py:536
  44.7 0.1 shard_map.44.own_ref
  44.8 2.4 %collective-permute-start.2 = (f32[24,128]{1,0:T(8,128)S(1)}, f32[24,128]{1,0:T(8,128)S(1)}, u32[]{:S(2)}, u32[]{:S(2)}) collective-permute-start(f32[24,128]{1,0:T(8,128)S(1)} %shard_map.44.own_ref), channel_id=1, source_target_pairs={{0,16},{2,18},{4,20},{6,22},{8,24},{10,26},{12,28},{14,30},{16,0},... | collective-permute-start | bytes 36872 | tf_op jit(solution)/shard_map/ppermute | solution.py:543
  47.2 1.1 %collective-permute-done.2.other_ref = f32[24,128]{1,0:T(8,128)S(1)} collective-permute-done((f32[24,128]{1,0:T(8,128)S(1)}, f32[24,128]{1,0:T(8,128)S(1)}, u32[]{:S(2)}, u32[]{:S(2)}) %collective-permute-start.2) | collective-permute-done | bytes 12320 | tf_op jit(solution)/shard_map/ppermute | solution.py:543
  48.3 0.1 shard_map.45
  48.5 7.7 %all_to_all.23 = f32[8,48,128]{2,1,0:T(8,128)S(1)} all-to-all(f32[8,48,128]{2,1,0:T(8,128)S(1)} %bitcast.19), channel_id=1, replica_groups={{0,2,4,6,8,10,12,14},{16,18,20,22,24,26,28,30},{1,3,5,7,9,11,13,15},{17..., dimensions={0} | all-to-all | bytes 393216 | tf_op jit(solution)/shard_map/all_to_all | solution.py:536
  56.2 0.9 %shard_map.46 = (f32[3,16,16,512]{3,2,1,0:T(8,128)S(1)}, f32[2,48,512]{2,1,0:T(8,128)S(1)}) custom-call(f32[3,16,16,512]{3,2,1,0:T(8,128)S(1)} %get-tuple-element.19.field_ref, f32[3,16,16,512]{3,2,1,0:T(8,128)S(1)} %copy-done.1, f32[2,3,16,512]{3,2,1,0:T(8,128)S(1)} %copy-done.3, f32[384,128]{1,0:T(8,128)S(1)} %bitcast.17), custom_call_target="tpu_custom_call" | custom-call | tf_op jit(solution)/shard_map/pallas_call | solution.py:521
  57.1 3.6 %collective-permute-start.3 = (f32[2,48,512]{2,1,0:T(8,128)S(1)}, f32[2,48,512]{2,1,0:T(8,128)S(1)}, u32[]{:S(2)}, u32[]{:S(2)}) collective-permute-start(f32[2,48,512]{2,1,0:T(8,128)S(1)} %get-tuple-element.23.edge_ref), channel_id=1, source_target_pairs={{0,1},{1,0},{2,3},{3,2},{4,5},{5,4},{6,7},{7,6},{8,9},{9,8},{10,11... | collective-permute-start | bytes 589832 | tf_op jit(solution)/shard_map/ppermute | solution.py:550
  60.7 1.4 %shard_map.47 = (f32[3,16,16,512]{3,2,1,0:T(8,128)S(1)}, f32[2,48,512]{2,1,0:T(8,128)S(1)}) custom-call(f32[3,16,16,512]{3,2,1,0:T(8,128)S(1)} %get-tuple-element.21.field_ref, f32[3,16,16,512]{3,2,1,0:T(8,128)S(1)} %copy-done.1), custom_call_target="tpu_custom_call" | custom-call | tf_op jit(solution)/shard_map/pallas_call | solution.py:521
  62.2 1.4 %shard_map.48 = f32[3,16,16,512]{3,2,1,0:T(8,128)} custom-call(f32[3,16,16,512]{3,2,1,0:T(8,128)S(1)} %get-tuple-element.22.turned_ref, f32[2,48,512]{2,1,0:T(8,128)S(1)} %get-tuple-element.23.edge_ref, f32[2,48,512]{2,1,0:T(8,128)S(1)} %get-tuple-element.24.raw_ref, f32[2,48,512]{2,1,0:T(8,128)S(1)} %collective-permute-done.3.beyond_ref), custom_call_target="tpu_custom_call" | custom-call | tf_op jit(solution)/shard_map/pallas_call | solution.py:521
  (8 shorter events, 0.0 us)
Async XLA Ops:
  0.0 1.4 %copy-start = (f32[3,16,16,512]{3,2,1,0:T(8,128)S(1)}, f32[3,16,16,512]{3,2,1,0:T(8,128)}, u32[]{:S(2)}) copy-start(f32[3,16,16,512]{3,2,1,0:T(8,128)} %axes_ref.13) | copy-start | bytes 4718596
  1.4 1.4 %copy-start.2 = (f32[3,16,16,512]{3,2,1,0:T(8,128)S(1)}, f32[3,16,16,512]{3,2,1,0:T(8,128)}, u32[]{:S(2)}) copy-start(f32[3,16,16,512]{3,2,1,0:T(8,128)} %field_ref.3) | copy-start | bytes 4718596
  1.4 1.4 %copy-start.3 = (f32[2,3,16,512]{3,2,1,0:T(8,128)S(1)}, f32[2,3,16,512]{3,2,1,0:T(8,128)}, u32[]{:S(2)}) copy-start(f32[2,3,16,512]{3,2,1,0:T(8,128)} %pins_ref.7) | copy-start | bytes 589828
  16.9 11.6 %copy-start.1 = (f32[3,16,16,512]{3,2,1,0:T(8,128)S(1)}, f32[3,16,16,512]{3,2,1,0:T(8,128)}, u32[]{:S(2)}) copy-start(f32[3,16,16,512]{3,2,1,0:T(8,128)} %axes_ref.13) | copy-start | bytes 4718596
  17.2 3.6 %collective-permute-start = (f32[48,128]{1,0:T(8,128)S(1)}, f32[48,128]{1,0:T(8,128)S(1)}, u32[]{:S(2)}, u32[]{:S(2)}) collective-permute-start(f32[48,128]{1,0:T(8,128)S(1)} %shard_map.39.own_ref.own_coupling_ref), channel_id=1, source_target_pairs={{0,16},{2,18},{4,20},{6,22},{8,24},{10,26},{12,28},{14,30},{16,0},... | collective-permute-start | bytes 73736 | tf_op jit(solution)/shard_map/ppermute | solution.py:543
  29.5 6.1 %collective-permute-start.1 = (f32[2,48,512]{2,1,0:T(8,128)S(1)}, f32[2,48,512]{2,1,0:T(8,128)S(1)}, u32[]{:S(2)}, u32[]{:S(2)}) collective-permute-start(f32[2,48,512]{2,1,0:T(8,128)S(1)} %get-tuple-element.17.edge_ref), channel_id=1, source_target_pairs={{0,1},{1,0},{2,3},{3,2},{4,5},{5,4},{6,7},{7,6},{8,9},{9,8},{10,11... | collective-permute-start | bytes 589832 | tf_op jit(solution)/shard_map/ppermute | solution.py:550
  44.8 3.5 %collective-permute-start.2 = (f32[24,128]{1,0:T(8,128)S(1)}, f32[24,128]{1,0:T(8,128)S(1)}, u32[]{:S(2)}, u32[]{:S(2)}) collective-permute-start(f32[24,128]{1,0:T(8,128)S(1)} %shard_map.44.own_ref), channel_id=1, source_target_pairs={{0,16},{2,18},{4,20},{6,22},{8,24},{10,26},{12,28},{14,30},{16,0},... | collective-permute-start | bytes 36872 | tf_op jit(solution)/shard_map/ppermute | solution.py:543
  57.1 5.0 %collective-permute-start.3 = (f32[2,48,512]{2,1,0:T(8,128)S(1)}, f32[2,48,512]{2,1,0:T(8,128)S(1)}, u32[]{:S(2)}, u32[]{:S(2)}) collective-permute-start(f32[2,48,512]{2,1,0:T(8,128)S(1)} %get-tuple-element.23.edge_ref), channel_id=1, source_target_pairs={{0,1},{1,0},{2,3},{3,2},{4,5},{5,4},{6,7},{7,6},{8,9},{9,8},{10,11... | collective-permute-start | bytes 589832 | tf_op jit(solution)/shard_map/ppermute | solution.py:550
